TPU v7x, 512 devices: a whole 4x4x16 slice. The times are simulated.
512 devices in a mesh: ctx: 64 (over z, x), kv: 8 (over y, core).
Axes of the slice: x: 4, y: 4, z: 16, core: 2. Of those that a mesh axis runs over, the one named last changes fastest.
Arguments:
- queries: bfloat16 [4096, 4, 64, 128], P(('ctx', 'kv')), may hold values from -60 to 60
- new_keys: bfloat16 [4096, 4, 8, 128], P(('ctx', 'kv')), may hold values from -6 to 50
- new_values: bfloat16 [4096, 4, 8, 128], P(('ctx', 'kv')), may hold values from -6 to 6
- suffix_keys: bfloat16 [4096, 32, 8, 128], P(('ctx', 'kv')), may hold values from -6 to 50
- suffix_values: bfloat16 [4096, 32, 8, 128], P(('ctx', 'kv')), may hold values from -6 to 6
- suffix_length: int32 [4096], P(('ctx', 'kv')), may hold values from 1 to 32, 81920 in all
- row_nodes: int32 [4096, 2], P('ctx'), may hold values from 0 to 63, all different within a row; in each aligned block of 64 rows (0 to 63, 64 to 127, ...) at most 3 rows name the same one
- prefix_keys: bfloat16 [64, 1024, 8, 128], P('ctx', None, 'kv'), may hold values from -6 to 50
- prefix_values: bfloat16 [64, 1024, 8, 128], P('ctx', None, 'kv'), may hold values from -6 to 6
- node_length: int32 [64], P('ctx'), may hold values from 1 to 1024, 49152 in all
Outputs:
- attended: bfloat16 [4096, 4, 64, 128], P(('ctx', 'kv'))
Inputs may be any that keep to these rules, and one draw needn't show every extreme that they name: `row_nodes`: each row names 2 different nodes; among the rows of one ctx index (aligned blocks of 64 rows) no node is named by more than 3 rows, and some node is named that often.
All inputs are finite; a program needn't handle non-finite values. No bound on the sum of `suffix_length` or of `node_length` on one device may be relied on, other than what follows from the above.
Results may differ from a plain program's by a relative error of at most 0.012.
Values may be sent and summed in bfloat16 or wider, within the bound.
No kernel may reach another device: no remote copies, remote signals or barrier semaphores. Data moves between devices by JAX's collectives and lax.ppermute only.
A program may use at most 64 MiB of HBM per device.

v0:
```python
import jax
import jax.numpy as jnp
from jax import lax
from jax.sharding import PartitionSpec as P


def node_partials(arrived, node_keys, node_values, node_len, score_scale):
    sources, items, step_count, heads_here, head_dim = arrived.shape
    kv_local = node_keys.shape[1]
    group_size = heads_here // kv_local
    width = 1
    while (
        width * 2 <= sources
        and sources % (width * 2) == 0
        and (width * 2 * items * step_count * heads_here <= 1024)
    ):
        width = width * 2
    shaped = arrived.reshape(
        sources // width, width, items, step_count, kv_local, group_size, head_dim
    )
    valid_keys = jnp.arange(node_keys.shape[0]) < node_len

    def one_block(block_queries):
        scores = (
            jnp.einsum(
                "pksjgd,ljd->pksjgl", block_queries, node_keys, preferred_element_type=jnp.float32
            )
            * score_scale
        )
        scores = jnp.where(valid_keys, scores, -jnp.inf)
        maxima = jnp.max(scores, axis=-1)
        weights = jnp.exp(scores - maxima[..., None])
        totals = jnp.sum(weights, axis=-1)
        outputs = jnp.einsum(
            "pksjgl,ljd->pksjgd",
            weights.astype(jnp.bfloat16),
            node_values,
            preferred_element_type=jnp.float32,
        )
        outputs = (outputs / totals[..., None]).astype(jnp.bfloat16)
        return (
            outputs.reshape(width, items, step_count, heads_here, head_dim),
            maxima.reshape(width, items, step_count, heads_here),
            totals.reshape(width, items, step_count, heads_here),
        )

    results = lax.map(one_block, shaped)
    return tuple((piece.reshape((sources,) + piece.shape[2:]) for piece in results))


def combine_path(entry_out, entry_max, entry_total):
    path_max = jnp.max(entry_max, axis=1)
    path_weight = entry_total * jnp.exp(entry_max - path_max[:, None])
    path_total = jnp.sum(path_weight, axis=1)
    path_sum = jnp.sum(path_weight[..., None] * entry_out.astype(jnp.float32), axis=1)
    path_output = (path_sum / path_total[..., None]).astype(jnp.bfloat16)
    return (path_output, path_max, path_total)


def per_device(
    queries,
    new_keys,
    new_values,
    suffix_keys,
    suffix_values,
    suffix_length,
    row_nodes,
    prefix_keys,
    prefix_values,
    node_length,
):
    n_ctx = lax.axis_size("ctx")
    rows_dev, path_depth = row_nodes.shape
    rows_here, step_count, head_count, head_dim = queries.shape
    kv_all = suffix_keys.shape[2]
    group_size = head_count // kv_all
    score_scale = head_dim ** (-0.5)
    capacity = 3 * rows_dev * path_depth // (2 * n_ctx)
    slots_all = n_ctx * capacity
    entries = rows_dev * path_depth
    grouped = lax.all_to_all(queries, "kv", split_axis=2, concat_axis=0, tiled=True)
    heads_here = grouped.shape[2]
    target = row_nodes.reshape(entries)
    target_hits = (target[:, None] == jnp.arange(n_ctx, dtype=jnp.int32)[None, :]).astype(jnp.int32)
    earlier = jnp.cumsum(target_hits, axis=0) - target_hits
    slot_rank = jnp.sum(earlier * target_hits, axis=1)
    slot_index = target * capacity + slot_rank
    slot_match = slot_index[:, None] == jnp.arange(slots_all, dtype=jnp.int32)[None, :]
    entry_of_slot = (
        jnp.sum(jnp.where(slot_match, jnp.arange(entries, dtype=jnp.int32)[:, None] + 1, 0), axis=0)
        - 1
    )
    filled = entry_of_slot >= 0
    source_row = jnp.maximum(entry_of_slot, 0) // path_depth
    outgoing = jnp.take(grouped, source_row, axis=0)
    outgoing = jnp.where(filled[:, None, None, None], outgoing, jnp.zeros((), jnp.bfloat16))
    outgoing = outgoing.reshape(n_ctx, capacity, step_count, heads_here, head_dim)
    keys_here = prefix_keys[0]
    values_here = prefix_values[0]
    length_here = node_length[0]
    returned = []
    for step in range(step_count):
        step_part = node_partials(
            lax.all_to_all(
                outgoing[:, :, step : step + 1], "ctx", split_axis=0, concat_axis=0, tiled=True
            ),
            keys_here,
            values_here,
            length_here,
            score_scale,
        )
        returned.append(
            (
                lax.all_to_all(
                    step_part[0].astype(jnp.float32), "ctx", split_axis=0, concat_axis=0, tiled=True
                ).astype(jnp.bfloat16),
                lax.all_to_all(step_part[1], "ctx", split_axis=0, concat_axis=0, tiled=True),
                lax.all_to_all(step_part[2], "ctx", split_axis=0, concat_axis=0, tiled=True),
            )
        )
    back_out = jnp.concatenate([piece[0] for piece in returned], axis=2)
    back_max = jnp.concatenate([piece[1] for piece in returned], axis=2)
    back_total = jnp.concatenate([piece[2] for piece in returned], axis=2)
    entry_out = jnp.take(back_out.reshape((slots_all,) + back_out.shape[2:]), slot_index, axis=0)
    entry_out = entry_out.reshape(rows_dev, path_depth, step_count, heads_here, head_dim)
    entry_max = jnp.take(back_max.reshape((slots_all,) + back_max.shape[2:]), slot_index, axis=0)
    entry_max = entry_max.reshape(rows_dev, path_depth, step_count, heads_here)
    entry_total = jnp.take(
        back_total.reshape((slots_all,) + back_total.shape[2:]), slot_index, axis=0
    )
    entry_total = entry_total.reshape(rows_dev, path_depth, step_count, heads_here)
    query_heads = queries.reshape(rows_here, step_count, kv_all, group_size, head_dim)
    own_scores = (
        jnp.einsum(
            "rsjgd,rtjd->rsjgt", query_heads, suffix_keys, preferred_element_type=jnp.float32
        )
        * score_scale
    )
    own_valid = jnp.arange(suffix_keys.shape[1])[None, :] < suffix_length[:, None]
    own_scores = jnp.where(own_valid[:, None, None, None, :], own_scores, -jnp.inf)
    fresh_scores = (
        jnp.einsum("rsjgd,rtjd->rsjgt", query_heads, new_keys, preferred_element_type=jnp.float32)
        * score_scale
    )
    fresh_valid = jnp.arange(step_count)[None, :] <= jnp.arange(step_count)[:, None]
    fresh_scores = jnp.where(fresh_valid[None, :, None, None, :], fresh_scores, -jnp.inf)
    suffix_max = jnp.maximum(jnp.max(own_scores, axis=-1), jnp.max(fresh_scores, axis=-1))
    own_weights = jnp.exp(own_scores - suffix_max[..., None])
    fresh_weights = jnp.exp(fresh_scores - suffix_max[..., None])
    suffix_total = jnp.sum(own_weights, axis=-1) + jnp.sum(fresh_weights, axis=-1)
    suffix_sum = jnp.einsum(
        "rsjgt,rtjd->rsjgd",
        own_weights.astype(jnp.bfloat16),
        suffix_values,
        preferred_element_type=jnp.float32,
    )
    suffix_sum = suffix_sum + jnp.einsum(
        "rsjgt,rtjd->rsjgd",
        fresh_weights.astype(jnp.bfloat16),
        new_values,
        preferred_element_type=jnp.float32,
    )
    suffix_max = suffix_max.reshape(rows_here, step_count, head_count)
    suffix_total = suffix_total.reshape(rows_here, step_count, head_count)
    suffix_sum = suffix_sum.reshape(rows_here, step_count, head_count, head_dim)
    home_out, home_max, home_total = (
        lax.all_to_all(
            entry_out.astype(jnp.float32), "kv", split_axis=0, concat_axis=3, tiled=True
        ).astype(entry_out.dtype),
        lax.all_to_all(entry_max, "kv", split_axis=0, concat_axis=3, tiled=True),
        lax.all_to_all(entry_total, "kv", split_axis=0, concat_axis=3, tiled=True),
    )
    path_output, path_max, path_total = combine_path(home_out, home_max, home_total)
    top_score = jnp.maximum(path_max, suffix_max)
    weight_prefix = path_total * jnp.exp(path_max - top_score)
    weight_suffix = jnp.exp(suffix_max - top_score)
    numerator = (
        weight_prefix[..., None] * path_output.astype(jnp.float32)
        + weight_suffix[..., None] * suffix_sum
    )
    denominator = weight_prefix + weight_suffix * suffix_total
    return (numerator / denominator[..., None]).astype(jnp.bfloat16)


def solution(mesh):
    return jax.shard_map(
        per_device,
        mesh=mesh,
        in_specs=(
            P(("ctx", "kv"), None, None, None),
            P(("ctx", "kv"), None, None, None),
            P(("ctx", "kv"), None, None, None),
            P(("ctx", "kv"), None, None, None),
            P(("ctx", "kv"), None, None, None),
            P(("ctx", "kv")),
            P("ctx", None),
            P("ctx", None, "kv", None),
            P("ctx", None, "kv", None),
            P("ctx"),
        ),
        out_specs=P(("ctx", "kv"), None, None, None),
        check_vma=False,
    )
```

profile of v0, /device:TPU:1, one launch (start us, length us, event | category | flops | bytes accessed | tf_op | source)
XLA Modules:
  0.0 477.3 jit_solution(17158128813222669277)
XLA Ops:
  0.0 2.2 copy.263
  2.2 10.3 %all-to-all-start = ((bf16[8,4,64,128]{3,0,1,2:T(8,128)(2,1)}), bf16[8,4,64,128]{3,0,1,2:T(8,128)(2,1)S(1)}, u32[]{:S(2)}, u32[]{:S(2)}) async-start(bf16[8,4,64,128]{3,0,1,2:T(8,128)(2,1)} %copy.263), calls=%async_computation | async-start | bytes 1048576 | tf_op jit(solution)/shard_map/all_to_all | solution.py:81
  14.5 7.5 %all-to-all-done = bf16[8,4,64,128]{3,0,1,2:T(8,128)(2,1)S(1)} async-done(((bf16[8,4,64,128]{3,0,1,2:T(8,128)(2,1)}), bf16[8,4,64,128]{3,0,1,2:T(8,128)(2,1)S(1)}, u32[]{:S(2)}, u32[]{:S(2)}) %all-to-all-start) | async-done | bytes 524320 | tf_op jit(solution)/shard_map/all_to_all | solution.py:81
  24.9 38.0 %all_to_all.137 = bf16[64,3,1,8,128]{4,3,2,1,0:T(8,128)(2,1)S(1)} all-to-all(bf16[64,3,1,8,128]{4,3,2,1,0:T(8,128)(2,1)S(1)} %get-tuple-element.355), channel_id=1, replica_groups=mesh['ctx'=64,'kv'=8] {'ctx'}, dimensions={0} | all-to-all | bytes 786432 | tf_op jit(solution)/shard_map/all_to_all | solution.py:104
  62.9 31.5 %all_to_all.138 = bf16[64,3,1,8,128]{4,3,2,1,0:T(8,128)(2,1)S(1)} all-to-all(bf16[64,3,1,8,128]{4,3,2,1,0:T(8,128)(2,1)S(1)} %get-tuple-element.358), channel_id=1, replica_groups=mesh['ctx'=64,'kv'=8] {'ctx'}, dimensions={0} | all-to-all | bytes 786432 | tf_op jit(solution)/shard_map/all_to_all | solution.py:104
  94.4 8.8 %all-to-all-start.5 = ((bf16[64,3,1,8,128]{4,3,2,1,0:T(8,128)(2,1)}), bf16[64,3,1,8,128]{4,3,2,1,0:T(8,128)(2,1)S(1)}, u32[]{:S(2)}, u32[]{:S(2)}) async-start(bf16[64,3,1,8,128]{4,3,2,1,0:T(8,128)(2,1)} %get-tuple-element.357), calls=%async_computation.5 | async-start | bytes 786432 | tf_op jit(solution)/shard_map/all_to_all | solution.py:104
  103.2 23.7 %all-to-all-done.5 = bf16[64,3,1,8,128]{4,3,2,1,0:T(8,128)(2,1)S(1)} async-done(((bf16[64,3,1,8,128]{4,3,2,1,0:T(8,128)(2,1)}), bf16[64,3,1,8,128]{4,3,2,1,0:T(8,128)(2,1)S(1)}, u32[]{:S(2)}, u32[]{:S(2)}) %all-to-all-start.5) | async-done | bytes 393248 | tf_op jit(solution)/shard_map/all_to_all | solution.py:104
  126.9 8.8 %all-to-all-start.7 = ((bf16[64,3,1,8,128]{4,3,2,1,0:T(8,128)(2,1)}), bf16[64,3,1,8,128]{4,3,2,1,0:T(8,128)(2,1)S(1)}, u32[]{:S(2)}, u32[]{:S(2)}) async-start(bf16[64,3,1,8,128]{4,3,2,1,0:T(8,128)(2,1)} %get-tuple-element.356), calls=%async_computation.7 | async-start | bytes 786432 | tf_op jit(solution)/shard_map/all_to_all | solution.py:104
  136.5 7.5 %while.60 = (s32[]{:T(128)}, bf16[2,32,3,1,8,128]{5,4,2,1,3,0:T(8,128)(2,1)}, f32[2,32,3,1,8]{4,2,1,3,0:T(4,128)S(1)}, f32[2,32,3,1,8]{4,2,1,3,0:T(4,128)S(1)}, ...) while((s32[]{:T(128)}, ...), condition=%wide.region_6.7_spmd.clone, body=%wide.region_3.6_spmd.clone.sunk | while | flops 411500032 | bytes 10636905 | solution.py:47
  144.8 14.5 %all-to-all-done.7 = bf16[64,3,1,8,128]{4,3,2,1,0:T(8,128)(2,1)S(1)} async-done(((bf16[64,3,1,8,128]{4,3,2,1,0:T(8,128)(2,1)}), bf16[64,3,1,8,128]{4,3,2,1,0:T(8,128)(2,1)S(1)}, u32[]{:S(2)}, u32[]{:S(2)}) %all-to-all-start.7) | async-done | bytes 393248 | tf_op jit(solution)/shard_map/all_to_all | solution.py:104
  159.3 8.9 %all-to-all-start.2 = ((f32[64,3,1,8]{3,2,1,0:T(1,128)}), f32[64,3,1,8]{3,2,1,0:T(1,128)S(1)}, u32[]{:S(2)}, u32[]{:S(2)}) async-start(f32[64,3,1,8]{3,2,1,0:T(1,128)} %copy.267), calls=%async_computation.2 | async-start | bytes 196608 | tf_op jit(solution)/shard_map/all_to_all | solution.py:118
  169.1 7.5 %while.61 = (s32[]{:T(128)}, bf16[2,32,3,1,8,128]{5,4,2,1,3,0:T(8,128)(2,1)}, f32[2,32,3,1,8]{4,2,1,3,0:T(4,128)S(1)}, f32[2,32,3,1,8]{4,2,1,3,0:T(4,128)S(1)}, ...) while((s32[]{:T(128)}, ...), condition=%wide.region_10.11_spmd.clone, body=%wide.region_7.10_spmd.clone.sunk | while | flops 411500032 | bytes 10636905 | solution.py:47
  177.4 5.4 %all-to-all-done.2 = f32[64,3,1,8]{3,2,1,0:T(1,128)S(1)} async-done(((f32[64,3,1,8]{3,2,1,0:T(1,128)}), f32[64,3,1,8]{3,2,1,0:T(1,128)S(1)}, u32[]{:S(2)}, u32[]{:S(2)}) %all-to-all-start.2) | async-done | bytes 6176 | tf_op jit(solution)/shard_map/all_to_all | solution.py:118
  182.8 9.3 %all-to-all-start.4 = ((f32[64,3,1,8]{3,2,1,0:T(1,128)}), f32[64,3,1,8]{3,2,1,0:T(1,128)S(1)}, u32[]{:S(2)}, u32[]{:S(2)}) async-start(f32[64,3,1,8]{3,2,1,0:T(1,128)} %copy.269), calls=%async_computation.4 | async-start | bytes 196608 | tf_op jit(solution)/shard_map/all_to_all | solution.py:118
  192.2 6.3 %while.62 = (s32[]{:T(128)}, bf16[2,32,3,1,8,128]{5,4,2,1,3,0:T(8,128)(2,1)S(1)}, f32[2,32,3,1,8]{4,2,1,3,0:T(4,128)S(1)}, f32[2,32,3,1,8]{4,2,1,3,0:T(4,128)S(1...) while((s32[]{:T(128)}, ...), condition=%wide.region_14.15_spmd.clone, body=%wide.region_11.14_spmd.clone.sunk | while | flops 411500032 | bytes 10761325 | solution.py:47
  199.2 7.3 %all-to-all-done.4 = f32[64,3,1,8]{3,2,1,0:T(1,128)S(1)} async-done(((f32[64,3,1,8]{3,2,1,0:T(1,128)}), f32[64,3,1,8]{3,2,1,0:T(1,128)S(1)}, u32[]{:S(2)}, u32[]{:S(2)}) %all-to-all-start.4) | async-done | bytes 6176 | tf_op jit(solution)/shard_map/all_to_all | solution.py:118
  206.6 7.2 %all-to-all-start.6 = ((f32[64,3,1,8]{3,2,1,0:T(1,128)}), f32[64,3,1,8]{3,2,1,0:T(1,128)S(1)}, u32[]{:S(2)}, u32[]{:S(2)}) async-start(f32[64,3,1,8]{3,2,1,0:T(1,128)} %copy.271), calls=%async_computation.6 | async-start | bytes 196608 | tf_op jit(solution)/shard_map/all_to_all | solution.py:118
  213.9 6.3 %while.63 = (s32[]{:T(128)}, bf16[2,32,3,1,8,128]{5,4,2,1,3,0:T(8,128)(2,1)S(1)}, f32[2,32,3,1,8]{4,2,1,3,0:T(4,128)S(1)}, f32[2,32,3,1,8]{4,2,1,3,0:T(4,128)S(1...) while((s32[]{:T(128)}, ...), condition=%wide.region_18.19_spmd.clone, body=%wide.region_15.18_spmd.clone.sunk | while | flops 411500032 | bytes 10761325 | solution.py:47
  221.0 7.4 %all-to-all-done.6 = f32[64,3,1,8]{3,2,1,0:T(1,128)S(1)} async-done(((f32[64,3,1,8]{3,2,1,0:T(1,128)}), f32[64,3,1,8]{3,2,1,0:T(1,128)S(1)}, u32[]{:S(2)}, u32[]{:S(2)}) %all-to-all-start.6) | async-done | bytes 6176 | tf_op jit(solution)/shard_map/all_to_all | solution.py:118
  228.4 7.1 %all-to-all-start.8 = ((f32[64,3,1,8]{3,2,1,0:T(1,128)}), f32[64,3,1,8]{3,2,1,0:T(1,128)S(1)}, u32[]{:S(2)}, u32[]{:S(2)}) async-start(f32[64,3,1,8]{3,2,1,0:T(1,128)} %copy.273), calls=%async_computation.8 | async-start | bytes 196608 | tf_op jit(solution)/shard_map/all_to_all | solution.py:118
  236.2 13.8 %all-to-all-done.8 = f32[64,3,1,8]{3,2,1,0:T(1,128)S(1)} async-done(((f32[64,3,1,8]{3,2,1,0:T(1,128)}), f32[64,3,1,8]{3,2,1,0:T(1,128)S(1)}, u32[]{:S(2)}, u32[]{:S(2)}) %all-to-all-start.8) | async-done | bytes 6176 | tf_op jit(solution)/shard_map/all_to_all | solution.py:118
  250.0 4.6 all-to-all-start.10
  255.4 13.7 %all-to-all-done.10 = f32[64,3,1,8]{3,2,1,0:T(1,128)S(1)} async-done(((f32[64,3,1,8]{3,2,1,0:T(1,128)}), f32[64,3,1,8]{3,2,1,0:T(1,128)S(1)}, u32[]{:S(2)}, u32[]{:S(2)}) %all-to-all-start.10) | async-done | bytes 6176 | tf_op jit(solution)/shard_map/all_to_all | solution.py:117
  269.1 4.8 all-to-all-start.11
  274.6 13.8 %all-to-all-done.11 = f32[64,3,1,8]{3,2,1,0:T(1,128)S(1)} async-done(((f32[64,3,1,8]{3,2,1,0:T(1,128)}), f32[64,3,1,8]{3,2,1,0:T(1,128)S(1)}, u32[]{:S(2)}, u32[]{:S(2)}) %all-to-all-start.11) | async-done | bytes 6176 | tf_op jit(solution)/shard_map/all_to_all | solution.py:117
  288.5 4.6 all-to-all-start.12
  293.2 14.4 %all-to-all-done.12 = f32[64,3,1,8]{3,2,1,0:T(1,128)S(1)} async-done(((f32[64,3,1,8]{3,2,1,0:T(1,128)}), f32[64,3,1,8]{3,2,1,0:T(1,128)S(1)}, u32[]{:S(2)}, u32[]{:S(2)}) %all-to-all-start.12) | async-done | bytes 6176 | tf_op jit(solution)/shard_map/all_to_all | solution.py:117
  307.6 19.0 %all_to_all.139 = f32[64,3,1,8]{3,2,1,0:T(1,128)} all-to-all(f32[64,3,1,8]{3,2,1,0:T(1,128)S(1)} %copy.281), channel_id=1, replica_groups=mesh['ctx'=64,'kv'=8] {'ctx'}, dimensions={0} | all-to-all | bytes 12288 | tf_op jit(solution)/shard_map/all_to_all | solution.py:117
  326.6 23.4 %all_to_all.140 = bf16[64,3,1,8,128]{4,3,1,2,0:T(8,128)(2,1)S(1)} all-to-all(bf16[64,3,1,8,128]{4,3,1,2,0:T(8,128)(2,1)S(1)} %bitcast.647), channel_id=1, replica_groups=mesh['ctx'=64,'kv'=8] {'ctx'}, dimensions={0} | all-to-all | bytes 786432 | tf_op jit(solution)/shard_map/all_to_all | solution.py:114
  349.9 24.5 %all_to_all.141 = bf16[64,3,1,8,128]{4,3,1,2,0:T(8,128)(2,1)S(1)} all-to-all(bf16[64,3,1,8,128]{4,3,1,2,0:T(8,128)(2,1)S(1)} %bitcast.648), channel_id=1, replica_groups=mesh['ctx'=64,'kv'=8] {'ctx'}, dimensions={0} | all-to-all | bytes 786432 | tf_op jit(solution)/shard_map/all_to_all | solution.py:114
  374.4 5.3 %all-to-all-start.16 = ((bf16[64,3,1,8,128]{4,3,1,2,0:T(8,128)(2,1)}), bf16[64,3,1,8,128]{4,3,1,2,0:T(8,128)(2,1)S(1)}, u32[]{:S(2)}, u32[]{:S(2)}) async-start(bf16[64,3,1,8,128]{4,3,1,2,0:T(8,128)(2,1)} %bitcast.125), calls=%async_computation.16 | async-start | bytes 786432 | tf_op jit(solution)/shard_map/all_to_all | solution.py:114
  380.1 3.3 fusion.167
  383.5 3.3 fusion.166
  386.7 12.6 %all-to-all-done.16 = bf16[64,3,1,8,128]{4,3,1,2,0:T(8,128)(2,1)S(1)} async-done(((bf16[64,3,1,8,128]{4,3,1,2,0:T(8,128)(2,1)}), bf16[64,3,1,8,128]{4,3,1,2,0:T(8,128)(2,1)S(1)}, u32[]{:S(2)}, u32[]{:S(2)}) %all-to-all-start.16) | async-done | bytes 393248 | tf_op jit(solution)/shard_map/all_to_all | solution.py:114
  399.3 5.5 %all-to-all-start.15 = ((bf16[64,3,1,8,128]{4,3,1,2,0:T(8,128)(2,1)}), bf16[64,3,1,8,128]{4,3,1,2,0:T(8,128)(2,1)S(1)}, u32[]{:S(2)}, u32[]{:S(2)}) async-start(bf16[64,3,1,8,128]{4,3,1,2,0:T(8,128)(2,1)} %bitcast.124), calls=%async_computation.15 | async-start | bytes 786432 | tf_op jit(solution)/shard_map/all_to_all | solution.py:114
  408.0 1.9 fusion.143
  409.9 2.3 fusion.153
  418.5 6.0 %all-to-all-done.15 = bf16[64,3,1,8,128]{4,3,1,2,0:T(8,128)(2,1)S(1)} async-done(((bf16[64,3,1,8,128]{4,3,1,2,0:T(8,128)(2,1)}), bf16[64,3,1,8,128]{4,3,1,2,0:T(8,128)(2,1)S(1)}, u32[]{:S(2)}, u32[]{:S(2)}) %all-to-all-start.15) | async-done | bytes 393248 | tf_op jit(solution)/shard_map/all_to_all | solution.py:114
  424.5 17.1 %all-to-all-start.14 = ((f32[8,1,512]{2,1,0:T(1,128)}), f32[8,1,512]{2,1,0:T(1,128)S(1)}, u32[]{:S(2)}, u32[]{:S(2)}) async-start(f32[8,1,512]{2,1,0:T(1,128)} %reshape.632), calls=%async_computation.14 | async-start | bytes 32768 | tf_op jit(solution)/shard_map/all_to_all | solution.py:170
  443.9 2.3 all-to-all-done.14
  446.2 4.0 all-to-all-start.9
  450.2 1.9 select_convert_fusion
  452.1 2.8 all-to-all-done.9
  454.9 4.2 all-to-all-start.19
  459.7 1.6 max.51
  461.3 2.7 fusion.134
  469.7 4.5 all-to-all-done.19
  474.9 2.0 fusion.141
  (172 shorter events, 58.4 us)
Async XLA Ops:
  0.0 461.3 %copy-start = (bf16[8,32,8,128]{3,2,1,0:T(8,128)(2,1)S(1)}, bf16[8,32,8,128]{3,2,1,0:T(8,128)(2,1)}, u32[]{:S(2)}) copy-start(bf16[8,32,8,128]{3,2,1,0:T(8,128)(2,1)} %param.24) | copy-start | bytes 1572868
  2.2 19.8 %all-to-all-start = ((bf16[8,4,64,128]{3,0,1,2:T(8,128)(2,1)}), bf16[8,4,64,128]{3,0,1,2:T(8,128)(2,1)S(1)}, u32[]{:S(2)}, u32[]{:S(2)}) async-start(bf16[8,4,64,128]{3,0,1,2:T(8,128)(2,1)} %copy.263), calls=%async_computation | async-start | bytes 1048576 | tf_op jit(solution)/shard_map/all_to_all | solution.py:81
  23.7 112.8 %copy-start.1 = (bf16[1,1024,1,128]{3,1,2,0:T(8,128)(2,1)S(1)}, bf16[1,1024,1,128]{3,1,2,0:T(8,128)(2,1)}, u32[]{:S(2)}) copy-start(bf16[1,1024,1,128]{3,1,2,0:T(8,128)(2,1)} %param.27) | copy-start | bytes 786436
  23.7 112.8 %copy-start.21 = (bf16[1,1024,1,128]{3,1,2,0:T(8,128)(2,1)S(1)}, bf16[1,1024,1,128]{3,1,2,0:T(8,128)(2,1)}, u32[]{:S(2)}) copy-start(bf16[1,1024,1,128]{3,1,2,0:T(8,128)(2,1)} %param.28) | copy-start | bytes 786436
  94.4 32.5 %all-to-all-start.5 = ((bf16[64,3,1,8,128]{4,3,2,1,0:T(8,128)(2,1)}), bf16[64,3,1,8,128]{4,3,2,1,0:T(8,128)(2,1)S(1)}, u32[]{:S(2)}, u32[]{:S(2)}) async-start(bf16[64,3,1,8,128]{4,3,2,1,0:T(8,128)(2,1)} %get-tuple-element.357), calls=%async_computation.5 | async-start | bytes 786432 | tf_op jit(solution)/shard_map/all_to_all | solution.py:104
  126.9 32.4 %all-to-all-start.7 = ((bf16[64,3,1,8,128]{4,3,2,1,0:T(8,128)(2,1)}), bf16[64,3,1,8,128]{4,3,2,1,0:T(8,128)(2,1)S(1)}, u32[]{:S(2)}, u32[]{:S(2)}) async-start(bf16[64,3,1,8,128]{4,3,2,1,0:T(8,128)(2,1)} %get-tuple-element.356), calls=%async_computation.7 | async-start | bytes 786432 | tf_op jit(solution)/shard_map/all_to_all | solution.py:104
  159.3 23.4 %all-to-all-start.2 = ((f32[64,3,1,8]{3,2,1,0:T(1,128)}), f32[64,3,1,8]{3,2,1,0:T(1,128)S(1)}, u32[]{:S(2)}, u32[]{:S(2)}) async-start(f32[64,3,1,8]{3,2,1,0:T(1,128)} %copy.267), calls=%async_computation.2 | async-start | bytes 196608 | tf_op jit(solution)/shard_map/all_to_all | solution.py:118
  182.8 23.8 %all-to-all-start.4 = ((f32[64,3,1,8]{3,2,1,0:T(1,128)}), f32[64,3,1,8]{3,2,1,0:T(1,128)S(1)}, u32[]{:S(2)}, u32[]{:S(2)}) async-start(f32[64,3,1,8]{3,2,1,0:T(1,128)} %copy.269), calls=%async_computation.4 | async-start | bytes 196608 | tf_op jit(solution)/shard_map/all_to_all | solution.py:118
  206.6 7.3 %copy-start.9 = (f32[64,3,1,8]{3,2,1,0:T(1,128)}, f32[64,3,1,8]{3,2,1,0:T(1,128)S(1)}, u32[]{:S(2)}) copy-start(f32[64,3,1,8]{3,2,1,0:T(1,128)S(1)} %all-to-all-done.4) | copy-start | bytes 18436
  206.6 21.8 %all-to-all-start.6 = ((f32[64,3,1,8]{3,2,1,0:T(1,128)}), f32[64,3,1,8]{3,2,1,0:T(1,128)S(1)}, u32[]{:S(2)}, u32[]{:S(2)}) async-start(f32[64,3,1,8]{3,2,1,0:T(1,128)} %copy.271), calls=%async_computation.6 | async-start | bytes 196608 | tf_op jit(solution)/shard_map/all_to_all | solution.py:118
  220.2 159.8 %copy-start.22 = (s32[8]{0:T(128)S(1)}, s32[8]{0:T(128)}, u32[]{:S(2)}) copy-start(s32[8]{0:T(128)} %param.25) | copy-start | bytes 100
  220.2 159.9 %copy-start.20 = (s32[64,2]{0,1:T(2,128)S(1)}, s32[64,2]{0,1:T(2,128)}, u32[]{:S(2)}) copy-start(s32[64,2]{0,1:T(2,128)} %param.26) | copy-start | bytes 1540
  220.2 159.9 %copy-start.8 = (bf16[8,4,64,128]{3,2,1,0:T(8,128)(2,1)S(1)}, bf16[8,4,64,128]{3,2,1,0:T(8,128)(2,1)}, u32[]{:S(2)}) copy-start(bf16[8,4,64,128]{3,2,1,0:T(8,128)(2,1)} %param.20) | copy-start | bytes 1572868
  228.4 151.7 %copy-start.11 = (f32[64,3,1,8]{3,2,1,0:T(1,128)}, f32[64,3,1,8]{3,2,1,0:T(1,128)S(1)}, u32[]{:S(2)}) copy-start(f32[64,3,1,8]{3,2,1,0:T(1,128)S(1)} %all-to-all-done.6) | copy-start | bytes 18436
  228.4 21.6 %all-to-all-start.8 = ((f32[64,3,1,8]{3,2,1,0:T(1,128)}), f32[64,3,1,8]{3,2,1,0:T(1,128)S(1)}, u32[]{:S(2)}, u32[]{:S(2)}) async-start(f32[64,3,1,8]{3,2,1,0:T(1,128)} %copy.273), calls=%async_computation.8 | async-start | bytes 196608 | tf_op jit(solution)/shard_map/all_to_all | solution.py:118
  250.0 130.1 %copy-start.12 = (f32[64,3,1,8]{3,2,1,0:T(1,128)}, f32[64,3,1,8]{3,2,1,0:T(1,128)S(1)}, u32[]{:S(2)}) copy-start(f32[64,3,1,8]{3,2,1,0:T(1,128)S(1)} %all-to-all-done.8) | copy-start | bytes 18436
  250.0 19.1 %all-to-all-start.10 = ((f32[64,3,1,8]{3,2,1,0:T(1,128)}), f32[64,3,1,8]{3,2,1,0:T(1,128)S(1)}, u32[]{:S(2)}, u32[]{:S(2)}) async-start(f32[64,3,1,8]{3,2,1,0:T(1,128)} %copy.275), calls=%async_computation.10 | async-start | bytes 196608 | tf_op jit(solution)/shard_map/all_to_all | solution.py:117
  269.1 111.0 %copy-start.13 = (f32[64,3,1,8]{3,2,1,0:T(1,128)}, f32[64,3,1,8]{3,2,1,0:T(1,128)S(1)}, u32[]{:S(2)}) copy-start(f32[64,3,1,8]{3,2,1,0:T(1,128)S(1)} %all-to-all-done.10) | copy-start | bytes 18436
  269.1 19.4 %all-to-all-start.11 = ((f32[64,3,1,8]{3,2,1,0:T(1,128)}), f32[64,3,1,8]{3,2,1,0:T(1,128)S(1)}, u32[]{:S(2)}, u32[]{:S(2)}) async-start(f32[64,3,1,8]{3,2,1,0:T(1,128)} %copy.277), calls=%async_computation.11 | async-start | bytes 196608 | tf_op jit(solution)/shard_map/all_to_all | solution.py:117
  288.5 98.3 %copy-start.14 = (f32[64,3,1,8]{3,2,1,0:T(1,128)}, f32[64,3,1,8]{3,2,1,0:T(1,128)S(1)}, u32[]{:S(2)}) copy-start(f32[64,3,1,8]{3,2,1,0:T(1,128)S(1)} %all-to-all-done.11) | copy-start | bytes 18436
  288.5 19.1 %all-to-all-start.12 = ((f32[64,3,1,8]{3,2,1,0:T(1,128)}), f32[64,3,1,8]{3,2,1,0:T(1,128)S(1)}, u32[]{:S(2)}, u32[]{:S(2)}) async-start(f32[64,3,1,8]{3,2,1,0:T(1,128)} %copy.279), calls=%async_computation.12 | async-start | bytes 196608 | tf_op jit(solution)/shard_map/all_to_all | solution.py:117
  307.6 79.2 %copy-start.15 = (f32[64,3,1,8]{3,2,1,0:T(1,128)}, f32[64,3,1,8]{3,2,1,0:T(1,128)S(1)}, u32[]{:S(2)}) copy-start(f32[64,3,1,8]{3,2,1,0:T(1,128)S(1)} %all-to-all-done.12) | copy-start | bytes 18436
  374.4 24.9 %all-to-all-start.16 = ((bf16[64,3,1,8,128]{4,3,1,2,0:T(8,128)(2,1)}), bf16[64,3,1,8,128]{4,3,1,2,0:T(8,128)(2,1)S(1)}, u32[]{:S(2)}, u32[]{:S(2)}) async-start(bf16[64,3,1,8,128]{4,3,1,2,0:T(8,128)(2,1)} %bitcast.125), calls=%async_computation.16 | async-start | bytes 786432 | tf_op jit(solution)/shard_map/all_to_all | solution.py:114
  383.4 28.7 %copy-start.2 = (f32[8,4,8,8,4]{3,4,1,2,0:T(4,128)}, f32[8,4,8,8,4]{3,4,1,2,0:T(4,128)S(1)}, u32[]{:S(2)}) copy-start(f32[8,4,8,8,4]{3,4,1,2,0:T(4,128)S(1)} %get-tuple-element.366) | copy-start | bytes 98308
  386.7 25.4 %copy-start.10 = (f32[64,3,1,8]{3,2,1,0:T(1,128)S(1)}, f32[64,3,1,8]{3,2,1,0:T(1,128)}, u32[]{:S(2)}) copy-start(f32[64,3,1,8]{3,2,1,0:T(1,128)} %copy-done.9) | copy-start | bytes 18436
  399.3 42.2 %copy-start.4 = (bf16[64,3,1,8,128]{4,3,1,2,0:T(8,128)(2,1)}, bf16[64,3,1,8,128]{4,3,1,2,0:T(8,128)(2,1)S(1)}, u32[]{:S(2)}) copy-start(bf16[64,3,1,8,128]{4,3,1,2,0:T(8,128)(2,1)S(1)} %all-to-all-done.16) | copy-start | bytes 1179652
  399.3 25.2 %all-to-all-start.15 = ((bf16[64,3,1,8,128]{4,3,1,2,0:T(8,128)(2,1)}), bf16[64,3,1,8,128]{4,3,1,2,0:T(8,128)(2,1)S(1)}, u32[]{:S(2)}, u32[]{:S(2)}) async-start(bf16[64,3,1,8,128]{4,3,1,2,0:T(8,128)(2,1)} %bitcast.124), calls=%async_computation.15 | async-start | bytes 786432 | tf_op jit(solution)/shard_map/all_to_all | solution.py:114
  424.5 17.1 %copy-start.5 = (bf16[64,3,1,8,128]{4,3,1,2,0:T(8,128)(2,1)}, bf16[64,3,1,8,128]{4,3,1,2,0:T(8,128)(2,1)S(1)}, u32[]{:S(2)}) copy-start(bf16[64,3,1,8,128]{4,3,1,2,0:T(8,128)(2,1)S(1)} %all-to-all-done.15) | copy-start | bytes 1179652
  424.5 21.7 %all-to-all-start.14 = ((f32[8,1,512]{2,1,0:T(1,128)}), f32[8,1,512]{2,1,0:T(1,128)S(1)}, u32[]{:S(2)}, u32[]{:S(2)}) async-start(f32[8,1,512]{2,1,0:T(1,128)} %reshape.632), calls=%async_computation.14 | async-start | bytes 32768 | tf_op jit(solution)/shard_map/all_to_all | solution.py:170
  443.9 15.1 %copy-start.3 = (f32[8,4,8,8,4]{3,4,1,2,0:T(4,128)S(1)}, f32[8,4,8,8,4]{3,4,1,2,0:T(4,128)}, u32[]{:S(2)}) copy-start(f32[8,4,8,8,4]{3,4,1,2,0:T(4,128)} %copy-done.2) | copy-start | bytes 98308
  443.9 17.4 %copy-start.6 = (f32[8,4,8,8,32]{4,3,1,2,0:T(8,128)S(1)}, f32[8,4,8,8,32]{4,3,1,2,0:T(8,128)}, u32[]{:S(2)}) copy-start(f32[8,4,8,8,32]{4,3,1,2,0:T(8,128)} %get-tuple-element.364) | copy-start | bytes 786436
  446.2 13.3 %copy-start.16 = (f32[8,1,512]{2,1,0:T(1,128)}, f32[8,1,512]{2,1,0:T(1,128)S(1)}, u32[]{:S(2)}) copy-start(f32[8,1,512]{2,1,0:T(1,128)S(1)} %all-to-all-done.14) | copy-start | bytes 49156
  446.2 8.6 %all-to-all-start.9 = ((f32[8,1,512]{2,1,0:T(1,128)}), f32[8,1,512]{2,1,0:T(1,128)S(1)}, u32[]{:S(2)}, u32[]{:S(2)}) async-start(f32[8,1,512]{2,1,0:T(1,128)} %reshape.630), calls=%async_computation.9 | async-start | bytes 32768 | tf_op jit(solution)/shard_map/all_to_all | solution.py:171
  454.9 4.2 copy-start.18
  454.9 19.3 %all-to-all-start.19 = ((bf16[64,2,4,8,128]{4,3,2,1,0:T(8,128)(2,1)}), bf16[64,2,4,8,128]{4,3,2,1,0:T(8,128)(2,1)S(1)}, u32[]{:S(2)}, u32[]{:S(2)}) async-start(bf16[64,2,4,8,128]{4,3,2,1,0:T(8,128)(2,1)} %select_convert_fusion), calls=%async_computation.19 | async-start | bytes 2097152 | tf_op jit(solution)/shard_map/all_to_all | solution.py:167
  459.6 4.9 %copy-start.17 = (f32[8,1,512]{2,1,0:T(1,128)S(1)}, f32[8,1,512]{2,1,0:T(1,128)}, u32[]{:S(2)}) copy-start(f32[8,1,512]{2,1,0:T(1,128)} %copy-done.16) | copy-start | bytes 49156
  459.6 6.0 %copy-start.19 = (f32[8,1,512]{2,1,0:T(1,128)S(1)}, f32[8,1,512]{2,1,0:T(1,128)}, u32[]{:S(2)}) copy-start(f32[8,1,512]{2,1,0:T(1,128)} %copy-done.18) | copy-start | bytes 49156
  464.0 10.9 %copy-start.7 = (f32[8,4,8,8,128]{4,3,1,2,0:T(8,128)S(1)}, f32[8,4,8,8,128]{4,3,1,2,0:T(8,128)}, u32[]{:S(2)}) copy-start(f32[8,4,8,8,128]{4,3,1,2,0:T(8,128)} %fusion.134) | copy-start | bytes 3145732
where the time goes:
time: 486 us; the launch traced here: 477 us
  waiting for transfers between devices  150 us (31%)
  blocking collectives  136 us (28%)
  starting transfers between devices  110 us (23%)
  other arithmetic  28.5 us (6%)
  matrix products  27 us (6%)
  local copies, waits for them, and re-layouts  24.1 us (5%)
    all_to_all x2, blocking collectives, per_device(): lax.all_to_all(outgoing[:, :, step:step + 1], 'ctx', split_axis=0, concat...  69.5 us
    all_to_all x2, blocking collectives, per_device(): lax.all_to_all(step_part[0].astype(jnp.float32), 'ctx', split_axis=0, con...  47.9 us
    all_to_all x3, waiting for transfers between devices, per_device(): lax.all_to_all(step_part[1], 'ctx', split_axis=0, concat_axis=0, tiled=True)  42 us
    all_to_all x2, waiting for transfers between devices, per_device(): lax.all_to_all(outgoing[:, :, step:step + 1], 'ctx', split_axis=0, concat...  38.2 us
    all_to_all x4, waiting for transfers between devices, per_device(): lax.all_to_all(step_part[2], 'ctx', split_axis=0, concat_axis=0, tiled=True)  33.9 us
    all_to_all x4, starting transfers between devices, per_device(): lax.all_to_all(step_part[2], 'ctx', split_axis=0, concat_axis=0, tiled=True)  32.6 us
    all_to_all x1, blocking collectives, per_device(): lax.all_to_all(step_part[1], 'ctx', split_axis=0, concat_axis=0, tiled=True)  19 us
    all_to_all x2, waiting for transfers between devices, per_device(): lax.all_to_all(step_part[0].astype(jnp.float32), 'ctx', split_axis=0, con...  18.6 us
  transfers between devices with their start and end apart: 15, of which 15 were waited for; matrix products, arithmetic and copies ran while one was open for 15% of the time, Pallas kernels for 0%

commit v1 on v0

v1 whole, which is shorter than its diff:
```python
import functools
import math

import jax
import jax.numpy as jnp
from jax import lax
from jax.experimental import pallas as pl
from jax.experimental.pallas import tpu as pltpu
from jax.sharding import Mesh
from jax.sharding import PartitionSpec as P

NZ, NX, NY, NC = 16, 4, 4, 2
NKV = NY * NC
CAP = 3
F32 = jnp.float32
BF16 = jnp.bfloat16
VMEM_LIMIT = 48 * 1024 * 1024
VM = pl.BlockSpec(memory_space=pltpu.VMEM)


def params():
    return pltpu.CompilerParams(vmem_limit_bytes=VMEM_LIMIT)


def split3(x):
    hi = x.astype(BF16).astype(F32)
    rest = x - hi
    mid = rest.astype(BF16).astype(F32)
    return [hi, mid, rest - mid]


def lane_stats(values, rows):
    lane = lax.broadcasted_iota(jnp.int32, (rows, 128), 1)
    out = jnp.zeros((rows, 128), F32)
    for i, v in enumerate(values):
        out = jnp.where(lane == i, v, out)
    return out


def pad_rows(x, rows):
    if x.shape[0] == rows:
        return x
    return jnp.concatenate([x, jnp.zeros((rows - x.shape[0], x.shape[1]), x.dtype)], axis=0)


def suffix_kernel(scale, steps, len_ref, q_ref, k_ref, nk_ref, v_ref, nv_ref, sum_ref, stat_ref):
    row = pl.program_id(0)
    length = len_ref[row]
    q = q_ref[0]
    heads = q.shape[0] // steps
    kvh = nk_ref.shape[1] // steps
    group = heads // kvh

    def scores(keys):
        return lax.dot_general(q, keys, (((1,), (1,)), ((), ())), preferred_element_type=F32) * scale

    def masks(cols):
        qi = lax.broadcasted_iota(jnp.int32, (q.shape[0], cols), 0)
        ci = lax.broadcasted_iota(jnp.int32, (q.shape[0], cols), 1)
        same = ((qi % heads) // group) == (ci % kvh)
        return same, ci // kvh, qi // heads

    same, slot, _ = masks(k_ref.shape[1])
    own = jnp.where(same & (slot < length), scores(k_ref[0]), -jnp.inf)
    same, slot, step = masks(nk_ref.shape[1])
    fresh = jnp.where(same & (slot <= step), scores(nk_ref[0]), -jnp.inf)
    top = jnp.maximum(jnp.max(own, axis=1, keepdims=True), jnp.max(fresh, axis=1, keepdims=True))
    own_w = jnp.exp(own - top)
    fresh_w = jnp.exp(fresh - top)
    total = jnp.sum(own_w, axis=1, keepdims=True) + jnp.sum(fresh_w, axis=1, keepdims=True)
    acc = jnp.dot(own_w.astype(BF16), v_ref[0], preferred_element_type=F32)
    acc = acc + jnp.dot(fresh_w.astype(BF16), nv_ref[0], preferred_element_type=F32)
    sum_ref[0] = acc
    both = lane_stats([top, total], q.shape[0])
    for b in range(0, q.shape[0], 128):
        columns = both[b : b + 128]
        stat_ref[0, :, b : b + 128] = pad_rows(columns, 128).T[:8, : columns.shape[0]]


def suffix_part(queries, new_keys, new_values, suffix_keys, suffix_values, suffix_length):
    rows, steps, heads, dim = queries.shape
    slots, kvh = suffix_keys.shape[1:3]
    qn, kn, fn = steps * heads, slots * kvh, steps * kvh
    block = lambda n: pl.BlockSpec((1, n, dim), lambda i, s: (i, 0, 0))
    ssum, sstat = pl.pallas_call(
        functools.partial(suffix_kernel, dim ** (-0.5), steps),
        grid_spec=pltpu.PrefetchScalarGridSpec(
            num_scalar_prefetch=1,
            grid=(rows,),
            in_specs=[block(qn), block(kn), block(fn), block(kn), block(fn)],
            out_specs=[block(qn), pl.BlockSpec((1, 8, qn), lambda i, s: (i, 0, 0))],
        ),
        out_shape=[
            jax.ShapeDtypeStruct((rows, qn, dim), F32),
            jax.ShapeDtypeStruct((rows, 8, qn), F32),
        ],
        compiler_params=params(),
        cost_estimate=pl.CostEstimate(
            flops=4 * rows * qn * kn * dim, bytes_accessed=4 << 20, transcendentals=rows * qn * kn
        ),
        name="suffix",
    )(
        suffix_length,
        queries.reshape(rows, qn, dim),
        suffix_keys.reshape(rows, kn, dim),
        new_keys.reshape(rows, fn, dim),
        suffix_values.reshape(rows, kn, dim),
        new_values.reshape(rows, fn, dim),
    )
    group = heads // kvh
    stat = sstat[:, :2].reshape(rows, 2, steps, kvh, group).transpose(1, 3, 0, 2, 4)
    stat = stat.reshape(2, kvh, rows, steps * group)
    return ssum, jnp.pad(stat, ((0, 0), (0, 0), (0, 0), (0, 128 - steps * group)))


def pack_kernel(table_ref, q_ref, out_ref):
    rows = q_ref.shape[0]

    def one(j, carry):
        entry = jnp.maximum(table_ref[j], 0)
        out_ref[j] = q_ref[lax.rem(entry, rows)]
        return carry

    lax.fori_loop(0, out_ref.shape[0], one, 0, unroll=8)


def pack_part(table, grouped):
    rows, per_row, dim = grouped.shape
    return pl.pallas_call(
        pack_kernel,
        grid_spec=pltpu.PrefetchScalarGridSpec(
            num_scalar_prefetch=1, grid=(), in_specs=[VM], out_specs=VM
        ),
        out_shape=jax.ShapeDtypeStruct((table.shape[0], per_row, dim), BF16),
        compiler_params=params(),
        cost_estimate=pl.CostEstimate(flops=1 << 16, bytes_accessed=2 << 20, transcendentals=0),
        name="pack",
    )(table, grouped)


def node_kernel(scale, count, *refs):
    q_refs, kv_refs, out_ref = refs[:count], refs[count:-1], refs[-1]
    stats = []
    for i in range(count):
        q = q_refs[i][...]
        each = q.shape[1] * q.shape[2]
        m_all = NX * each
        q = q.reshape(m_all, q.shape[3])
        slots = (kv_refs[i].shape[0] - 16) // 2
        keys, values, tail = kv_refs[i][:slots], kv_refs[i][slots : 2 * slots], kv_refs[i][2 * slots :]
        length = tail[:8].astype(F32)
        length = length[0:1, :] * 32.0 + length[1:2, :]
        length = jnp.concatenate([length] * (slots // 128), axis=1)
        s = lax.dot_general(q, keys, (((1,), (1,)), ((), ())), preferred_element_type=F32)
        col = lax.broadcasted_iota(jnp.int32, (1, slots), 1).astype(F32)
        s = jnp.where(col < length, s, -jnp.inf)
        top = jnp.max(s, axis=1, keepdims=True)
        w = jnp.exp2((s - top) * (scale * math.log2(math.e)))
        total = jnp.sum(w, axis=1, keepdims=True)
        o = jnp.dot(w.astype(BF16), values, preferred_element_type=F32) * (1.0 / total)
        o = o.astype(BF16).reshape(NX, each, o.shape[1])
        for x in range(NX):
            out_ref[x, i * each : (i + 1) * each] = o[x]
        stats += split3(top * scale) + split3(total)
    packed = lane_stats(stats, m_all)
    for x in range(NX):
        block = pad_rows(packed[x * each : (x + 1) * each], 128)
        out_ref[x, count * each :] = block.T[: out_ref.shape[1] - count * each].astype(BF16)


def node_part(q_slots, offsets, kvs):
    count = len(offsets)
    per_row, dim = q_slots.shape[2:]
    each = CAP * per_row
    work = NX * each * 1024 * count
    q_block = lambda off: pl.BlockSpec((NX, CAP, per_row, dim), lambda i: (0, off, 0, 0))
    return pl.pallas_call(
        functools.partial(node_kernel, dim ** (-0.5), count),
        grid=(1,),
        in_specs=[q_block(o) for o in offsets] + [VM] * len(kvs),
        out_specs=pl.BlockSpec((NX, count * each + 16, dim), lambda i: (0, 0, 0)),
        out_shape=jax.ShapeDtypeStruct((NX, count * each + 16, dim), BF16),
        compiler_params=params(),
        cost_estimate=pl.CostEstimate(flops=4 * work * dim, bytes_accessed=count << 20, transcendentals=work),
        name="node",
    )(*[q_slots] * count, *kvs)


def merge_kernel(groups, rows, per_row, table_ref, *refs):
    arrived = refs[: len(groups)]
    out_ref, e_out, e_max, e_total = refs[len(groups) :]
    each = CAP * per_row
    for ref, steps in zip(arrived, groups):
        base = 0
        for offsets in steps:
            count = len(offsets)
            for x in range(NX):
                tile = ref[x, base + count * each : base + count * each + 16].astype(F32)
                for i, off in enumerate(offsets):
                    top = tile[6 * i : 6 * i + 1] + tile[6 * i + 1 : 6 * i + 2] + tile[6 * i + 2 : 6 * i + 3]
                    total = tile[6 * i + 3 : 6 * i + 4] + tile[6 * i + 4 : 6 * i + 5] + tile[6 * i + 5 : 6 * i + 6]
                    for k in range(CAP):
                        entry = table_ref[(x * NZ + off) * CAP + k]
                        entry = jnp.where(entry < 0, 2 * rows, entry)
                        start = base + i * each + k * per_row
                        e_out[entry] = ref[x, start : start + per_row]
                        if k:
                            top_k = pltpu.roll(top, 128 - k * per_row, 1)
                            total_k = pltpu.roll(total, 128 - k * per_row, 1)
                        else:
                            top_k, total_k = top, total
                        e_max[pl.ds(entry, 1), :] = top_k
                        e_total[pl.ds(entry, 1), :] = total_k
            base += count * each + 16
    m0, m1 = e_max[:rows], e_max[rows : 2 * rows]
    top = jnp.maximum(m0, m1)
    w0 = e_total[:rows] * jnp.exp(m0 - top)
    w1 = e_total[rows : 2 * rows] * jnp.exp(m1 - top)
    total = w0 + w1
    f0 = pad_rows(w0 / total, 128).T
    f1 = pad_rows(w1 / total, 128).T
    rows_here = rows // NKV
    pieces = split3(top) + split3(total)
    tail = rows_here * per_row
    for y in range(NKV):
        for r in range(rows_here):
            row = y * rows_here + r
            o = f0[:per_row, row : row + 1] * e_out[row].astype(F32)
            o = o + f1[:per_row, row : row + 1] * e_out[rows + row].astype(F32)
            out_ref[y, r * per_row : (r + 1) * per_row] = o.astype(BF16)
        part = [p[y * rows_here : (y + 1) * rows_here] for p in pieces]
        part = pad_rows(jnp.concatenate(part, axis=0), out_ref.shape[1] - tail)
        out_ref[y, tail:] = part.astype(BF16)


def merge_part(table, arrived, groups, rows, per_row):
    dim = arrived[0].shape[2]
    rows_here = rows // NKV
    stat_rows = -(-6 * rows_here // 16) * 16
    shape = (NKV, rows_here * per_row + stat_rows, dim)
    return pl.pallas_call(
        functools.partial(merge_kernel, groups, rows, per_row),
        grid_spec=pltpu.PrefetchScalarGridSpec(
            num_scalar_prefetch=1,
            grid=(),
            in_specs=[VM] * len(arrived),
            out_specs=VM,
            scratch_shapes=[
                pltpu.VMEM((2 * rows + 1, per_row, dim), BF16),
                pltpu.VMEM((2 * rows + 8, 128), F32),
                pltpu.VMEM((2 * rows + 8, 128), F32),
            ],
        ),
        out_shape=jax.ShapeDtypeStruct(shape, BF16),
        compiler_params=params(),
        cost_estimate=pl.CostEstimate(flops=1 << 22, bytes_accessed=4 << 20, transcendentals=1 << 16),
        name="merge",
    )(table, *arrived)


def final_kernel(rows, steps, arrived_ref, ssum_ref, sstat_ref, out_ref, res_ref):
    group = ssum_ref.shape[2]
    per_row = steps * group
    here = rows * per_row
    w_prefix, w_suffix = [], []
    for j in range(NKV):
        tile = arrived_ref[j, here:].astype(F32)
        part = [tile[i * rows : (i + 1) * rows] for i in range(6)]
        p_max, p_total = part[0] + part[1] + part[2], part[3] + part[4] + part[5]
        s_max, s_total = sstat_ref[0, j], sstat_ref[1, j]
        top = jnp.maximum(p_max, s_max)
        wp = p_total * jnp.exp(p_max - top)
        ws = jnp.exp(s_max - top)
        inverse = 1.0 / (wp + ws * s_total)
        w_prefix.append(wp * inverse)
        w_suffix.append(ws * inverse)
    w_prefix = pad_rows(jnp.concatenate(w_prefix, axis=0), 128).T
    w_suffix = pad_rows(jnp.concatenate(w_suffix, axis=0), 128).T
    for j in range(NKV):
        for r in range(rows):
            at = j * rows + r
            o = arrived_ref[j, r * per_row : (r + 1) * per_row].astype(F32)
            own = ssum_ref[r * steps : (r + 1) * steps, j].reshape(per_row, o.shape[1])
            mixed = w_prefix[:per_row, at : at + 1] * o + w_suffix[:per_row, at : at + 1] * own
            res_ref[r * steps : (r + 1) * steps, j] = mixed.reshape(steps, group, o.shape[1])
    out_ref[...] = res_ref[...].reshape(out_ref.shape).astype(BF16)


def final_part(arrived, ssum, sstat, rows, steps, heads, dim):
    shape = (rows * steps, NKV, heads // NKV, dim)
    out = pl.pallas_call(
        functools.partial(final_kernel, rows, steps),
        in_specs=[VM] * 3,
        out_specs=VM,
        out_shape=jax.ShapeDtypeStruct((rows * steps * heads, dim), BF16),
        scratch_shapes=[pltpu.VMEM(shape, F32)],
        compiler_params=params(),
        cost_estimate=pl.CostEstimate(flops=1 << 22, bytes_accessed=4 << 20, transcendentals=1 << 16),
        name="final",
    )(arrived, ssum.reshape(shape), sstat)
    return out.reshape(rows, steps, heads, dim)


def entry_table(row_nodes, zi):
    rows, depth = row_nodes.shape
    node = row_nodes.T.reshape(rows * depth)
    entry = jnp.arange(rows * depth, dtype=jnp.int32)
    earlier = (node[:, None] == node[None, :]) & (entry[None, :] < entry[:, None])
    rank = jnp.sum(earlier.astype(jnp.int32), axis=1)
    offset = jnp.mod(node // NX - zi, NZ)
    place = (jnp.mod(node, NX) * NZ + offset) * CAP + rank
    hit = place[:, None] == jnp.arange(NX * NZ * CAP, dtype=jnp.int32)[None, :]
    return jnp.sum(jnp.where(hit, entry[:, None] + 1, 0), axis=0) - 1


def per_device(
    queries, new_keys, new_values, suffix_keys, suffix_values, suffix_length,
    row_nodes, prefix_keys, prefix_values, node_length,
):
    rows_dev, depth = row_nodes.shape
    rows_here, steps, heads, dim = queries.shape
    group = heads // NKV
    per_row = steps * group
    zi = lax.axis_index("z")
    half = NZ // 2

    slots = prefix_keys.shape[1]
    length = node_length[0]
    digits = jnp.stack([length // 32, length % 32]).astype(BF16)
    tail = jnp.broadcast_to(jnp.pad(digits, (0, 14))[:, None], (16, dim))
    own = jnp.concatenate([prefix_keys.reshape(slots, dim), prefix_values.reshape(slots, dim), tail])
    up = [(i, (i + 1) % NZ) for i in range(NZ)]
    down = [(i, (i - 1) % NZ) for i in range(NZ)]

    tie = lax.optimization_barrier
    by_head = queries.reshape(rows_here * steps, NKV, group, dim).transpose(1, 0, 2, 3)
    by_head, own = tie((by_head, own))
    grouped = lax.all_to_all(by_head, ("y", "core"), split_axis=0, concat_axis=0, tiled=True)
    grouped = grouped.reshape(rows_dev, per_row, dim)
    table = entry_table(row_nodes, zi)
    ssum, sstat = suffix_part(queries, new_keys, new_values, suffix_keys, suffix_values, suffix_length)

    plan = [[0]] + [[NZ - s, s] for s in range(1, half)] + [[half]]
    cuts = [range(0, 4), range(4, half - 1), range(half - 1, half + 1)]
    groups = [[plan[s] for s in cut] for cut in cuts]

    def send_back(blocks):
        return lax.all_to_all(jnp.concatenate(blocks, axis=1), "x", split_axis=0, concat_axis=0, tiled=True)

    due = {2: [], 4: [], 5: [0, 1, 2], 6: [3, 4], 7: [5, 6]}
    arrived = [[own]]
    sent = []
    going_up = going_down = own
    for s in range(1, half):
        going_up, going_down = lax.ppermute(going_up, "z", up), lax.ppermute(going_down, "z", down)
        if s == 2:
            going_up, grouped = tie((going_up, grouped))
            packed = pack_part(table, grouped).reshape(NX, NZ * CAP, per_row, dim)
            q_slots = lax.all_to_all(packed, "x", split_axis=0, concat_axis=0, tiled=True)
        elif s == 4:
            going_up, q_slots = tie((going_up, q_slots))
        if due.get(s):
            fresh = [node_part(q_slots, plan[t], arrived[t]) for t in due[s]]
            going_up, fresh = tie((going_up, fresh))
            sent += fresh
        arrived.append([going_up, going_down])
    farthest = lax.ppermute(going_up, "z", up)
    sent.append(node_part(q_slots, plan[half - 1], arrived[half - 1]))
    sent.append(node_part(q_slots, plan[half], [farthest]))
    back = [send_back([sent[s] for s in cut]) for cut in cuts]
    merged = merge_part(table, back, groups, rows_dev, per_row)
    home = lax.all_to_all(merged, ("y", "core"), split_axis=0, concat_axis=0, tiled=True)
    return final_part(home, ssum, sstat, rows_here, steps, heads, dim)


def solution(mesh):
    fine = Mesh(mesh.devices.reshape(NZ, NX, NY, NC), ("z", "x", "y", "core"))
    ctx, kv = ("z", "x"), ("y", "core")
    everything = ctx + kv
    return jax.shard_map(
        per_device,
        mesh=fine,
        in_specs=(
            P(everything), P(everything), P(everything), P(everything), P(everything), P(everything),
            P(ctx, None),
            P(ctx, None, kv, None),
            P(ctx, None, kv, None),
            P(ctx),
        ),
        out_specs=P(everything),
        check_vma=False,
    )
```

time: 486 us -> 181 us (0.37); the launches traced: 477 us -> 180 us
  blocking collectives: 136 us -> 9.78 us
  waiting for transfers between devices: 150 us -> 42.5 us
  Pallas kernels: 0 us -> 33.4 us
  matrix products: 27 us -> 0 us
  starting transfers between devices: 110 us -> 84 us
  other arithmetic: 28.5 us -> 2.58 us
  local copies, waits for them, and re-layouts: 24.1 us -> 6.77 us
    all_to_all x15 -> x5, waiting for transfers between devices: 150 us -> 8.16 us  [the longest x1 4.49 us: per_device(): lax.all_to_all(merged, ('y', 'core'), split_axis=0, concat_axis=0, tiled=...]
    all_to_all x5 -> x1, blocking collectives: 136 us -> 9.78 us  [send_back(): lax.all_to_all(jnp.concatenate(blocks, axis=1), 'x', split_axis=0, concat...]
    all_to_all x15 -> x5, starting transfers between devices: 110 us -> 30.9 us  [the longest x1 13.8 us: per_device(): lax.all_to_all(merged, ('y', 'core'), split_axis=0, concat_axis=0, tiled=...]
    ppermute x0 -> x15, starting transfers between devices: none -> 53.1 us  [the longest x7 33.6 us: per_device(): lax.ppermute(going_down, 'z', down)]
    ppermute x0 -> x15, waiting for transfers between devices: none -> 34.4 us  [the longest x7 17.9 us: per_device(): lax.ppermute(going_down, 'z', down)]
    pallas_call x0 -> x13, Pallas kernels: none -> 33.4 us  [the longest x9 22 us: node_part(): pl.pallas_call(functools.partial(node_kernel, dim ** (-0.5), count), grid...]
    dot_general x20 -> x0, matrix products: 27 us -> none  [the longest x8 9.64 us: one_block(): jnp.einsum('pksjgl,ljd->pksjgd', weights.astype(jnp.bfloat16), node_value...]
    reduce_sum x14 -> x2, other arithmetic: 10 us -> 0.29 us  [the longest x1 0.17 us: entry_table(): rank = jnp.sum(earlier.astype(jnp.int32), axis=1)]
  transfers between devices with their start and end apart: 15 -> 20, of which waited for: 15 -> 10; matrix products, arithmetic and copies ran while one was open for 15% -> 1% of each run, Pallas kernels for 0% -> 16%
where the time goes in v1:
time: 181 us; the launch traced here: 180 us
  starting transfers between devices  84 us (46%)
  waiting for transfers between devices  42.5 us (23%)
  Pallas kernels  33.4 us (18%)
  blocking collectives  9.78 us (5%)
  local copies, waits for them, and re-layouts  6.77 us (4%)
  other arithmetic  2.58 us (1%)
    ppermute x7, starting transfers between devices, per_device(): lax.ppermute(going_down, 'z', down)  33.6 us
    pallas_call x9, Pallas kernels, node_part(): pl.pallas_call(functools.partial(node_kernel, dim ** (-0.5), count), grid...  22 us
    ppermute x7, waiting for transfers between devices, per_device(): lax.ppermute(going_down, 'z', down)  17.9 us
    ppermute x7, starting transfers between devices, per_device(): lax.ppermute(going_up, 'z', up)  17.6 us
    ppermute x7, waiting for transfers between devices, per_device(): lax.ppermute(going_up, 'z', up)  14.9 us
    all_to_all x1, starting transfers between devices, per_device(): lax.all_to_all(merged, ('y', 'core'), split_axis=0, concat_axis=0, tiled=...  13.8 us
    all_to_all x1, blocking collectives, send_back(): lax.all_to_all(jnp.concatenate(blocks, axis=1), 'x', split_axis=0, concat...  9.78 us
    all_to_all x2, starting transfers between devices, send_back(): lax.all_to_all(jnp.concatenate(blocks, axis=1), 'x', split_axis=0, concat...  7.69 us
  transfers between devices with their start and end apart: 20, of which 10 were waited for; matrix products, arithmetic and copies ran while one was open for 1% of the time, Pallas kernels for 16%

profile of v1, /device:TPU:1, one launch (start us, length us, event | category | flops | bytes accessed | tf_op | source)
XLA Modules:
  0.0 180.2 jit_solution(1111257090437143052)
XLA Ops:
  0.7 1.9 %copy.17 = bf16[32,8,8,128]{3,2,0,1:T(8,128)(2,1)} copy(bf16[32,8,8,128]{3,2,1,0:T(8,128)(2,1)} %bitcast.26) | data formatting | bytes 1048576 | tf_op jit(solution)/shard_map/reshape | solution.py:336
  3.1 4.4 %collective-permute-start = (bf16[2064,128]{1,0:T(8,128)(2,1)S(1)}, bf16[2064,128]{1,0:T(8,128)(2,1)S(1)}, u32[]{:S(2)}, u32[]{:S(2)}) collective-permute-start(bf16[2064,128]{1,0:T(8,128)(2,1)S(1)} %maximum_maximum_fusion.refs_1_), channel_id=1, source_target_pairs={{0,32},{32,64},{64,96},{96,128},{128,160},{160,192},{192,224},{224... | collective-permute-start | bytes 1585160 | tf_op jit(solution)/shard_map/ppermute | solution.py:355
  7.5 9.5 %collective-permute-start.5 = (bf16[2064,128]{1,0:T(8,128)(2,1)S(1)}, bf16[2064,128]{1,0:T(8,128)(2,1)S(1)}, u32[]{:S(2)}, u32[]{:S(2)}) collective-permute-start(bf16[2064,128]{1,0:T(8,128)(2,1)S(1)} %maximum_maximum_fusion.refs_1_), channel_id=1, source_target_pairs={{0,480},{32,0},{64,32},{96,64},{128,96},{160,128},{192,160},{224,1... | collective-permute-start | bytes 1585160 | tf_op jit(solution)/shard_map/ppermute | solution.py:355
  17.0 5.4 %all-to-all-start = ((bf16[8,32,8,128]{3,2,1,0:T(8,128)(2,1)}), bf16[8,32,8,128]{3,2,1,0:T(8,128)(2,1)S(1)}, u32[]{:S(2)}, u32[]{:S(2)}) async-start(bf16[8,32,8,128]{3,2,1,0:T(8,128)(2,1)} %bitcast.20), calls=%async_computation | async-start | bytes 1048576 | tf_op jit(solution)/shard_map/all_to_all | solution.py:338
  22.7 4.1 %collective-permute-done.refs_2_ = bf16[2064,128]{1,0:T(8,128)(2,1)S(1)} collective-permute-done((bf16[2064,128]{1,0:T(8,128)(2,1)S(1)}, bf16[2064,128]{1,0:T(8,128)(2,1)S(1)}, u32[]{:S(2)}, u32[]{:S(2)}) %collective-permute-start) | collective-permute-done | bytes 528416 | tf_op jit(solution)/shard_map/ppermute | solution.py:355
  26.8 1.9 %collective-permute-start.1 = (bf16[2064,128]{1,0:T(8,128)(2,1)S(1)}, bf16[2064,128]{1,0:T(8,128)(2,1)S(1)}, u32[]{:S(2)}, u32[]{:S(2)}) collective-permute-start(bf16[2064,128]{1,0:T(8,128)(2,1)S(1)} %collective-permute-done.refs_2_), channel_id=1, source_target_pairs={{0,32},{32,64},{64,96},{96,128},{128,160},{160,192},{192,224},{224... | collective-permute-start | bytes 1585160 | tf_op jit(solution)/shard_map/ppermute | solution.py:355
  28.9 3.1 %all-to-all-done = bf16[8,32,8,128]{3,2,1,0:T(8,128)(2,1)S(1)} async-done(((bf16[8,32,8,128]{3,2,1,0:T(8,128)(2,1)}), bf16[8,32,8,128]{3,2,1,0:T(8,128)(2,1)S(1)}, u32[]{:S(2)}, u32[]{:S(2)}) %all-to-all-start) | async-done | bytes 524320 | tf_op jit(solution)/shard_map/all_to_all | solution.py:338
  31.9 10.2 %collective-permute-done.1.refs_2_ = bf16[2064,128]{1,0:T(8,128)(2,1)S(1)} collective-permute-done((bf16[2064,128]{1,0:T(8,128)(2,1)S(1)}, bf16[2064,128]{1,0:T(8,128)(2,1)S(1)}, u32[]{:S(2)}, u32[]{:S(2)}) %collective-permute-start.1) | collective-permute-done | bytes 528416 | tf_op jit(solution)/shard_map/ppermute | solution.py:355
  42.2 0.8 copy-done.1
  43.0 2.2 %pack.1 = bf16[192,32,128]{2,1,0:T(8,128)(2,1)} custom-call(s32[192]{0:T(256)S(1)} %broadcast_add_fusion.table_ref, bf16[64,32,128]{2,1,0:T(8,128)(2,1)S(1)} %bitcast.28), custom_call_target="tpu_custom_call" | custom-call | flops 65536 | bytes 2097152 | tf_op jit(solution)/shard_map/pack/pallas_call | solution.py:129
  45.7 4.0 %all-to-all-start.1 = ((bf16[4,48,32,128]{3,2,1,0:T(8,128)(2,1)}), bf16[4,48,32,128]{3,2,1,0:T(8,128)(2,1)S(1)}, u32[]{:S(2)}, u32[]{:S(2)}) async-start(bf16[4,48,32,128]{3,2,1,0:T(8,128)(2,1)} %bitcast.9), calls=%async_computation.1 | async-start | bytes 3145728 | tf_op jit(solution)/shard_map/all_to_all | solution.py:359
  49.8 1.9 %collective-permute-start.6 = (bf16[2064,128]{1,0:T(8,128)(2,1)S(1)}, bf16[2064,128]{1,0:T(8,128)(2,1)S(1)}, u32[]{:S(2)}, u32[]{:S(2)}) collective-permute-start(bf16[2064,128]{1,0:T(8,128)(2,1)S(1)} %collective-permute-done.5.refs_3_), channel_id=1, source_target_pairs={{0,480},{32,0},{64,32},{96,64},{128,96},{160,128},{192,160},{224,1... | collective-permute-start | bytes 1585160 | tf_op jit(solution)/shard_map/ppermute | solution.py:355
  51.7 3.4 %collective-permute-start.2 = (bf16[2064,128]{1,0:T(8,128)(2,1)}, bf16[2064,128]{1,0:T(8,128)(2,1)S(1)}, u32[]{:S(2)}, u32[]{:S(2)}) collective-permute-start(bf16[2064,128]{1,0:T(8,128)(2,1)} %copy-done.1), channel_id=1, source_target_pairs={{0,32},{32,64},{64,96},{96,128},{128,160},{160,192},{192,224},{224... | collective-permute-start | bytes 1585160 | tf_op jit(solution)/shard_map/ppermute | solution.py:355
  55.0 7.7 %collective-permute-done.6.refs_3_ = bf16[2064,128]{1,0:T(8,128)(2,1)S(1)} collective-permute-done((bf16[2064,128]{1,0:T(8,128)(2,1)S(1)}, bf16[2064,128]{1,0:T(8,128)(2,1)S(1)}, u32[]{:S(2)}, u32[]{:S(2)}) %collective-permute-start.6) | collective-permute-done | bytes 528416 | tf_op jit(solution)/shard_map/ppermute | solution.py:355
  62.7 3.2 %collective-permute-start.8 = (bf16[2064,128]{1,0:T(8,128)(2,1)S(1)}, bf16[2064,128]{1,0:T(8,128)(2,1)}, u32[]{:S(2)}, u32[]{:S(2)}) collective-permute-start(bf16[2064,128]{1,0:T(8,128)(2,1)S(1)} %collective-permute-done.6.refs_3_), channel_id=1, source_target_pairs={{0,480},{32,0},{64,32},{96,64},{128,96},{160,128},{192,160},{224,1... | collective-permute-start | bytes 1585160 | tf_op jit(solution)/shard_map/ppermute | solution.py:355
  65.9 0.8 copy-done.7
  66.7 2.1 %collective-permute-start.3 = (bf16[2064,128]{1,0:T(8,128)(2,1)S(1)}, bf16[2064,128]{1,0:T(8,128)(2,1)}, u32[]{:S(2)}, u32[]{:S(2)}) collective-permute-start(bf16[2064,128]{1,0:T(8,128)(2,1)S(1)} %collective-permute-done.2.refs_2_), channel_id=1, source_target_pairs={{0,32},{32,64},{64,96},{96,128},{128,160},{160,192},{192,224},{224... | collective-permute-start | bytes 1585160 | tf_op jit(solution)/shard_map/ppermute | solution.py:355
  68.8 0.8 copy-done.3
  69.6 5.3 %collective-permute-done.8.refs_3_ = bf16[2064,128]{1,0:T(8,128)(2,1)} collective-permute-done((bf16[2064,128]{1,0:T(8,128)(2,1)S(1)}, bf16[2064,128]{1,0:T(8,128)(2,1)}, u32[]{:S(2)}, u32[]{:S(2)}) %collective-permute-start.8) | collective-permute-done | bytes 528416 | tf_op jit(solution)/shard_map/ppermute | solution.py:355
  74.9 4.5 %collective-permute-start.9 = (bf16[2064,128]{1,0:T(8,128)(2,1)}, bf16[2064,128]{1,0:T(8,128)(2,1)}, u32[]{:S(2)}, u32[]{:S(2)}) collective-permute-start(bf16[2064,128]{1,0:T(8,128)(2,1)} %collective-permute-done.8.refs_3_), channel_id=1, source_target_pairs={{0,480},{32,0},{64,32},{96,64},{128,96},{160,128},{192,160},{224,1... | collective-permute-start | bytes 1585160 | tf_op jit(solution)/shard_map/ppermute | solution.py:355
  79.9 1.9 %collective-permute-start.4 = (bf16[2064,128]{1,0:T(8,128)(2,1)}, bf16[2064,128]{1,0:T(8,128)(2,1)S(1)}, u32[]{:S(2)}, u32[]{:S(2)}) collective-permute-start(bf16[2064,128]{1,0:T(8,128)(2,1)} %collective-permute-done.3.refs_2_), channel_id=1, source_target_pairs={{0,32},{32,64},{64,96},{96,128},{128,160},{160,192},{192,224},{224... | collective-permute-start | bytes 1585160 | tf_op jit(solution)/shard_map/ppermute | solution.py:355
  81.8 5.0 %collective-permute-done.9.refs_3_ = bf16[2064,128]{1,0:T(8,128)(2,1)} collective-permute-done((bf16[2064,128]{1,0:T(8,128)(2,1)}, bf16[2064,128]{1,0:T(8,128)(2,1)}, u32[]{:S(2)}, u32[]{:S(2)}) %collective-permute-start.9) | collective-permute-done | bytes 528416 | tf_op jit(solution)/shard_map/ppermute | solution.py:355
  86.8 5.3 %collective-permute-start.11 = (bf16[2064,128]{1,0:T(8,128)(2,1)}, bf16[2064,128]{1,0:T(8,128)(2,1)}, u32[]{:S(2)}, u32[]{:S(2)}) collective-permute-start(bf16[2064,128]{1,0:T(8,128)(2,1)} %collective-permute-done.9.refs_3_), channel_id=1, source_target_pairs={{0,480},{32,0},{64,32},{96,64},{128,96},{160,128},{192,160},{224,1... | collective-permute-start | bytes 1585160 | tf_op jit(solution)/shard_map/ppermute | solution.py:355
  92.1 1.2 node.9
  93.3 1.9 %node.10 = bf16[4,208,128]{2,1,0:T(8,128)(2,1)S(1)} custom-call(bf16[4,48,32,128]{3,2,1,0:T(8,128)(2,1)S(1)} %all-to-all-done.1.refs_0_.refs_1_, bf16[4,48,32,128]{3,2,1,0:T(8,128)(2,1)S(1)} %all-to-all-done.1.refs_0_.refs_1_, bf16[2064,128]{1,0:T(8,128)(2,1)S(1)} %collective-permute-done.refs_2_, bf16[2064,128]{1,0:T(8,128)(2,1)S(1)} %collective-permute-done.5.refs_3_), custom_call_target="tpu_custom_call" | custom-call | flops 402653184 | bytes 2097152 | tf_op jit(solution)/shard_map/node/pallas_call | solution.py:177
  95.2 1.9 %node.11 = bf16[4,208,128]{2,1,0:T(8,128)(2,1)S(1)} custom-call(bf16[4,48,32,128]{3,2,1,0:T(8,128)(2,1)S(1)} %all-to-all-done.1.refs_0_.refs_1_, bf16[4,48,32,128]{3,2,1,0:T(8,128)(2,1)S(1)} %all-to-all-done.1.refs_0_.refs_1_, bf16[2064,128]{1,0:T(8,128)(2,1)S(1)} %copy-done.2, bf16[2064,128]{1,0:T(8,128)(2,1)S(1)} %copy-done.8), custom_call_target="tpu_custom_call" | custom-call | flops 402653184 | bytes 2097152 | tf_op jit(solution)/shard_map/node/pallas_call | solution.py:177
  97.1 1.9 %collective-permute-start.7 = (bf16[2064,128]{1,0:T(8,128)(2,1)S(1)}, bf16[2064,128]{1,0:T(8,128)(2,1)}, u32[]{:S(2)}, u32[]{:S(2)}) collective-permute-start(bf16[2064,128]{1,0:T(8,128)(2,1)S(1)} %collective-permute-done.4.refs_2_), channel_id=1, source_target_pairs={{0,32},{32,64},{64,96},{96,128},{128,160},{160,192},{192,224},{224... | collective-permute-start | bytes 1585160 | tf_op jit(solution)/shard_map/ppermute | solution.py:355
  99.0 2.9 %node.12 = bf16[4,208,128]{2,1,0:T(8,128)(2,1)S(1)} custom-call(bf16[4,48,32,128]{3,2,1,0:T(8,128)(2,1)S(1)} %all-to-all-done.1.refs_0_.refs_1_, bf16[4,48,32,128]{3,2,1,0:T(8,128)(2,1)S(1)} %all-to-all-done.1.refs_0_.refs_1_, bf16[2064,128]{1,0:T(8,128)(2,1)S(1)} %copy-done.4, bf16[2064,128]{1,0:T(8,128)(2,1)} %collective-permute-done.8.refs_3_), custom_call_target="tpu_custom_call" | custom-call | flops 402653184 | bytes 2097152 | tf_op jit(solution)/shard_map/node/pallas_call | solution.py:177
  101.9 4.6 %collective-permute-start.12 = (bf16[2064,128]{1,0:T(8,128)(2,1)}, bf16[2064,128]{1,0:T(8,128)(2,1)}, u32[]{:S(2)}, u32[]{:S(2)}) collective-permute-start(bf16[2064,128]{1,0:T(8,128)(2,1)} %collective-permute-done.11.refs_3_), channel_id=1, source_target_pairs={{0,480},{32,0},{64,32},{96,64},{128,96},{160,128},{192,160},{224,1... | collective-permute-start | bytes 1585160 | tf_op jit(solution)/shard_map/ppermute | solution.py:355
  106.5 3.0 %node.13 = bf16[4,208,128]{2,1,0:T(8,128)(2,1)S(1)} custom-call(bf16[4,48,32,128]{3,2,1,0:T(8,128)(2,1)S(1)} %all-to-all-done.1.refs_0_.refs_1_, bf16[4,48,32,128]{3,2,1,0:T(8,128)(2,1)S(1)} %all-to-all-done.1.refs_0_.refs_1_, bf16[2064,128]{1,0:T(8,128)(2,1)} %collective-permute-done.3.refs_2_, bf16[2064,128]{1,0:T(8,128)(2,1)} %collective-permute-done.9.refs_3_), custom_call_target="tpu_custom_call" | custom-call | flops 402653184 | bytes 2097152 | tf_op jit(solution)/shard_map/node/pallas_call | solution.py:177
  109.6 2.1 %collective-permute-start.10 = (bf16[2064,128]{1,0:T(8,128)(2,1)}, bf16[2064,128]{1,0:T(8,128)(2,1)}, u32[]{:S(2)}, u32[]{:S(2)}) collective-permute-start(bf16[2064,128]{1,0:T(8,128)(2,1)} %collective-permute-done.7.refs_2_), channel_id=1, source_target_pairs={{0,32},{32,64},{64,96},{96,128},{128,160},{160,192},{192,224},{224... | collective-permute-start | bytes 1585160 | tf_op jit(solution)/shard_map/ppermute | solution.py:355
  111.6 0.9 pad_maximum_fusion
  112.6 3.7 %all-to-all-start.2 = ((bf16[4,736,128]{2,1,0:T(8,128)(2,1)}), bf16[4,736,128]{2,1,0:T(8,128)(2,1)S(1)}, u32[]{:S(2)}, u32[]{:S(2)}) async-start(bf16[4,736,128]{2,1,0:T(8,128)(2,1)} %pad_maximum_fusion), calls=%async_computation.2 | async-start | bytes 1507328 | tf_op jit(solution)/shard_map/all_to_all | solution.py:348
  116.3 2.9 %node.14 = bf16[4,208,128]{2,1,0:T(8,128)(2,1)S(1)} custom-call(bf16[4,48,32,128]{3,2,1,0:T(8,128)(2,1)S(1)} %all-to-all-done.1.refs_0_.refs_1_, bf16[4,48,32,128]{3,2,1,0:T(8,128)(2,1)S(1)} %all-to-all-done.1.refs_0_.refs_1_, bf16[2064,128]{1,0:T(8,128)(2,1)S(1)} %copy-done.6, bf16[2064,128]{1,0:T(8,128)(2,1)} %collective-permute-done.11.refs_3_), custom_call_target="tpu_custom_call" | custom-call | flops 402653184 | bytes 2097152 | tf_op jit(solution)/shard_map/node/pallas_call | solution.py:177
  119.1 4.6 %collective-permute-start.13 = (bf16[2064,128]{1,0:T(8,128)(2,1)}, bf16[2064,128]{1,0:T(8,128)(2,1)}, u32[]{:S(2)}, u32[]{:S(2)}) collective-permute-start(bf16[2064,128]{1,0:T(8,128)(2,1)} %collective-permute-done.12.refs_3_), channel_id=1, source_target_pairs={{0,480},{32,0},{64,32},{96,64},{128,96},{160,128},{192,160},{224,1... | collective-permute-start | bytes 1585160 | tf_op jit(solution)/shard_map/ppermute | solution.py:355
  123.7 3.0 %node.15 = bf16[4,208,128]{2,1,0:T(8,128)(2,1)S(1)} custom-call(bf16[4,48,32,128]{3,2,1,0:T(8,128)(2,1)S(1)} %all-to-all-done.1.refs_0_.refs_1_, bf16[4,48,32,128]{3,2,1,0:T(8,128)(2,1)S(1)} %all-to-all-done.1.refs_0_.refs_1_, bf16[2064,128]{1,0:T(8,128)(2,1)} %collective-permute-done.7.refs_2_, bf16[2064,128]{1,0:T(8,128)(2,1)} %collective-permute-done.12.refs_3_), custom_call_target="tpu_custom_call" | custom-call | flops 402653184 | bytes 2097152 | tf_op jit(solution)/shard_map/node/pallas_call | solution.py:177
  126.8 1.9 %collective-permute-start.14 = (bf16[2064,128]{1,0:T(8,128)(2,1)}, bf16[2064,128]{1,0:T(8,128)(2,1)}, u32[]{:S(2)}, u32[]{:S(2)}) collective-permute-start(bf16[2064,128]{1,0:T(8,128)(2,1)} %collective-permute-done.10.refs_2_), channel_id=1, source_target_pairs={{0,32},{32,64},{64,96},{96,128},{128,160},{160,192},{192,224},{224... | collective-permute-start | bytes 1585160 | tf_op jit(solution)/shard_map/ppermute | solution.py:367
  128.7 0.9 pad_maximum_fusion.1
  129.6 4.0 %all-to-all-start.3 = ((bf16[4,624,128]{2,1,0:T(8,128)(2,1)}), bf16[4,624,128]{2,1,0:T(8,128)(2,1)S(1)}, u32[]{:S(2)}, u32[]{:S(2)}) async-start(bf16[4,624,128]{2,1,0:T(8,128)(2,1)} %pad_maximum_fusion.1), calls=%async_computation.3 | async-start | bytes 1277952 | tf_op jit(solution)/shard_map/all_to_all | solution.py:348
  133.6 3.0 %node.16 = bf16[4,208,128]{2,1,0:T(8,128)(2,1)S(1)} custom-call(bf16[4,48,32,128]{3,2,1,0:T(8,128)(2,1)S(1)} %all-to-all-done.1.refs_0_.refs_1_, bf16[4,48,32,128]{3,2,1,0:T(8,128)(2,1)S(1)} %all-to-all-done.1.refs_0_.refs_1_, bf16[2064,128]{1,0:T(8,128)(2,1)} %collective-permute-done.10.refs_2_, bf16[2064,128]{1,0:T(8,128)(2,1)} %collective-permute-done.13.refs_3_), custom_call_target="tpu_custom_call" | custom-call | flops 402653184 | bytes 2097152 | tf_op jit(solution)/shard_map/node/pallas_call | solution.py:177
  136.6 1.6 collective-permute-done.14.refs_1_
  138.3 2.3 %node.17 = bf16[4,112,128]{2,1,0:T(8,128)(2,1)S(1)} custom-call(bf16[4,48,32,128]{3,2,1,0:T(8,128)(2,1)S(1)} %all-to-all-done.1.refs_0_.refs_1_, bf16[2064,128]{1,0:T(8,128)(2,1)} %collective-permute-done.14.refs_1_), custom_call_target="tpu_custom_call" | custom-call | flops 201326592 | bytes 1048576 | tf_op jit(solution)/shard_map/node/pallas_call | solution.py:177
  141.2 9.8 %all_to_all.30.refs_2_ = bf16[4,320,128]{2,1,0:T(8,128)(2,1)S(1)} all-to-all(bf16[4,320,128]{2,1,0:T(8,128)(2,1)S(1)} %pad_maximum_fusion.2), channel_id=1, replica_groups=mesh['z'=16,'x'=4,'y'=4,'core'=2] {'x'}, dimensions={0} | all-to-all | bytes 655360 | tf_op jit(solution)/shard_map/all_to_all | solution.py:348
  151.6 2.7 %merge.1 = bf16[8,304,128]{2,1,0:T(8,128)(2,1)} custom-call(s32[192]{0:T(256)S(1)} %copy-done.14, bf16[4,736,128]{2,1,0:T(8,128)(2,1)S(1)} %all-to-all-done.2.refs_0_, bf16[4,624,128]{2,1,0:T(8,128)(2,1)S(1)} %all-to-all-done.3.refs_1_, bf16[4,320,128]{2,1,0:T(8,128)(2,1)S(1)} %all_to_all.30.refs_2_), custom_call_target="tpu_custom_call" | custom-call | flops 4194304 | bytes 4194304 | tf_op jit(solution)/shard_map/merge/pallas_call | solution.py:241
  154.3 13.8 %all-to-all-start.5 = ((bf16[8,304,128]{2,1,0:T(8,128)(2,1)}), bf16[8,304,128]{2,1,0:T(8,128)(2,1)S(1)}, u32[]{:S(2)}, u32[]{:S(2)}) async-start(bf16[8,304,128]{2,1,0:T(8,128)(2,1)} %merge.1), calls=%async_computation.5 | async-start | bytes 1245184 | tf_op jit(solution)/shard_map/all_to_all | solution.py:372
  168.8 4.9 %suffix.1 = (f32[8,256,128]{2,1,0:T(8,128)S(1)}, f32[8,8,256]{2,1,0:T(8,128)S(1)}) custom-call(s32[8]{0:T(128)S(1)} %copy-done.15, bf16[8,256,128]{2,1,0:T(8,128)(2,1)S(1)} %bitcast.27, bf16[8,256,128]{2,1,0:T(8,128)(2,1)S(1)} %bitcast.30, bf16[8,32,128]{2,1,0:T(8,128)(2,1)S(1)} %bitcast.32, bf16[8,256,128]{2,1,0:T(8,128)(2,1)S(1)} %bitcast.31, ...), custom_call_target="tpu_custom_call" | custom-call | flops 268435456 | bytes 4194304 | tf_op jit(solution)/shard_map/suffix/pallas_call | solution.py:85
  174.1 4.5 %all-to-all-done.5.arrived_ref = bf16[8,304,128]{2,1,0:T(8,128)(2,1)S(1)} async-done(((bf16[8,304,128]{2,1,0:T(8,128)(2,1)}), bf16[8,304,128]{2,1,0:T(8,128)(2,1)S(1)}, u32[]{:S(2)}, u32[]{:S(2)}) %all-to-all-start.5) | async-done | bytes 622624 | tf_op jit(solution)/shard_map/all_to_all | solution.py:372
  178.6 1.6 final.1
  (61 shorter events, 4.3 us)
Async XLA Ops:
  0.0 2.8 %copy-start.16 = (bf16[1,1024,1,128]{3,1,2,0:T(8,128)(2,1)S(1)}, bf16[1,1024,1,128]{3,1,2,0:T(8,128)(2,1)}, u32[]{:S(2)}) copy-start(bf16[1,1024,1,128]{3,1,2,0:T(8,128)(2,1)} %param.18) | copy-start | bytes 786436
  0.0 2.8 %copy-start.17 = (bf16[1,1024,1,128]{3,1,2,0:T(8,128)(2,1)S(1)}, bf16[1,1024,1,128]{3,1,2,0:T(8,128)(2,1)}, u32[]{:S(2)}) copy-start(bf16[1,1024,1,128]{3,1,2,0:T(8,128)(2,1)} %param.17) | copy-start | bytes 786436
  2.7 19.8 %copy-start.18 = (s32[64,2]{0,1:T(2,128)S(1)}, s32[64,2]{0,1:T(2,128)}, u32[]{:S(2)}) copy-start(s32[64,2]{0,1:T(2,128)} %param.16) | copy-start | bytes 1540
  3.1 23.7 %collective-permute-start = (bf16[2064,128]{1,0:T(8,128)(2,1)S(1)}, bf16[2064,128]{1,0:T(8,128)(2,1)S(1)}, u32[]{:S(2)}, u32[]{:S(2)}) collective-permute-start(bf16[2064,128]{1,0:T(8,128)(2,1)S(1)} %maximum_maximum_fusion.refs_1_), channel_id=1, source_target_pairs={{0,32},{32,64},{64,96},{96,128},{128,160},{160,192},{192,224},{224... | collective-permute-start | bytes 1585160 | tf_op jit(solution)/shard_map/ppermute | solution.py:355
  7.5 42.3 %collective-permute-start.5 = (bf16[2064,128]{1,0:T(8,128)(2,1)S(1)}, bf16[2064,128]{1,0:T(8,128)(2,1)S(1)}, u32[]{:S(2)}, u32[]{:S(2)}) collective-permute-start(bf16[2064,128]{1,0:T(8,128)(2,1)S(1)} %maximum_maximum_fusion.refs_1_), channel_id=1, source_target_pairs={{0,480},{32,0},{64,32},{96,64},{128,96},{160,128},{192,160},{224,1... | collective-permute-start | bytes 1585160 | tf_op jit(solution)/shard_map/ppermute | solution.py:355
  17.0 14.9 %all-to-all-start = ((bf16[8,32,8,128]{3,2,1,0:T(8,128)(2,1)}), bf16[8,32,8,128]{3,2,1,0:T(8,128)(2,1)S(1)}, u32[]{:S(2)}, u32[]{:S(2)}) async-start(bf16[8,32,8,128]{3,2,1,0:T(8,128)(2,1)} %bitcast.20), calls=%async_computation | async-start | bytes 1048576 | tf_op jit(solution)/shard_map/all_to_all | solution.py:338
  26.8 15.4 %collective-permute-start.1 = (bf16[2064,128]{1,0:T(8,128)(2,1)S(1)}, bf16[2064,128]{1,0:T(8,128)(2,1)S(1)}, u32[]{:S(2)}, u32[]{:S(2)}) collective-permute-start(bf16[2064,128]{1,0:T(8,128)(2,1)S(1)} %collective-permute-done.refs_2_), channel_id=1, source_target_pairs={{0,32},{32,64},{64,96},{96,128},{128,160},{160,192},{192,224},{224... | collective-permute-start | bytes 1585160 | tf_op jit(solution)/shard_map/ppermute | solution.py:355
  42.2 0.8 copy-start.1
  45.2 0.6 copy-start.13
  45.7 34.1 %all-to-all-start.1 = ((bf16[4,48,32,128]{3,2,1,0:T(8,128)(2,1)}), bf16[4,48,32,128]{3,2,1,0:T(8,128)(2,1)S(1)}, u32[]{:S(2)}, u32[]{:S(2)}) async-start(bf16[4,48,32,128]{3,2,1,0:T(8,128)(2,1)} %bitcast.9), calls=%async_computation.1 | async-start | bytes 3145728 | tf_op jit(solution)/shard_map/all_to_all | solution.py:359
  49.8 13.0 %collective-permute-start.6 = (bf16[2064,128]{1,0:T(8,128)(2,1)S(1)}, bf16[2064,128]{1,0:T(8,128)(2,1)S(1)}, u32[]{:S(2)}, u32[]{:S(2)}) collective-permute-start(bf16[2064,128]{1,0:T(8,128)(2,1)S(1)} %collective-permute-done.5.refs_3_), channel_id=1, source_target_pairs={{0,480},{32,0},{64,32},{96,64},{128,96},{160,128},{192,160},{224,1... | collective-permute-start | bytes 1585160 | tf_op jit(solution)/shard_map/ppermute | solution.py:355
  51.7 15.1 %collective-permute-start.2 = (bf16[2064,128]{1,0:T(8,128)(2,1)}, bf16[2064,128]{1,0:T(8,128)(2,1)S(1)}, u32[]{:S(2)}, u32[]{:S(2)}) collective-permute-start(bf16[2064,128]{1,0:T(8,128)(2,1)} %copy-done.1), channel_id=1, source_target_pairs={{0,32},{32,64},{64,96},{96,128},{128,160},{160,192},{192,224},{224... | collective-permute-start | bytes 1585160 | tf_op jit(solution)/shard_map/ppermute | solution.py:355
  62.7 12.1 %collective-permute-start.8 = (bf16[2064,128]{1,0:T(8,128)(2,1)S(1)}, bf16[2064,128]{1,0:T(8,128)(2,1)}, u32[]{:S(2)}, u32[]{:S(2)}) collective-permute-start(bf16[2064,128]{1,0:T(8,128)(2,1)S(1)} %collective-permute-done.6.refs_3_), channel_id=1, source_target_pairs={{0,480},{32,0},{64,32},{96,64},{128,96},{160,128},{192,160},{224,1... | collective-permute-start | bytes 1585160 | tf_op jit(solution)/shard_map/ppermute | solution.py:355
  65.9 0.8 copy-start.7
  66.7 13.2 %collective-permute-start.3 = (bf16[2064,128]{1,0:T(8,128)(2,1)S(1)}, bf16[2064,128]{1,0:T(8,128)(2,1)}, u32[]{:S(2)}, u32[]{:S(2)}) collective-permute-start(bf16[2064,128]{1,0:T(8,128)(2,1)S(1)} %collective-permute-done.2.refs_2_), channel_id=1, source_target_pairs={{0,32},{32,64},{64,96},{96,128},{128,160},{160,192},{192,224},{224... | collective-permute-start | bytes 1585160 | tf_op jit(solution)/shard_map/ppermute | solution.py:355
  68.8 0.8 copy-start.3
  74.9 11.9 %collective-permute-start.9 = (bf16[2064,128]{1,0:T(8,128)(2,1)}, bf16[2064,128]{1,0:T(8,128)(2,1)}, u32[]{:S(2)}, u32[]{:S(2)}) collective-permute-start(bf16[2064,128]{1,0:T(8,128)(2,1)} %collective-permute-done.8.refs_3_), channel_id=1, source_target_pairs={{0,480},{32,0},{64,32},{96,64},{128,96},{160,128},{192,160},{224,1... | collective-permute-start | bytes 1585160 | tf_op jit(solution)/shard_map/ppermute | solution.py:355
  79.9 17.2 %collective-permute-start.4 = (bf16[2064,128]{1,0:T(8,128)(2,1)}, bf16[2064,128]{1,0:T(8,128)(2,1)S(1)}, u32[]{:S(2)}, u32[]{:S(2)}) collective-permute-start(bf16[2064,128]{1,0:T(8,128)(2,1)} %collective-permute-done.3.refs_2_), channel_id=1, source_target_pairs={{0,32},{32,64},{64,96},{96,128},{128,160},{160,192},{192,224},{224... | collective-permute-start | bytes 1585160 | tf_op jit(solution)/shard_map/ppermute | solution.py:355
  86.8 15.2 %collective-permute-start.11 = (bf16[2064,128]{1,0:T(8,128)(2,1)}, bf16[2064,128]{1,0:T(8,128)(2,1)}, u32[]{:S(2)}, u32[]{:S(2)}) collective-permute-start(bf16[2064,128]{1,0:T(8,128)(2,1)} %collective-permute-done.9.refs_3_), channel_id=1, source_target_pairs={{0,480},{32,0},{64,32},{96,64},{128,96},{160,128},{192,160},{224,1... | collective-permute-start | bytes 1585160 | tf_op jit(solution)/shard_map/ppermute | solution.py:355
  93.3 1.9 %copy-start.2 = (bf16[2064,128]{1,0:T(8,128)(2,1)S(1)}, bf16[2064,128]{1,0:T(8,128)(2,1)}, u32[]{:S(2)}) copy-start(bf16[2064,128]{1,0:T(8,128)(2,1)} %copy-done.1) | copy-start | bytes 1585156
  93.3 1.9 %copy-start.8 = (bf16[2064,128]{1,0:T(8,128)(2,1)S(1)}, bf16[2064,128]{1,0:T(8,128)(2,1)}, u32[]{:S(2)}) copy-start(bf16[2064,128]{1,0:T(8,128)(2,1)} %copy-done.7) | copy-start | bytes 1585156
  95.2 3.8 %copy-start.4 = (bf16[2064,128]{1,0:T(8,128)(2,1)S(1)}, bf16[2064,128]{1,0:T(8,128)(2,1)}, u32[]{:S(2)}) copy-start(bf16[2064,128]{1,0:T(8,128)(2,1)} %copy-done.3) | copy-start | bytes 1585156
  97.1 4.8 %copy-start.5 = (bf16[2064,128]{1,0:T(8,128)(2,1)}, bf16[2064,128]{1,0:T(8,128)(2,1)S(1)}, u32[]{:S(2)}) copy-start(bf16[2064,128]{1,0:T(8,128)(2,1)S(1)} %collective-permute-done.4.refs_2_) | copy-start | bytes 1585156
  97.1 12.5 %collective-permute-start.7 = (bf16[2064,128]{1,0:T(8,128)(2,1)S(1)}, bf16[2064,128]{1,0:T(8,128)(2,1)}, u32[]{:S(2)}, u32[]{:S(2)}) collective-permute-start(bf16[2064,128]{1,0:T(8,128)(2,1)S(1)} %collective-permute-done.4.refs_2_), channel_id=1, source_target_pairs={{0,32},{32,64},{64,96},{96,128},{128,160},{160,192},{192,224},{224... | collective-permute-start | bytes 1585160 | tf_op jit(solution)/shard_map/ppermute | solution.py:355
  101.9 17.2 %collective-permute-start.12 = (bf16[2064,128]{1,0:T(8,128)(2,1)}, bf16[2064,128]{1,0:T(8,128)(2,1)}, u32[]{:S(2)}, u32[]{:S(2)}) collective-permute-start(bf16[2064,128]{1,0:T(8,128)(2,1)} %collective-permute-done.11.refs_3_), channel_id=1, source_target_pairs={{0,480},{32,0},{64,32},{96,64},{128,96},{160,128},{192,160},{224,1... | collective-permute-start | bytes 1585160 | tf_op jit(solution)/shard_map/ppermute | solution.py:355
  109.6 6.7 %copy-start.6 = (bf16[2064,128]{1,0:T(8,128)(2,1)S(1)}, bf16[2064,128]{1,0:T(8,128)(2,1)}, u32[]{:S(2)}) copy-start(bf16[2064,128]{1,0:T(8,128)(2,1)} %copy-done.5) | copy-start | bytes 1585156
  109.6 17.2 %collective-permute-start.10 = (bf16[2064,128]{1,0:T(8,128)(2,1)}, bf16[2064,128]{1,0:T(8,128)(2,1)}, u32[]{:S(2)}, u32[]{:S(2)}) collective-permute-start(bf16[2064,128]{1,0:T(8,128)(2,1)} %collective-permute-done.7.refs_2_), channel_id=1, source_target_pairs={{0,32},{32,64},{64,96},{96,128},{128,160},{160,192},{192,224},{224... | collective-permute-start | bytes 1585160 | tf_op jit(solution)/shard_map/ppermute | solution.py:355
  112.6 17.0 %all-to-all-start.2 = ((bf16[4,736,128]{2,1,0:T(8,128)(2,1)}), bf16[4,736,128]{2,1,0:T(8,128)(2,1)S(1)}, u32[]{:S(2)}, u32[]{:S(2)}) async-start(bf16[4,736,128]{2,1,0:T(8,128)(2,1)} %pad_maximum_fusion), calls=%async_computation.2 | async-start | bytes 1507328 | tf_op jit(solution)/shard_map/all_to_all | solution.py:348
  119.1 14.5 %collective-permute-start.13 = (bf16[2064,128]{1,0:T(8,128)(2,1)}, bf16[2064,128]{1,0:T(8,128)(2,1)}, u32[]{:S(2)}, u32[]{:S(2)}) collective-permute-start(bf16[2064,128]{1,0:T(8,128)(2,1)} %collective-permute-done.12.refs_3_), channel_id=1, source_target_pairs={{0,480},{32,0},{64,32},{96,64},{128,96},{160,128},{192,160},{224,1... | collective-permute-start | bytes 1585160 | tf_op jit(solution)/shard_map/ppermute | solution.py:355
  126.8 11.5 %collective-permute-start.14 = (bf16[2064,128]{1,0:T(8,128)(2,1)}, bf16[2064,128]{1,0:T(8,128)(2,1)}, u32[]{:S(2)}, u32[]{:S(2)}) collective-permute-start(bf16[2064,128]{1,0:T(8,128)(2,1)} %collective-permute-done.10.refs_2_), channel_id=1, source_target_pairs={{0,32},{32,64},{64,96},{96,128},{128,160},{160,192},{192,224},{224... | collective-permute-start | bytes 1585160 | tf_op jit(solution)/shard_map/ppermute | solution.py:367
  129.6 11.6 %all-to-all-start.3 = ((bf16[4,624,128]{2,1,0:T(8,128)(2,1)}), bf16[4,624,128]{2,1,0:T(8,128)(2,1)S(1)}, u32[]{:S(2)}, u32[]{:S(2)}) async-start(bf16[4,624,128]{2,1,0:T(8,128)(2,1)} %pad_maximum_fusion.1), calls=%async_computation.3 | async-start | bytes 1277952 | tf_op jit(solution)/shard_map/all_to_all | solution.py:348
  150.9 0.7 copy-start.14
  151.6 16.5 %copy-start = (bf16[8,4,64,128]{3,2,1,0:T(8,128)(2,1)S(1)}, bf16[8,4,64,128]{3,2,1,0:T(8,128)(2,1)}, u32[]{:S(2)}) copy-start(bf16[8,4,64,128]{3,2,1,0:T(8,128)(2,1)} %param.10) | copy-start | bytes 1572868
  151.6 16.5 %copy-start.11 = (bf16[8,4,8,128]{3,2,1,0:T(8,128)(2,1)S(1)}, bf16[8,4,8,128]{3,2,1,0:T(8,128)(2,1)}, u32[]{:S(2)}) copy-start(bf16[8,4,8,128]{3,2,1,0:T(8,128)(2,1)} %param.11) | copy-start | bytes 196612
  154.3 13.8 %copy-start.9 = (bf16[8,32,8,128]{3,2,1,0:T(8,128)(2,1)S(1)}, bf16[8,32,8,128]{3,2,1,0:T(8,128)(2,1)}, u32[]{:S(2)}) copy-start(bf16[8,32,8,128]{3,2,1,0:T(8,128)(2,1)} %param.13) | copy-start | bytes 1572868
  154.3 13.8 %copy-start.10 = (bf16[8,32,8,128]{3,2,1,0:T(8,128)(2,1)S(1)}, bf16[8,32,8,128]{3,2,1,0:T(8,128)(2,1)}, u32[]{:S(2)}) copy-start(bf16[8,32,8,128]{3,2,1,0:T(8,128)(2,1)} %param.14) | copy-start | bytes 1572868
  154.3 13.8 %copy-start.12 = (bf16[8,4,8,128]{3,2,1,0:T(8,128)(2,1)S(1)}, bf16[8,4,8,128]{3,2,1,0:T(8,128)(2,1)}, u32[]{:S(2)}) copy-start(bf16[8,4,8,128]{3,2,1,0:T(8,128)(2,1)} %param.12) | copy-start | bytes 196612
  154.3 24.3 %all-to-all-start.5 = ((bf16[8,304,128]{2,1,0:T(8,128)(2,1)}), bf16[8,304,128]{2,1,0:T(8,128)(2,1)S(1)}, u32[]{:S(2)}, u32[]{:S(2)}) async-start(bf16[8,304,128]{2,1,0:T(8,128)(2,1)} %merge.1), calls=%async_computation.5 | async-start | bytes 1245184 | tf_op jit(solution)/shard_map/all_to_all | solution.py:372
  168.1 0.7 copy-start.15

commit v2 on v1

--- a/solution.py
+++ b/solution.py
@@ -12,10 +12,16 @@
 NZ, NX, NY, NC = 16, 4, 4, 2
 NKV = NY * NC
 CAP = 3
+CALLS = [[0, 1], [2, 3, 4], [5], [6], [7]]
+DUE = [4, 5, 6, 7, 8]
+CUTS = [[0, 1, 2], [3, 4]]
 F32 = jnp.float32
 BF16 = jnp.bfloat16
-VMEM_LIMIT = 48 * 1024 * 1024
+VMEM_LIMIT = 20 * 1024 * 1024
 VM = pl.BlockSpec(memory_space=pltpu.VMEM)
+
+
+SMALL = pl.CostEstimate(flops=1 << 10, bytes_accessed=1 << 10, transcendentals=0)
 
 
 def params():
@@ -133,7 +139,7 @@
         ),
         out_shape=jax.ShapeDtypeStruct((table.shape[0], per_row, dim), BF16),
         compiler_params=params(),
-        cost_estimate=pl.CostEstimate(flops=1 << 16, bytes_accessed=2 << 20, transcendentals=0),
+        cost_estimate=SMALL,
         name="pack",
     )(table, grouped)
 
@@ -168,34 +174,39 @@
         out_ref[x, count * each :] = block.T[: out_ref.shape[1] - count * each].astype(BF16)
 
 
-def node_part(q_slots, offsets, kvs):
-    count = len(offsets)
+def stat_rows(count):
+    return -(-6 * count // 16) * 16
+
+
+def node_part(q_slots, places, kvs):
+    count = len(places)
     per_row, dim = q_slots.shape[2:]
     each = CAP * per_row
     work = NX * each * 1024 * count
+    shape = (NX, count * each + stat_rows(count), dim)
     q_block = lambda off: pl.BlockSpec((NX, CAP, per_row, dim), lambda i: (0, off, 0, 0))
     return pl.pallas_call(
         functools.partial(node_kernel, dim ** (-0.5), count),
         grid=(1,),
-        in_specs=[q_block(o) for o in offsets] + [VM] * len(kvs),
-        out_specs=pl.BlockSpec((NX, count * each + 16, dim), lambda i: (0, 0, 0)),
-        out_shape=jax.ShapeDtypeStruct((NX, count * each + 16, dim), BF16),
+        in_specs=[q_block(p) for p in places] + [VM] * len(kvs),
+        out_specs=pl.BlockSpec(shape, lambda i: (0, 0, 0)),
+        out_shape=jax.ShapeDtypeStruct(shape, BF16),
         compiler_params=params(),
-        cost_estimate=pl.CostEstimate(flops=4 * work * dim, bytes_accessed=count << 20, transcendentals=work),
+        cost_estimate=SMALL,
         name="node",
     )(*[q_slots] * count, *kvs)
 
 
 def merge_kernel(groups, rows, per_row, table_ref, *refs):
     arrived = refs[: len(groups)]
-    out_ref, e_out, e_max, e_total = refs[len(groups) :]
+    out_ref, e_out, e_max, e_total = refs[-4:]
     each = CAP * per_row
     for ref, steps in zip(arrived, groups):
         base = 0
         for offsets in steps:
             count = len(offsets)
             for x in range(NX):
-                tile = ref[x, base + count * each : base + count * each + 16].astype(F32)
+                tile = ref[x, base + count * each : base + count * each + stat_rows(count)].astype(F32)
                 for i, off in enumerate(offsets):
                     top = tile[6 * i : 6 * i + 1] + tile[6 * i + 1 : 6 * i + 2] + tile[6 * i + 2 : 6 * i + 3]
                     total = tile[6 * i + 3 : 6 * i + 4] + tile[6 * i + 4 : 6 * i + 5] + tile[6 * i + 5 : 6 * i + 6]
@@ -211,7 +222,7 @@
                             top_k, total_k = top, total
                         e_max[pl.ds(entry, 1), :] = top_k
                         e_total[pl.ds(entry, 1), :] = total_k
-            base += count * each + 16
+            base += count * each + stat_rows(count)
     m0, m1 = e_max[:rows], e_max[rows : 2 * rows]
     top = jnp.maximum(m0, m1)
     w0 = e_total[:rows] * jnp.exp(m0 - top)
@@ -236,8 +247,7 @@
 def merge_part(table, arrived, groups, rows, per_row):
     dim = arrived[0].shape[2]
     rows_here = rows // NKV
-    stat_rows = -(-6 * rows_here // 16) * 16
-    shape = (NKV, rows_here * per_row + stat_rows, dim)
+    shape = (NKV, rows_here * per_row + stat_rows(rows_here), dim)
     return pl.pallas_call(
         functools.partial(merge_kernel, groups, rows, per_row),
         grid_spec=pltpu.PrefetchScalarGridSpec(
@@ -322,8 +332,6 @@
     group = heads // NKV
     per_row = steps * group
     zi = lax.axis_index("z")
-    half = NZ // 2
-
     slots = prefix_keys.shape[1]
     length = node_length[0]
     digits = jnp.stack([length // 32, length % 32]).astype(BF16)
@@ -334,40 +342,57 @@
 
     tie = lax.optimization_barrier
     by_head = queries.reshape(rows_here * steps, NKV, group, dim).transpose(1, 0, 2, 3)
-    by_head, own = tie((by_head, own))
     grouped = lax.all_to_all(by_head, ("y", "core"), split_axis=0, concat_axis=0, tiled=True)
     grouped = grouped.reshape(rows_dev, per_row, dim)
     table = entry_table(row_nodes, zi)
     ssum, sstat = suffix_part(queries, new_keys, new_values, suffix_keys, suffix_values, suffix_length)
 
-    plan = [[0]] + [[NZ - s, s] for s in range(1, half)] + [[half]]
-    cuts = [range(0, 4), range(4, half - 1), range(half - 1, half + 1)]
-    groups = [[plan[s] for s in cut] for cut in cuts]
-
-    def send_back(blocks):
-        return lax.all_to_all(jnp.concatenate(blocks, axis=1), "x", split_axis=0, concat_axis=0, tiled=True)
-
-    due = {2: [], 4: [], 5: [0, 1, 2], 6: [3, 4], 7: [5, 6]}
-    arrived = [[own]]
-    sent = []
+    half = NZ // 2
+    arrives = [0] + [min(off, NZ - off) for off in range(1, NZ)]
+    calls = [[off for off in range(NZ) if arrives[off] in steps] for steps in CALLS]
+    groups = [[calls[c] for c in cut] for cut in CUTS]
+    groups[-1] = groups[-1] + [[half]]
+
+    def attend(c):
+        return node_part(q_slots, calls[c], [held[off] for off in calls[c]])
+
+    def send_back(c):
+        blocks = [outs[i] for i in CUTS[c]]
+        blocks = blocks[0] if len(blocks) == 1 else jnp.concatenate(blocks, axis=1)
+        return lax.all_to_all(blocks, "x", split_axis=0, concat_axis=0, tiled=True)
+
+    def attend_due(s):
+        for c, at in enumerate(DUE):
+            if at == s:
+                outs[c] = attend(c)
+
+    held = {0: own}
+    outs = {}
     going_up = going_down = own
     for s in range(1, half):
         going_up, going_down = lax.ppermute(going_up, "z", up), lax.ppermute(going_down, "z", down)
         if s == 2:
-            going_up, grouped = tie((going_up, grouped))
             packed = pack_part(table, grouped).reshape(NX, NZ * CAP, per_row, dim)
+            going_up, going_down, packed = tie((going_up, going_down, packed))
             q_slots = lax.all_to_all(packed, "x", split_axis=0, concat_axis=0, tiled=True)
         elif s == 4:
-            going_up, q_slots = tie((going_up, q_slots))
-        if due.get(s):
-            fresh = [node_part(q_slots, plan[t], arrived[t]) for t in due[s]]
-            going_up, fresh = tie((going_up, fresh))
-            sent += fresh
-        arrived.append([going_up, going_down])
-    farthest = lax.ppermute(going_up, "z", up)
-    sent.append(node_part(q_slots, plan[half - 1], arrived[half - 1]))
-    sent.append(node_part(q_slots, plan[half], [farthest]))
-    back = [send_back([sent[s] for s in cut]) for cut in cuts]
+            attend_due(s)
+            far = lax.ppermute(q_slots[:, half * CAP : (half + 1) * CAP], "z", [(i, (i + 2) % NZ) for i in range(NZ)])
+            going_up, going_down, outs, far, q_slots = tie((going_up, going_down, outs, far, q_slots))
+        elif s == 5 or s == 6:
+            attend_due(s)
+            if s == 6:
+                back = [send_back(0)]
+            going_up, going_down, outs = tie((going_up, going_down, outs))
+        elif s == 7:
+            attend_due(s)
+            far = node_part(far, [0], [held[half - 2]])
+            far = lax.ppermute(far, "z", [(i, (i - 2) % NZ) for i in range(NZ)])
+            going_up, going_down, outs, far, back = tie((going_up, going_down, outs, far, back))
+        held[NZ - s], held[s] = going_up, going_down
+    attend_due(half)
+    last = jnp.concatenate([outs[c] for c in CUTS[1]] + [far], axis=1)
+    back.append(lax.all_to_all(last, "x", split_axis=0, concat_axis=0, tiled=True))
     merged = merge_part(table, back, groups, rows_dev, per_row)
     home = lax.all_to_all(merged, ("y", "core"), split_axis=0, concat_axis=0, tiled=True)
     return final_part(home, ssum, sstat, rows_here, steps, heads, dim)

time: 181 us -> 173 us (0.956)
  waiting for transfers between devices: 42.5 us -> 36.1 us
  local copies, waits for them, and re-layouts: 6.77 us -> 2.08 us
  starting transfers between devices: 84 us -> 88.2 us
  Pallas kernels: 33.4 us -> 29.8 us
    ppermute x7, waiting for transfers between devices: 17.9 us -> 3.41 us  [per_device(): lax.ppermute(going_down, 'z', down)]
    ppermute x7, waiting for transfers between devices: 14.9 us -> 24.7 us  [per_device(): lax.ppermute(going_up, 'z', up)]
    ppermute x7, starting transfers between devices: 33.6 us -> 37.6 us  [per_device(): lax.ppermute(going_down, 'z', down)]
    all_to_all x2 -> x1, starting transfers between devices: 7.69 us -> 3.66 us  [send_back(): return lax.all_to_all(blocks, 'x', split_axis=0, concat_axis=0, tiled=True)]
    unnamed x38 -> x20, local copies, waits for them, and re-layouts: 4.33 us -> 0.68 us
    pallas_call x9 -> x6, Pallas kernels: 22 us -> 18.4 us  [node_part(): pl.pallas_call(functools.partial(node_kernel, dim ** (-0.5), count), grid...]
    ppermute x1 -> x2, starting transfers between devices: 1.92 us -> 5.2 us  [the longest x1 3.28 us: per_device(): far = lax.ppermute(far, 'z', [(i, (i - 2) % NZ) for i in range(NZ)])]
    all_to_all x1, waiting for transfers between devices: 3.05 us -> 0.01 us  [per_device(): lax.all_to_all(by_head, ('y', 'core'), split_axis=0, concat_axis=0, tiled...]
  transfers between devices with their start and end apart: 20 -> 20, of which waited for: 10 -> 11; matrix products, arithmetic and copies ran while one was open for 1% -> 2% of each run, Pallas kernels for 16% -> 13%
where the time goes in v2:
time: 173 us; the launch traced here: 172 us
  starting transfers between devices  88.2 us (51%)
  waiting for transfers between devices  36.1 us (21%)
  Pallas kernels  29.8 us (17%)
  blocking collectives  11.1 us (6%)
  other arithmetic  3.8 us (2%)
  local copies, waits for them, and re-layouts  2.08 us (1%)
    ppermute x7, starting transfers between devices, per_device(): lax.ppermute(going_down, 'z', down)  37.6 us
    ppermute x7, waiting for transfers between devices, per_device(): lax.ppermute(going_up, 'z', up)  24.7 us
    pallas_call x6, Pallas kernels, node_part(): pl.pallas_call(functools.partial(node_kernel, dim ** (-0.5), count), grid...  18.4 us
    all_to_all x1, starting transfers between devices, per_device(): lax.all_to_all(merged, ('y', 'core'), split_axis=0, concat_axis=0, tiled=...  16.5 us
    ppermute x7, starting transfers between devices, per_device(): lax.ppermute(going_up, 'z', up)  15.8 us
    all_to_all x1, blocking collectives, per_device(): lax.all_to_all(last, 'x', split_axis=0, concat_axis=0, tiled=True)  11.1 us
    all_to_all x1, starting transfers between devices, per_device(): lax.all_to_all(by_head, ('y', 'core'), split_axis=0, concat_axis=0, tiled...  5.42 us
    all_to_all x1, waiting for transfers between devices, per_device(): lax.all_to_all(merged, ('y', 'core'), split_axis=0, concat_axis=0, tiled=...  5.14 us
  transfers between devices with their start and end apart: 20, of which 11 were waited for; matrix products, arithmetic and copies ran while one was open for 2% of the time, Pallas kernels for 13%

profile of v2, /device:TPU:1, one launch (start us, length us, event | category | flops | bytes accessed | tf_op | source)
XLA Modules:
  0.0 172.2 jit_solution(11376944596686009288)
XLA Ops:
  0.8 1.4 maximum_maximum_fusion.refs_3_
  2.2 4.4 %collective-permute-start = (bf16[2064,128]{1,0:T(8,128)(2,1)S(1)}, bf16[2064,128]{1,0:T(8,128)(2,1)S(1)}, u32[]{:S(2)}, u32[]{:S(2)}) collective-permute-start(bf16[2064,128]{1,0:T(8,128)(2,1)S(1)} %maximum_maximum_fusion.refs_3_), channel_id=1, source_target_pairs={{0,32},{32,64},{64,96},{96,128},{128,160},{160,192},{192,224},{224... | collective-permute-start | bytes 1585160 | tf_op jit(solution)/shard_map/ppermute | solution.py:373
  6.6 9.5 %collective-permute-start.2 = (bf16[2064,128]{1,0:T(8,128)(2,1)S(1)}, bf16[2064,128]{1,0:T(8,128)(2,1)S(1)}, u32[]{:S(2)}, u32[]{:S(2)}) collective-permute-start(bf16[2064,128]{1,0:T(8,128)(2,1)S(1)} %maximum_maximum_fusion.refs_3_), channel_id=1, source_target_pairs={{0,480},{32,0},{64,32},{96,64},{128,96},{160,128},{192,160},{224,1... | collective-permute-start | bytes 1585160 | tf_op jit(solution)/shard_map/ppermute | solution.py:373
  16.1 0.9 copy.17
  17.0 5.4 %all-to-all-start = ((bf16[8,32,8,128]{3,2,1,0:T(8,128)(2,1)}), bf16[8,32,8,128]{3,2,1,0:T(8,128)(2,1)S(1)}, u32[]{:S(2)}, u32[]{:S(2)}) async-start(bf16[8,32,8,128]{3,2,1,0:T(8,128)(2,1)} %bitcast.20), calls=%async_computation | async-start | bytes 1048576 | tf_op jit(solution)/shard_map/all_to_all | solution.py:345
  22.5 0.2 convert_reduce_fusion
  22.7 3.2 %collective-permute-done.refs_5_ = bf16[2064,128]{1,0:T(8,128)(2,1)S(1)} collective-permute-done((bf16[2064,128]{1,0:T(8,128)(2,1)S(1)}, bf16[2064,128]{1,0:T(8,128)(2,1)S(1)}, u32[]{:S(2)}, u32[]{:S(2)}) %collective-permute-start) | collective-permute-done | bytes 528416 | tf_op jit(solution)/shard_map/ppermute | solution.py:373
  25.9 1.9 %collective-permute-start.1 = (bf16[2064,128]{1,0:T(8,128)(2,1)S(1)}, bf16[2064,128]{1,0:T(8,128)(2,1)}, u32[]{:S(2)}, u32[]{:S(2)}) collective-permute-start(bf16[2064,128]{1,0:T(8,128)(2,1)S(1)} %collective-permute-done.refs_5_), channel_id=1, source_target_pairs={{0,32},{32,64},{64,96},{96,128},{128,160},{160,192},{192,224},{224... | collective-permute-start | bytes 1585160 | tf_op jit(solution)/shard_map/ppermute | solution.py:373
  27.8 4.6 %collective-permute-start.3 = (bf16[2064,128]{1,0:T(8,128)(2,1)S(1)}, bf16[2064,128]{1,0:T(8,128)(2,1)}, u32[]{:S(2)}, u32[]{:S(2)}) collective-permute-start(bf16[2064,128]{1,0:T(8,128)(2,1)S(1)} %collective-permute-done.2.refs_4_), channel_id=1, source_target_pairs={{0,480},{32,0},{64,32},{96,64},{128,96},{160,128},{192,160},{224,1... | collective-permute-start | bytes 1585160 | tf_op jit(solution)/shard_map/ppermute | solution.py:373
  32.6 2.2 %pack.1 = bf16[192,32,128]{2,1,0:T(8,128)(2,1)} custom-call(s32[192]{0:T(256)S(1)} %broadcast_add_fusion.table_ref, bf16[64,32,128]{2,1,0:T(8,128)(2,1)S(1)} %bitcast.28), custom_call_target="tpu_custom_call" | custom-call | flops 1024 | bytes 1024 | tf_op jit(solution)/shard_map/pack/pallas_call | solution.py:135
  34.8 6.6 %collective-permute-done.1.refs_11_ = bf16[2064,128]{1,0:T(8,128)(2,1)} collective-permute-done((bf16[2064,128]{1,0:T(8,128)(2,1)S(1)}, bf16[2064,128]{1,0:T(8,128)(2,1)}, u32[]{:S(2)}, u32[]{:S(2)}) %collective-permute-start.1) | collective-permute-done | bytes 528416 | tf_op jit(solution)/shard_map/ppermute | solution.py:373
  41.4 0.8 collective-permute-done.3.refs_6_
  42.2 4.0 %all-to-all-start.1 = ((bf16[4,48,32,128]{3,2,1,0:T(8,128)(2,1)}), bf16[4,48,32,128]{3,2,1,0:T(8,128)(2,1)S(1)}, u32[]{:S(2)}, u32[]{:S(2)}) async-start(bf16[4,48,32,128]{3,2,1,0:T(8,128)(2,1)} %bitcast.9), calls=%async_computation.1 | async-start | bytes 3145728 | tf_op jit(solution)/shard_map/all_to_all | solution.py:377
  46.2 1.9 %collective-permute-start.4 = (bf16[2064,128]{1,0:T(8,128)(2,1)}, bf16[2064,128]{1,0:T(8,128)(2,1)}, u32[]{:S(2)}, u32[]{:S(2)}) collective-permute-start(bf16[2064,128]{1,0:T(8,128)(2,1)} %collective-permute-done.1.refs_11_), channel_id=1, source_target_pairs={{0,32},{32,64},{64,96},{96,128},{128,160},{160,192},{192,224},{224... | collective-permute-start | bytes 1585160 | tf_op jit(solution)/shard_map/ppermute | solution.py:373
  48.1 5.4 %collective-permute-start.6 = (bf16[2064,128]{1,0:T(8,128)(2,1)}, bf16[2064,128]{1,0:T(8,128)(2,1)}, u32[]{:S(2)}, u32[]{:S(2)}) collective-permute-start(bf16[2064,128]{1,0:T(8,128)(2,1)} %collective-permute-done.3.refs_6_), channel_id=1, source_target_pairs={{0,480},{32,0},{64,32},{96,64},{128,96},{160,128},{192,160},{224,1... | collective-permute-start | bytes 1585160 | tf_op jit(solution)/shard_map/ppermute | solution.py:373
  53.5 8.0 %collective-permute-done.4.refs_10_ = bf16[2064,128]{1,0:T(8,128)(2,1)} collective-permute-done((bf16[2064,128]{1,0:T(8,128)(2,1)}, bf16[2064,128]{1,0:T(8,128)(2,1)}, u32[]{:S(2)}, u32[]{:S(2)}) %collective-permute-start.4) | collective-permute-done | bytes 528416 | tf_op jit(solution)/shard_map/ppermute | solution.py:373
  61.5 1.9 %collective-permute-start.5 = (bf16[2064,128]{1,0:T(8,128)(2,1)}, bf16[2064,128]{1,0:T(8,128)(2,1)}, u32[]{:S(2)}, u32[]{:S(2)}) collective-permute-start(bf16[2064,128]{1,0:T(8,128)(2,1)} %collective-permute-done.4.refs_10_), channel_id=1, source_target_pairs={{0,32},{32,64},{64,96},{96,128},{128,160},{160,192},{192,224},{224... | collective-permute-start | bytes 1585160 | tf_op jit(solution)/shard_map/ppermute | solution.py:373
  63.5 4.6 %collective-permute-start.7 = (bf16[2064,128]{1,0:T(8,128)(2,1)}, bf16[2064,128]{1,0:T(8,128)(2,1)}, u32[]{:S(2)}, u32[]{:S(2)}) collective-permute-start(bf16[2064,128]{1,0:T(8,128)(2,1)} %collective-permute-done.6.refs_7_), channel_id=1, source_target_pairs={{0,480},{32,0},{64,32},{96,64},{128,96},{160,128},{192,160},{224,1... | collective-permute-start | bytes 1585160 | tf_op jit(solution)/shard_map/ppermute | solution.py:373
  68.1 1.9 %collective-permute-start.8 = (bf16[4,3,32,128]{3,2,1,0:T(8,128)(2,1)S(1)}, bf16[4,3,32,128]{3,2,1,0:T(8,128)(2,1)S(1)}, u32[]{:S(2)}, u32[]{:S(2)}) collective-permute-start(bf16[4,3,32,128]{3,2,1,0:T(8,128)(2,1)S(1)} %slice.8), channel_id=1, source_target_pairs={{0,64},{32,96},{64,128},{96,160},{128,192},{160,224},{192,256},{22... | collective-permute-start | bytes 294920 | tf_op jit(solution)/shard_map/ppermute | solution.py:380
  70.0 2.4 %node.6 = bf16[4,320,128]{2,1,0:T(8,128)(2,1)S(1)} custom-call(bf16[4,48,32,128]{3,2,1,0:T(8,128)(2,1)S(1)} %all-to-all-done.1.refs_0_.refs_1_.refs_2_.refs_3_.refs_4_.refs_5_, bf16[4,48,32,128]{3,2,1,0:T(8,128)(2,1)S(1)} %all-to-all-done.1.refs_0_.refs_1_.refs_2_.refs_3_.refs_4_.refs_5_, ...), custom_call_target="tpu_custom_call" | custom-call | flops 1024 | bytes 1024 | tf_op jit(solution)/shard_map/node/pallas_call | solution.py:188
  72.4 2.7 %collective-permute-done.5.refs_9_ = bf16[2064,128]{1,0:T(8,128)(2,1)} collective-permute-done((bf16[2064,128]{1,0:T(8,128)(2,1)}, bf16[2064,128]{1,0:T(8,128)(2,1)}, u32[]{:S(2)}, u32[]{:S(2)}) %collective-permute-start.5) | collective-permute-done | bytes 528416 | tf_op jit(solution)/shard_map/ppermute | solution.py:373
  75.1 0.9 collective-permute-done.7.refs_8_
  76.0 1.2 collective-permute-done.8.refs_0_
  77.3 0.6 copy-done.4
  77.9 4.1 %collective-permute-start.10 = (bf16[2064,128]{1,0:T(8,128)(2,1)}, bf16[2064,128]{1,0:T(8,128)(2,1)}, u32[]{:S(2)}, u32[]{:S(2)}) collective-permute-start(bf16[2064,128]{1,0:T(8,128)(2,1)} %collective-permute-done.7.refs_8_), channel_id=1, source_target_pairs={{0,480},{32,0},{64,32},{96,64},{128,96},{160,128},{192,160},{224,1... | collective-permute-start | bytes 1585160 | tf_op jit(solution)/shard_map/ppermute | solution.py:373
  82.0 1.9 %collective-permute-start.9 = (bf16[2064,128]{1,0:T(8,128)(2,1)}, bf16[2064,128]{1,0:T(8,128)(2,1)}, u32[]{:S(2)}, u32[]{:S(2)}) collective-permute-start(bf16[2064,128]{1,0:T(8,128)(2,1)} %collective-permute-done.5.refs_9_), channel_id=1, source_target_pairs={{0,32},{32,64},{64,96},{96,128},{128,160},{160,192},{192,224},{224... | collective-permute-start | bytes 1585160 | tf_op jit(solution)/shard_map/ppermute | solution.py:373
  83.9 5.9 %node.7 = bf16[4,624,128]{2,1,0:T(8,128)(2,1)S(1)} custom-call(bf16[4,48,32,128]{3,2,1,0:T(8,128)(2,1)S(1)} %all-to-all-done.1.refs_0_.refs_1_.refs_2_.refs_3_.refs_4_.refs_5_, bf16[4,48,32,128]{3,2,1,0:T(8,128)(2,1)S(1)} %all-to-all-done.1.refs_0_.refs_1_.refs_2_.refs_3_.refs_4_.refs_5_, ...), custom_call_target="tpu_custom_call" | custom-call | flops 1024 | bytes 1024 | tf_op jit(solution)/shard_map/node/pallas_call | solution.py:188
  89.8 4.3 %collective-permute-done.9.refs_3_ = bf16[2064,128]{1,0:T(8,128)(2,1)} collective-permute-done((bf16[2064,128]{1,0:T(8,128)(2,1)}, bf16[2064,128]{1,0:T(8,128)(2,1)}, u32[]{:S(2)}, u32[]{:S(2)}) %collective-permute-start.9) | collective-permute-done | bytes 528416 | tf_op jit(solution)/shard_map/ppermute | solution.py:373
  94.1 1.9 %collective-permute-start.11 = (bf16[2064,128]{1,0:T(8,128)(2,1)}, bf16[2064,128]{1,0:T(8,128)(2,1)}, u32[]{:S(2)}, u32[]{:S(2)}) collective-permute-start(bf16[2064,128]{1,0:T(8,128)(2,1)} %collective-permute-done.9.refs_3_), channel_id=1, source_target_pairs={{0,32},{32,64},{64,96},{96,128},{128,160},{160,192},{192,224},{224... | collective-permute-start | bytes 1585160 | tf_op jit(solution)/shard_map/ppermute | solution.py:373
  96.0 3.0 %node.8 = bf16[4,208,128]{2,1,0:T(8,128)(2,1)S(1)} custom-call(bf16[4,48,32,128]{3,2,1,0:T(8,128)(2,1)S(1)} %all-to-all-done.1.refs_0_.refs_1_.refs_2_.refs_3_.refs_4_.refs_5_, bf16[4,48,32,128]{3,2,1,0:T(8,128)(2,1)S(1)} %all-to-all-done.1.refs_0_.refs_1_.refs_2_.refs_3_.refs_4_.refs_5_, bf16[2064,128]{1,0:T(8,128)(2,1)} %collective-permute-done.10.refs_2_, ...), custom_call_target="tpu_custom_call" | custom-call | flops 1024 | bytes 1024 | tf_op jit(solution)/shard_map/node/pallas_call | solution.py:188
  99.0 4.6 %collective-permute-start.12 = (bf16[2064,128]{1,0:T(8,128)(2,1)}, bf16[2064,128]{1,0:T(8,128)(2,1)S(1)}, u32[]{:S(2)}, u32[]{:S(2)}) collective-permute-start(bf16[2064,128]{1,0:T(8,128)(2,1)} %collective-permute-done.10.refs_2_), channel_id=1, source_target_pairs={{0,480},{32,0},{64,32},{96,64},{128,96},{160,128},{192,160},{224,1... | collective-permute-start | bytes 1585160 | tf_op jit(solution)/shard_map/ppermute | solution.py:373
  103.6 1.1 pad_maximum_fusion
  104.7 3.7 %all-to-all-start.2 = ((bf16[4,1152,128]{2,1,0:T(8,128)(2,1)}), bf16[4,1152,128]{2,1,0:T(8,128)(2,1)S(1)}, u32[]{:S(2)}, u32[]{:S(2)}) async-start(bf16[4,1152,128]{2,1,0:T(8,128)(2,1)} %pad_maximum_fusion), calls=%async_computation.2 | async-start | bytes 2359296 | tf_op jit(solution)/shard_map/all_to_all | solution.py:362
  108.4 1.7 collective-permute-done.12.refs_2_.refs_1_
  110.1 1.9 %collective-permute-start.13 = (bf16[2064,128]{1,0:T(8,128)(2,1)}, bf16[2064,128]{1,0:T(8,128)(2,1)}, u32[]{:S(2)}, u32[]{:S(2)}) collective-permute-start(bf16[2064,128]{1,0:T(8,128)(2,1)} %collective-permute-done.11.refs_3_), channel_id=1, source_target_pairs={{0,32},{32,64},{64,96},{96,128},{128,160},{160,192},{192,224},{224... | collective-permute-start | bytes 1585160 | tf_op jit(solution)/shard_map/ppermute | solution.py:373
  112.0 4.9 %collective-permute-start.14 = (bf16[2064,128]{1,0:T(8,128)(2,1)S(1)}, bf16[2064,128]{1,0:T(8,128)(2,1)}, u32[]{:S(2)}, u32[]{:S(2)}) collective-permute-start(bf16[2064,128]{1,0:T(8,128)(2,1)S(1)} %collective-permute-done.12.refs_2_.refs_1_), channel_id=1, source_target_pairs={{0,480},{32,0},{64,32},{96,64},{128,96},{160,128},{192,160},{224,1... | collective-permute-start | bytes 1585160 | tf_op jit(solution)/shard_map/ppermute | solution.py:373
  116.9 1.2 node.10
  118.1 3.3 %collective-permute-start.15 = (bf16[4,112,128]{2,1,0:T(8,128)(2,1)S(1)}, bf16[4,112,128]{2,1,0:T(8,128)(2,1)}, u32[]{:S(2)}, u32[]{:S(2)}) collective-permute-start(bf16[4,112,128]{2,1,0:T(8,128)(2,1)S(1)} %node.10), channel_id=1, source_target_pairs={{0,448},{32,480},{64,0},{96,32},{128,64},{160,96},{192,128},{224,1... | collective-permute-start | bytes 344072 | tf_op jit(solution)/shard_map/ppermute | solution.py:390
  121.4 2.9 %node.9 = bf16[4,208,128]{2,1,0:T(8,128)(2,1)S(1)} custom-call(bf16[4,48,32,128]{3,2,1,0:T(8,128)(2,1)S(1)} %all-to-all-done.1.refs_0_.refs_1_.refs_2_.refs_3_.refs_4_.refs_5_, bf16[4,48,32,128]{3,2,1,0:T(8,128)(2,1)S(1)} %all-to-all-done.1.refs_0_.refs_1_.refs_2_.refs_3_.refs_4_.refs_5_, bf16[2064,128]{1,0:T(8,128)(2,1)S(1)} %collective-permute-done.12.refs_2_.refs_1_, ...), custom_call_target="tpu_custom_call" | custom-call | flops 1024 | bytes 1024 | tf_op jit(solution)/shard_map/node/pallas_call | solution.py:188
  124.3 1.6 collective-permute-done.15
  125.9 3.0 %node.11 = bf16[4,208,128]{2,1,0:T(8,128)(2,1)S(1)} custom-call(bf16[4,48,32,128]{3,2,1,0:T(8,128)(2,1)S(1)} %all-to-all-done.1.refs_0_.refs_1_.refs_2_.refs_3_.refs_4_.refs_5_, bf16[4,48,32,128]{3,2,1,0:T(8,128)(2,1)S(1)} %all-to-all-done.1.refs_0_.refs_1_.refs_2_.refs_3_.refs_4_.refs_5_, bf16[2064,128]{1,0:T(8,128)(2,1)} %collective-permute-done.14.refs_2_, ...), custom_call_target="tpu_custom_call" | custom-call | flops 1024 | bytes 1024 | tf_op jit(solution)/shard_map/node/pallas_call | solution.py:188
  128.9 0.9 pad_maximum_fusion.1
  129.8 11.1 %all_to_all.25.refs_1_ = bf16[4,528,128]{2,1,0:T(8,128)(2,1)S(1)} all-to-all(bf16[4,528,128]{2,1,0:T(8,128)(2,1)S(1)} %pad_maximum_fusion.1), channel_id=1, replica_groups=mesh['z'=16,'x'=4,'y'=4,'core'=2] {'x'}, dimensions={0} | all-to-all | bytes 1081344 | tf_op jit(solution)/shard_map/all_to_all | solution.py:395
  140.9 2.7 %merge.1 = bf16[8,304,128]{2,1,0:T(8,128)(2,1)} custom-call(s32[192]{0:T(256)S(1)} %broadcast_add_fusion.table_ref, bf16[4,1152,128]{2,1,0:T(8,128)(2,1)S(1)} %all-to-all-done.2.refs_0_, bf16[4,528,128]{2,1,0:T(8,128)(2,1)S(1)} %all_to_all.25.refs_1_), custom_call_target="tpu_custom_call" | custom-call | flops 4194304 | bytes 4194304 | tf_op jit(solution)/shard_map/merge/pallas_call | solution.py:251
  143.6 16.5 %all-to-all-start.4 = ((bf16[8,304,128]{2,1,0:T(8,128)(2,1)}), bf16[8,304,128]{2,1,0:T(8,128)(2,1)S(1)}, u32[]{:S(2)}, u32[]{:S(2)}) async-start(bf16[8,304,128]{2,1,0:T(8,128)(2,1)} %merge.1), calls=%async_computation.4 | async-start | bytes 1245184 | tf_op jit(solution)/shard_map/all_to_all | solution.py:397
  160.1 4.9 %suffix.1 = (f32[8,256,128]{2,1,0:T(8,128)S(1)}, f32[8,8,256]{2,1,0:T(8,128)S(1)}) custom-call(s32[8]{0:T(128)S(1)} %copy-done.8, bf16[8,256,128]{2,1,0:T(8,128)(2,1)S(1)} %bitcast.27, bf16[8,256,128]{2,1,0:T(8,128)(2,1)S(1)} %bitcast.30, bf16[8,32,128]{2,1,0:T(8,128)(2,1)S(1)} %bitcast.32, bf16[8,256,128]{2,1,0:T(8,128)(2,1)S(1)} %bitcast.31, ...), custom_call_target="tpu_custom_call" | custom-call | flops 268435456 | bytes 4194304 | tf_op jit(solution)/shard_map/suffix/pallas_call | solution.py:91
  165.5 5.1 %all-to-all-done.4.arrived_ref = bf16[8,304,128]{2,1,0:T(8,128)(2,1)S(1)} async-done(((bf16[8,304,128]{2,1,0:T(8,128)(2,1)}), bf16[8,304,128]{2,1,0:T(8,128)(2,1)S(1)}, u32[]{:S(2)}, u32[]{:S(2)}) %all-to-all-start.4) | async-done | bytes 622624 | tf_op jit(solution)/shard_map/all_to_all | solution.py:397
  170.6 1.6 final.1
  (40 shorter events, 0.8 us)
Async XLA Ops:
  0.0 16.1 %copy-start = (bf16[8,4,64,128]{3,2,1,0:T(8,128)(2,1)S(1)}, bf16[8,4,64,128]{3,2,1,0:T(8,128)(2,1)}, u32[]{:S(2)}) copy-start(bf16[8,4,64,128]{3,2,1,0:T(8,128)(2,1)} %param.10) | copy-start | bytes 1572868
  2.2 20.2 %copy-start.9 = (s32[64,2]{0,1:T(2,128)S(1)}, s32[64,2]{0,1:T(2,128)}, u32[]{:S(2)}) copy-start(s32[64,2]{0,1:T(2,128)} %param.16) | copy-start | bytes 1540
  2.2 23.7 %collective-permute-start = (bf16[2064,128]{1,0:T(8,128)(2,1)S(1)}, bf16[2064,128]{1,0:T(8,128)(2,1)S(1)}, u32[]{:S(2)}, u32[]{:S(2)}) collective-permute-start(bf16[2064,128]{1,0:T(8,128)(2,1)S(1)} %maximum_maximum_fusion.refs_3_), channel_id=1, source_target_pairs={{0,32},{32,64},{64,96},{96,128},{128,160},{160,192},{192,224},{224... | collective-permute-start | bytes 1585160 | tf_op jit(solution)/shard_map/ppermute | solution.py:373
  6.6 21.2 %collective-permute-start.2 = (bf16[2064,128]{1,0:T(8,128)(2,1)S(1)}, bf16[2064,128]{1,0:T(8,128)(2,1)S(1)}, u32[]{:S(2)}, u32[]{:S(2)}) collective-permute-start(bf16[2064,128]{1,0:T(8,128)(2,1)S(1)} %maximum_maximum_fusion.refs_3_), channel_id=1, source_target_pairs={{0,480},{32,0},{64,32},{96,64},{128,96},{160,128},{192,160},{224,1... | collective-permute-start | bytes 1585160 | tf_op jit(solution)/shard_map/ppermute | solution.py:373
  17.0 15.6 %all-to-all-start = ((bf16[8,32,8,128]{3,2,1,0:T(8,128)(2,1)}), bf16[8,32,8,128]{3,2,1,0:T(8,128)(2,1)S(1)}, u32[]{:S(2)}, u32[]{:S(2)}) async-start(bf16[8,32,8,128]{3,2,1,0:T(8,128)(2,1)} %bitcast.20), calls=%async_computation | async-start | bytes 1048576 | tf_op jit(solution)/shard_map/all_to_all | solution.py:345
  25.9 15.5 %collective-permute-start.1 = (bf16[2064,128]{1,0:T(8,128)(2,1)S(1)}, bf16[2064,128]{1,0:T(8,128)(2,1)}, u32[]{:S(2)}, u32[]{:S(2)}) collective-permute-start(bf16[2064,128]{1,0:T(8,128)(2,1)S(1)} %collective-permute-done.refs_5_), channel_id=1, source_target_pairs={{0,32},{32,64},{64,96},{96,128},{128,160},{160,192},{192,224},{224... | collective-permute-start | bytes 1585160 | tf_op jit(solution)/shard_map/ppermute | solution.py:373
  27.8 14.4 %collective-permute-start.3 = (bf16[2064,128]{1,0:T(8,128)(2,1)S(1)}, bf16[2064,128]{1,0:T(8,128)(2,1)}, u32[]{:S(2)}, u32[]{:S(2)}) collective-permute-start(bf16[2064,128]{1,0:T(8,128)(2,1)S(1)} %collective-permute-done.2.refs_4_), channel_id=1, source_target_pairs={{0,480},{32,0},{64,32},{96,64},{128,96},{160,128},{192,160},{224,1... | collective-permute-start | bytes 1585160 | tf_op jit(solution)/shard_map/ppermute | solution.py:373
  42.2 25.9 %all-to-all-start.1 = ((bf16[4,48,32,128]{3,2,1,0:T(8,128)(2,1)}), bf16[4,48,32,128]{3,2,1,0:T(8,128)(2,1)S(1)}, u32[]{:S(2)}, u32[]{:S(2)}) async-start(bf16[4,48,32,128]{3,2,1,0:T(8,128)(2,1)} %bitcast.9), calls=%async_computation.1 | async-start | bytes 3145728 | tf_op jit(solution)/shard_map/all_to_all | solution.py:377
  46.2 15.3 %collective-permute-start.4 = (bf16[2064,128]{1,0:T(8,128)(2,1)}, bf16[2064,128]{1,0:T(8,128)(2,1)}, u32[]{:S(2)}, u32[]{:S(2)}) collective-permute-start(bf16[2064,128]{1,0:T(8,128)(2,1)} %collective-permute-done.1.refs_11_), channel_id=1, source_target_pairs={{0,32},{32,64},{64,96},{96,128},{128,160},{160,192},{192,224},{224... | collective-permute-start | bytes 1585160 | tf_op jit(solution)/shard_map/ppermute | solution.py:373
  48.1 15.3 %collective-permute-start.6 = (bf16[2064,128]{1,0:T(8,128)(2,1)}, bf16[2064,128]{1,0:T(8,128)(2,1)}, u32[]{:S(2)}, u32[]{:S(2)}) collective-permute-start(bf16[2064,128]{1,0:T(8,128)(2,1)} %collective-permute-done.3.refs_6_), channel_id=1, source_target_pairs={{0,480},{32,0},{64,32},{96,64},{128,96},{160,128},{192,160},{224,1... | collective-permute-start | bytes 1585160 | tf_op jit(solution)/shard_map/ppermute | solution.py:373
  61.5 13.6 %collective-permute-start.5 = (bf16[2064,128]{1,0:T(8,128)(2,1)}, bf16[2064,128]{1,0:T(8,128)(2,1)}, u32[]{:S(2)}, u32[]{:S(2)}) collective-permute-start(bf16[2064,128]{1,0:T(8,128)(2,1)} %collective-permute-done.4.refs_10_), channel_id=1, source_target_pairs={{0,32},{32,64},{64,96},{96,128},{128,160},{160,192},{192,224},{224... | collective-permute-start | bytes 1585160 | tf_op jit(solution)/shard_map/ppermute | solution.py:373
  63.5 12.5 %collective-permute-start.7 = (bf16[2064,128]{1,0:T(8,128)(2,1)}, bf16[2064,128]{1,0:T(8,128)(2,1)}, u32[]{:S(2)}, u32[]{:S(2)}) collective-permute-start(bf16[2064,128]{1,0:T(8,128)(2,1)} %collective-permute-done.6.refs_7_), channel_id=1, source_target_pairs={{0,480},{32,0},{64,32},{96,64},{128,96},{160,128},{192,160},{224,1... | collective-permute-start | bytes 1585160 | tf_op jit(solution)/shard_map/ppermute | solution.py:373
  68.1 9.2 %collective-permute-start.8 = (bf16[4,3,32,128]{3,2,1,0:T(8,128)(2,1)S(1)}, bf16[4,3,32,128]{3,2,1,0:T(8,128)(2,1)S(1)}, u32[]{:S(2)}, u32[]{:S(2)}) collective-permute-start(bf16[4,3,32,128]{3,2,1,0:T(8,128)(2,1)S(1)} %slice.8), channel_id=1, source_target_pairs={{0,64},{32,96},{64,128},{96,160},{128,192},{160,224},{192,256},{22... | collective-permute-start | bytes 294920 | tf_op jit(solution)/shard_map/ppermute | solution.py:380
  77.3 0.6 copy-start.4
  77.9 11.9 %collective-permute-start.10 = (bf16[2064,128]{1,0:T(8,128)(2,1)}, bf16[2064,128]{1,0:T(8,128)(2,1)}, u32[]{:S(2)}, u32[]{:S(2)}) collective-permute-start(bf16[2064,128]{1,0:T(8,128)(2,1)} %collective-permute-done.7.refs_8_), channel_id=1, source_target_pairs={{0,480},{32,0},{64,32},{96,64},{128,96},{160,128},{192,160},{224,1... | collective-permute-start | bytes 1585160 | tf_op jit(solution)/shard_map/ppermute | solution.py:373
  82.0 12.1 %collective-permute-start.9 = (bf16[2064,128]{1,0:T(8,128)(2,1)}, bf16[2064,128]{1,0:T(8,128)(2,1)}, u32[]{:S(2)}, u32[]{:S(2)}) collective-permute-start(bf16[2064,128]{1,0:T(8,128)(2,1)} %collective-permute-done.5.refs_9_), channel_id=1, source_target_pairs={{0,32},{32,64},{64,96},{96,128},{128,160},{160,192},{192,224},{224... | collective-permute-start | bytes 1585160 | tf_op jit(solution)/shard_map/ppermute | solution.py:373
  94.1 14.3 %collective-permute-start.11 = (bf16[2064,128]{1,0:T(8,128)(2,1)}, bf16[2064,128]{1,0:T(8,128)(2,1)}, u32[]{:S(2)}, u32[]{:S(2)}) collective-permute-start(bf16[2064,128]{1,0:T(8,128)(2,1)} %collective-permute-done.9.refs_3_), channel_id=1, source_target_pairs={{0,32},{32,64},{64,96},{96,128},{128,160},{160,192},{192,224},{224... | collective-permute-start | bytes 1585160 | tf_op jit(solution)/shard_map/ppermute | solution.py:373
  99.0 11.0 %collective-permute-start.12 = (bf16[2064,128]{1,0:T(8,128)(2,1)}, bf16[2064,128]{1,0:T(8,128)(2,1)S(1)}, u32[]{:S(2)}, u32[]{:S(2)}) collective-permute-start(bf16[2064,128]{1,0:T(8,128)(2,1)} %collective-permute-done.10.refs_2_), channel_id=1, source_target_pairs={{0,480},{32,0},{64,32},{96,64},{128,96},{160,128},{192,160},{224,1... | collective-permute-start | bytes 1585160 | tf_op jit(solution)/shard_map/ppermute | solution.py:373
  104.7 12.2 %copy-start.5 = (bf16[4,3,32,128]{3,2,1,0:T(8,128)(2,1)S(1)}, bf16[4,3,32,128]{3,2,1,0:T(8,128)(2,1)}, u32[]{:S(2)}) copy-start(bf16[4,3,32,128]{3,2,1,0:T(8,128)(2,1)} %copy-done.4) | copy-start | bytes 294916
  104.7 21.2 %all-to-all-start.2 = ((bf16[4,1152,128]{2,1,0:T(8,128)(2,1)}), bf16[4,1152,128]{2,1,0:T(8,128)(2,1)S(1)}, u32[]{:S(2)}, u32[]{:S(2)}) async-start(bf16[4,1152,128]{2,1,0:T(8,128)(2,1)} %pad_maximum_fusion), calls=%async_computation.2 | async-start | bytes 2359296 | tf_op jit(solution)/shard_map/all_to_all | solution.py:362
  110.1 15.8 %collective-permute-start.13 = (bf16[2064,128]{1,0:T(8,128)(2,1)}, bf16[2064,128]{1,0:T(8,128)(2,1)}, u32[]{:S(2)}, u32[]{:S(2)}) collective-permute-start(bf16[2064,128]{1,0:T(8,128)(2,1)} %collective-permute-done.11.refs_3_), channel_id=1, source_target_pairs={{0,32},{32,64},{64,96},{96,128},{128,160},{160,192},{192,224},{224... | collective-permute-start | bytes 1585160 | tf_op jit(solution)/shard_map/ppermute | solution.py:373
  112.0 13.9 %collective-permute-start.14 = (bf16[2064,128]{1,0:T(8,128)(2,1)S(1)}, bf16[2064,128]{1,0:T(8,128)(2,1)}, u32[]{:S(2)}, u32[]{:S(2)}) collective-permute-start(bf16[2064,128]{1,0:T(8,128)(2,1)S(1)} %collective-permute-done.12.refs_2_.refs_1_), channel_id=1, source_target_pairs={{0,480},{32,0},{64,32},{96,64},{128,96},{160,128},{192,160},{224,1... | collective-permute-start | bytes 1585160 | tf_op jit(solution)/shard_map/ppermute | solution.py:373
  118.1 7.7 %collective-permute-start.15 = (bf16[4,112,128]{2,1,0:T(8,128)(2,1)S(1)}, bf16[4,112,128]{2,1,0:T(8,128)(2,1)}, u32[]{:S(2)}, u32[]{:S(2)}) collective-permute-start(bf16[4,112,128]{2,1,0:T(8,128)(2,1)S(1)} %node.10), channel_id=1, source_target_pairs={{0,448},{32,480},{64,0},{96,32},{128,64},{160,96},{192,128},{224,1... | collective-permute-start | bytes 344072 | tf_op jit(solution)/shard_map/ppermute | solution.py:390
  140.9 19.1 %copy-start.3 = (bf16[8,32,8,128]{3,2,1,0:T(8,128)(2,1)S(1)}, bf16[8,32,8,128]{3,2,1,0:T(8,128)(2,1)}, u32[]{:S(2)}) copy-start(bf16[8,32,8,128]{3,2,1,0:T(8,128)(2,1)} %param.14) | copy-start | bytes 1572868
  143.6 16.5 %copy-start.1 = (bf16[8,4,64,128]{3,2,1,0:T(8,128)(2,1)S(1)}, bf16[8,4,64,128]{3,2,1,0:T(8,128)(2,1)}, u32[]{:S(2)}) copy-start(bf16[8,4,64,128]{3,2,1,0:T(8,128)(2,1)} %param.10) | copy-start | bytes 1572868
  143.6 16.5 %copy-start.2 = (bf16[8,32,8,128]{3,2,1,0:T(8,128)(2,1)S(1)}, bf16[8,32,8,128]{3,2,1,0:T(8,128)(2,1)}, u32[]{:S(2)}) copy-start(bf16[8,32,8,128]{3,2,1,0:T(8,128)(2,1)} %param.13) | copy-start | bytes 1572868
  143.6 16.5 %copy-start.6 = (bf16[8,4,8,128]{3,2,1,0:T(8,128)(2,1)S(1)}, bf16[8,4,8,128]{3,2,1,0:T(8,128)(2,1)}, u32[]{:S(2)}) copy-start(bf16[8,4,8,128]{3,2,1,0:T(8,128)(2,1)} %param.11) | copy-start | bytes 196612
  143.6 16.5 %copy-start.7 = (bf16[8,4,8,128]{3,2,1,0:T(8,128)(2,1)S(1)}, bf16[8,4,8,128]{3,2,1,0:T(8,128)(2,1)}, u32[]{:S(2)}) copy-start(bf16[8,4,8,128]{3,2,1,0:T(8,128)(2,1)} %param.12) | copy-start | bytes 196612
  143.6 16.5 %copy-start.8 = (s32[8]{0:T(128)S(1)}, s32[8]{0:T(128)}, u32[]{:S(2)}) copy-start(s32[8]{0:T(128)} %len_ref.1) | copy-start | bytes 100
  143.6 27.0 %all-to-all-start.4 = ((bf16[8,304,128]{2,1,0:T(8,128)(2,1)}), bf16[8,304,128]{2,1,0:T(8,128)(2,1)S(1)}, u32[]{:S(2)}, u32[]{:S(2)}) async-start(bf16[8,304,128]{2,1,0:T(8,128)(2,1)} %merge.1), calls=%async_computation.4 | async-start | bytes 1245184 | tf_op jit(solution)/shard_map/all_to_all | solution.py:397

commit v3 on v2

--- a/solution.py
+++ b/solution.py
@@ -13,7 +13,7 @@
 NKV = NY * NC
 CAP = 3
 CALLS = [[0, 1], [2, 3, 4], [5], [6], [7]]
-DUE = [4, 5, 6, 7, 8]
+DUE = [4, 6, 6, 7, 8]
 CUTS = [[0, 1, 2], [3, 4]]
 F32 = jnp.float32
 BF16 = jnp.bfloat16
@@ -373,16 +373,14 @@
         going_up, going_down = lax.ppermute(going_up, "z", up), lax.ppermute(going_down, "z", down)
         if s == 2:
             packed = pack_part(table, grouped).reshape(NX, NZ * CAP, per_row, dim)
-            going_up, going_down, packed = tie((going_up, going_down, packed))
             q_slots = lax.all_to_all(packed, "x", split_axis=0, concat_axis=0, tiled=True)
         elif s == 4:
             attend_due(s)
             far = lax.ppermute(q_slots[:, half * CAP : (half + 1) * CAP], "z", [(i, (i + 2) % NZ) for i in range(NZ)])
             going_up, going_down, outs, far, q_slots = tie((going_up, going_down, outs, far, q_slots))
-        elif s == 5 or s == 6:
+        elif s == 6:
             attend_due(s)
-            if s == 6:
-                back = [send_back(0)]
+            back = [send_back(0)]
             going_up, going_down, outs = tie((going_up, going_down, outs))
         elif s == 7:
             attend_due(s)

time: 173 us -> 162 us (0.936)
  waiting for transfers between devices: 36.1 us -> 28.6 us
  starting transfers between devices: 88.2 us -> 85 us
    ppermute x7, waiting for transfers between devices: 24.7 us -> 14 us  [per_device(): lax.ppermute(going_up, 'z', up)]
    ppermute x7, starting transfers between devices: 37.6 us -> 34 us  [per_device(): lax.ppermute(going_down, 'z', down)]
    ppermute x1, waiting for transfers between devices: 1.25 us -> 4.79 us  [per_device(): lax.ppermute(q_slots[:, half * CAP:(half + 1) * CAP], 'z', [(i, (i + 2) %...]
    ppermute x7, starting transfers between devices: 15.8 us -> 18.8 us  [per_device(): lax.ppermute(going_up, 'z', up)]
    all_to_all x1, starting transfers between devices: 16.5 us -> 13.5 us  [per_device(): lax.all_to_all(merged, ('y', 'core'), split_axis=0, concat_axis=0, tiled=...]
    ppermute x7, waiting for transfers between devices: 3.41 us -> 1.64 us  [per_device(): lax.ppermute(going_down, 'z', down)]
  transfers between devices with their start and end apart: 20 -> 20, of which waited for: 11 -> 7; matrix products, arithmetic and copies ran while one was open for 2% -> 2% of each run, Pallas kernels for 13% -> 14%
where the time goes in v3:
time: 162 us; the launch traced here: 161 us
  starting transfers between devices  85 us (52%)
  Pallas kernels  29.8 us (18%)
  waiting for transfers between devices  28.6 us (18%)
  blocking collectives  10.8 us (7%)
  other arithmetic  3.8 us (2%)
  local copies, waits for them, and re-layouts  2.08 us (1%)
    ppermute x7, starting transfers between devices, per_device(): lax.ppermute(going_down, 'z', down)  34 us
    ppermute x7, starting transfers between devices, per_device(): lax.ppermute(going_up, 'z', up)  18.8 us
    pallas_call x6, Pallas kernels, node_part(): pl.pallas_call(functools.partial(node_kernel, dim ** (-0.5), count), grid...  18.4 us
    ppermute x7, waiting for transfers between devices, per_device(): lax.ppermute(going_up, 'z', up)  14 us
    all_to_all x1, starting transfers between devices, per_device(): lax.all_to_all(merged, ('y', 'core'), split_axis=0, concat_axis=0, tiled=...  13.5 us
    all_to_all x1, blocking collectives, per_device(): lax.all_to_all(last, 'x', split_axis=0, concat_axis=0, tiled=True)  10.8 us
    all_to_all x1, starting transfers between devices, per_device(): lax.all_to_all(by_head, ('y', 'core'), split_axis=0, concat_axis=0, tiled...  5.42 us
    all_to_all x1, waiting for transfers between devices, per_device(): lax.all_to_all(merged, ('y', 'core'), split_axis=0, concat_axis=0, tiled=...  5.14 us
  transfers between devices with their start and end apart: 20, of which 7 were waited for; matrix products, arithmetic and copies ran while one was open for 2% of the time, Pallas kernels for 14%

profile of v3, /device:TPU:1, one launch (start us, length us, event | category | flops | bytes accessed | tf_op | source)
XLA Modules:
  0.0 161.2 jit_solution(6427694420060836483)
XLA Ops:
  0.8 1.4 maximum_maximum_fusion.refs_3_
  2.2 4.4 %collective-permute-start = (bf16[2064,128]{1,0:T(8,128)(2,1)S(1)}, bf16[2064,128]{1,0:T(8,128)(2,1)S(1)}, u32[]{:S(2)}, u32[]{:S(2)}) collective-permute-start(bf16[2064,128]{1,0:T(8,128)(2,1)S(1)} %maximum_maximum_fusion.refs_3_), channel_id=1, source_target_pairs={{0,32},{32,64},{64,96},{96,128},{128,160},{160,192},{192,224},{224... | collective-permute-start | bytes 1585160 | tf_op jit(solution)/shard_map/ppermute | solution.py:373
  6.6 9.5 %collective-permute-start.4 = (bf16[2064,128]{1,0:T(8,128)(2,1)S(1)}, bf16[2064,128]{1,0:T(8,128)(2,1)S(1)}, u32[]{:S(2)}, u32[]{:S(2)}) collective-permute-start(bf16[2064,128]{1,0:T(8,128)(2,1)S(1)} %maximum_maximum_fusion.refs_3_), channel_id=1, source_target_pairs={{0,480},{32,0},{64,32},{96,64},{128,96},{160,128},{192,160},{224,1... | collective-permute-start | bytes 1585160 | tf_op jit(solution)/shard_map/ppermute | solution.py:373
  16.1 0.9 copy.17
  17.0 5.4 %all-to-all-start = ((bf16[8,32,8,128]{3,2,1,0:T(8,128)(2,1)}), bf16[8,32,8,128]{3,2,1,0:T(8,128)(2,1)S(1)}, u32[]{:S(2)}, u32[]{:S(2)}) async-start(bf16[8,32,8,128]{3,2,1,0:T(8,128)(2,1)} %bitcast.20), calls=%async_computation | async-start | bytes 1048576 | tf_op jit(solution)/shard_map/all_to_all | solution.py:345
  22.4 0.1 reshape.119
  22.5 0.2 convert_reduce_fusion
  22.7 3.2 %collective-permute-done.refs_5_ = bf16[2064,128]{1,0:T(8,128)(2,1)S(1)} collective-permute-done((bf16[2064,128]{1,0:T(8,128)(2,1)S(1)}, bf16[2064,128]{1,0:T(8,128)(2,1)S(1)}, u32[]{:S(2)}, u32[]{:S(2)}) %collective-permute-start) | collective-permute-done | bytes 528416 | tf_op jit(solution)/shard_map/ppermute | solution.py:373
  25.9 1.9 %collective-permute-start.1 = (bf16[2064,128]{1,0:T(8,128)(2,1)S(1)}, bf16[2064,128]{1,0:T(8,128)(2,1)}, u32[]{:S(2)}, u32[]{:S(2)}) collective-permute-start(bf16[2064,128]{1,0:T(8,128)(2,1)S(1)} %collective-permute-done.refs_5_), channel_id=1, source_target_pairs={{0,32},{32,64},{64,96},{96,128},{128,160},{160,192},{192,224},{224... | collective-permute-start | bytes 1585160 | tf_op jit(solution)/shard_map/ppermute | solution.py:373
  27.8 4.6 %collective-permute-start.5 = (bf16[2064,128]{1,0:T(8,128)(2,1)S(1)}, bf16[2064,128]{1,0:T(8,128)(2,1)}, u32[]{:S(2)}, u32[]{:S(2)}) collective-permute-start(bf16[2064,128]{1,0:T(8,128)(2,1)S(1)} %collective-permute-done.4.refs_4_), channel_id=1, source_target_pairs={{0,480},{32,0},{64,32},{96,64},{128,96},{160,128},{192,160},{224,1... | collective-permute-start | bytes 1585160 | tf_op jit(solution)/shard_map/ppermute | solution.py:373
  32.4 0.1 select_reduce_fusion
  32.5 2.2 %pack.1 = bf16[192,32,128]{2,1,0:T(8,128)(2,1)} custom-call(s32[192]{0:T(256)S(1)} %broadcast_add_fusion.table_ref, bf16[64,32,128]{2,1,0:T(8,128)(2,1)S(1)} %bitcast.28), custom_call_target="tpu_custom_call" | custom-call | flops 1024 | bytes 1024 | tf_op jit(solution)/shard_map/pack/pallas_call | solution.py:135
  34.8 4.0 %all-to-all-start.1 = ((bf16[4,48,32,128]{3,2,1,0:T(8,128)(2,1)}), bf16[4,48,32,128]{3,2,1,0:T(8,128)(2,1)S(1)}, u32[]{:S(2)}, u32[]{:S(2)}) async-start(bf16[4,48,32,128]{3,2,1,0:T(8,128)(2,1)} %bitcast.9), calls=%async_computation.1 | async-start | bytes 3145728 | tf_op jit(solution)/shard_map/all_to_all | solution.py:376
  38.8 2.6 %collective-permute-done.1.refs_11_ = bf16[2064,128]{1,0:T(8,128)(2,1)} collective-permute-done((bf16[2064,128]{1,0:T(8,128)(2,1)S(1)}, bf16[2064,128]{1,0:T(8,128)(2,1)}, u32[]{:S(2)}, u32[]{:S(2)}) %collective-permute-start.1) | collective-permute-done | bytes 528416 | tf_op jit(solution)/shard_map/ppermute | solution.py:373
  41.4 1.9 %collective-permute-start.2 = (bf16[2064,128]{1,0:T(8,128)(2,1)}, bf16[2064,128]{1,0:T(8,128)(2,1)}, u32[]{:S(2)}, u32[]{:S(2)}) collective-permute-start(bf16[2064,128]{1,0:T(8,128)(2,1)} %collective-permute-done.1.refs_11_), channel_id=1, source_target_pairs={{0,32},{32,64},{64,96},{96,128},{128,160},{160,192},{192,224},{224... | collective-permute-start | bytes 1585160 | tf_op jit(solution)/shard_map/ppermute | solution.py:373
  43.3 4.6 %collective-permute-start.6 = (bf16[2064,128]{1,0:T(8,128)(2,1)}, bf16[2064,128]{1,0:T(8,128)(2,1)}, u32[]{:S(2)}, u32[]{:S(2)}) collective-permute-start(bf16[2064,128]{1,0:T(8,128)(2,1)} %collective-permute-done.5.refs_6_), channel_id=1, source_target_pairs={{0,480},{32,0},{64,32},{96,64},{128,96},{160,128},{192,160},{224,1... | collective-permute-start | bytes 1585160 | tf_op jit(solution)/shard_map/ppermute | solution.py:373
  47.9 8.3 %collective-permute-done.2.refs_10_ = bf16[2064,128]{1,0:T(8,128)(2,1)} collective-permute-done((bf16[2064,128]{1,0:T(8,128)(2,1)}, bf16[2064,128]{1,0:T(8,128)(2,1)}, u32[]{:S(2)}, u32[]{:S(2)}) %collective-permute-start.2) | collective-permute-done | bytes 528416 | tf_op jit(solution)/shard_map/ppermute | solution.py:373
  56.1 1.9 %collective-permute-start.3 = (bf16[2064,128]{1,0:T(8,128)(2,1)}, bf16[2064,128]{1,0:T(8,128)(2,1)}, u32[]{:S(2)}, u32[]{:S(2)}) collective-permute-start(bf16[2064,128]{1,0:T(8,128)(2,1)} %collective-permute-done.2.refs_10_), channel_id=1, source_target_pairs={{0,32},{32,64},{64,96},{96,128},{128,160},{160,192},{192,224},{224... | collective-permute-start | bytes 1585160 | tf_op jit(solution)/shard_map/ppermute | solution.py:373
  58.1 4.6 %collective-permute-start.7 = (bf16[2064,128]{1,0:T(8,128)(2,1)}, bf16[2064,128]{1,0:T(8,128)(2,1)}, u32[]{:S(2)}, u32[]{:S(2)}) collective-permute-start(bf16[2064,128]{1,0:T(8,128)(2,1)} %collective-permute-done.6.refs_7_), channel_id=1, source_target_pairs={{0,480},{32,0},{64,32},{96,64},{128,96},{160,128},{192,160},{224,1... | collective-permute-start | bytes 1585160 | tf_op jit(solution)/shard_map/ppermute | solution.py:373
  62.7 1.9 %collective-permute-start.8 = (bf16[4,3,32,128]{3,2,1,0:T(8,128)(2,1)S(1)}, bf16[4,3,32,128]{3,2,1,0:T(8,128)(2,1)S(1)}, u32[]{:S(2)}, u32[]{:S(2)}) collective-permute-start(bf16[4,3,32,128]{3,2,1,0:T(8,128)(2,1)S(1)} %slice.8), channel_id=1, source_target_pairs={{0,64},{32,96},{64,128},{96,160},{128,192},{160,224},{192,256},{22... | collective-permute-start | bytes 294920 | tf_op jit(solution)/shard_map/ppermute | solution.py:379
  64.6 2.4 %node.6 = bf16[4,320,128]{2,1,0:T(8,128)(2,1)S(1)} custom-call(bf16[4,48,32,128]{3,2,1,0:T(8,128)(2,1)S(1)} %all-to-all-done.1.refs_0_.refs_1_.refs_2_.refs_3_.refs_4_.refs_5_, bf16[4,48,32,128]{3,2,1,0:T(8,128)(2,1)S(1)} %all-to-all-done.1.refs_0_.refs_1_.refs_2_.refs_3_.refs_4_.refs_5_, ...), custom_call_target="tpu_custom_call" | custom-call | flops 1024 | bytes 1024 | tf_op jit(solution)/shard_map/node/pallas_call | solution.py:188
  67.0 4.8 %collective-permute-done.8.refs_0_ = bf16[4,3,32,128]{3,2,1,0:T(8,128)(2,1)S(1)} collective-permute-done((bf16[4,3,32,128]{3,2,1,0:T(8,128)(2,1)S(1)}, bf16[4,3,32,128]{3,2,1,0:T(8,128)(2,1)S(1)}, u32[]{:S(2)}, u32[]{:S(2)}) %collective-permute-start.8) | collective-permute-done | bytes 98336 | tf_op jit(solution)/shard_map/ppermute | solution.py:379
  71.8 0.6 copy-done.4
  72.5 4.0 %collective-permute-start.9 = (bf16[2064,128]{1,0:T(8,128)(2,1)}, bf16[2064,128]{1,0:T(8,128)(2,1)}, u32[]{:S(2)}, u32[]{:S(2)}) collective-permute-start(bf16[2064,128]{1,0:T(8,128)(2,1)} %collective-permute-done.3.refs_9_), channel_id=1, source_target_pairs={{0,32},{32,64},{64,96},{96,128},{128,160},{160,192},{192,224},{224... | collective-permute-start | bytes 1585160 | tf_op jit(solution)/shard_map/ppermute | solution.py:373
  76.5 2.5 %collective-permute-start.11 = (bf16[2064,128]{1,0:T(8,128)(2,1)}, bf16[2064,128]{1,0:T(8,128)(2,1)}, u32[]{:S(2)}, u32[]{:S(2)}) collective-permute-start(bf16[2064,128]{1,0:T(8,128)(2,1)} %collective-permute-done.7.refs_8_), channel_id=1, source_target_pairs={{0,480},{32,0},{64,32},{96,64},{128,96},{160,128},{192,160},{224,1... | collective-permute-start | bytes 1585160 | tf_op jit(solution)/shard_map/ppermute | solution.py:373
  79.0 5.9 %node.7 = bf16[4,624,128]{2,1,0:T(8,128)(2,1)S(1)} custom-call(bf16[4,48,32,128]{3,2,1,0:T(8,128)(2,1)S(1)} %all-to-all-done.1.refs_0_.refs_1_.refs_2_.refs_3_.refs_4_.refs_5_, bf16[4,48,32,128]{3,2,1,0:T(8,128)(2,1)S(1)} %all-to-all-done.1.refs_0_.refs_1_.refs_2_.refs_3_.refs_4_.refs_5_, ...), custom_call_target="tpu_custom_call" | custom-call | flops 1024 | bytes 1024 | tf_op jit(solution)/shard_map/node/pallas_call | solution.py:188
  84.9 2.8 %collective-permute-start.10 = (bf16[2064,128]{1,0:T(8,128)(2,1)}, bf16[2064,128]{1,0:T(8,128)(2,1)}, u32[]{:S(2)}, u32[]{:S(2)}) collective-permute-start(bf16[2064,128]{1,0:T(8,128)(2,1)} %collective-permute-done.9.refs_3_), channel_id=1, source_target_pairs={{0,32},{32,64},{64,96},{96,128},{128,160},{160,192},{192,224},{224... | collective-permute-start | bytes 1585160 | tf_op jit(solution)/shard_map/ppermute | solution.py:373
  87.7 3.0 %node.8 = bf16[4,208,128]{2,1,0:T(8,128)(2,1)S(1)} custom-call(bf16[4,48,32,128]{3,2,1,0:T(8,128)(2,1)S(1)} %all-to-all-done.1.refs_0_.refs_1_.refs_2_.refs_3_.refs_4_.refs_5_, bf16[4,48,32,128]{3,2,1,0:T(8,128)(2,1)S(1)} %all-to-all-done.1.refs_0_.refs_1_.refs_2_.refs_3_.refs_4_.refs_5_, bf16[2064,128]{1,0:T(8,128)(2,1)} %collective-permute-done.11.refs_2_, ...), custom_call_target="tpu_custom_call" | custom-call | flops 1024 | bytes 1024 | tf_op jit(solution)/shard_map/node/pallas_call | solution.py:188
  90.7 3.7 %collective-permute-start.12 = (bf16[2064,128]{1,0:T(8,128)(2,1)}, bf16[2064,128]{1,0:T(8,128)(2,1)S(1)}, u32[]{:S(2)}, u32[]{:S(2)}) collective-permute-start(bf16[2064,128]{1,0:T(8,128)(2,1)} %collective-permute-done.11.refs_2_), channel_id=1, source_target_pairs={{0,480},{32,0},{64,32},{96,64},{128,96},{160,128},{192,160},{224,1... | collective-permute-start | bytes 1585160 | tf_op jit(solution)/shard_map/ppermute | solution.py:373
  94.4 1.1 pad_maximum_fusion
  95.5 4.1 %all-to-all-start.2 = ((bf16[4,1152,128]{2,1,0:T(8,128)(2,1)}), bf16[4,1152,128]{2,1,0:T(8,128)(2,1)S(1)}, u32[]{:S(2)}, u32[]{:S(2)}) async-start(bf16[4,1152,128]{2,1,0:T(8,128)(2,1)} %pad_maximum_fusion), calls=%async_computation.2 | async-start | bytes 2359296 | tf_op jit(solution)/shard_map/all_to_all | solution.py:362
  99.7 1.6 %collective-permute-done.12.refs_2_.refs_1_ = bf16[2064,128]{1,0:T(8,128)(2,1)S(1)} collective-permute-done((bf16[2064,128]{1,0:T(8,128)(2,1)}, bf16[2064,128]{1,0:T(8,128)(2,1)S(1)}, u32[]{:S(2)}, u32[]{:S(2)}) %collective-permute-start.12) | collective-permute-done | bytes 528416 | tf_op jit(solution)/shard_map/ppermute | solution.py:373
  101.3 1.9 %collective-permute-start.13 = (bf16[2064,128]{1,0:T(8,128)(2,1)}, bf16[2064,128]{1,0:T(8,128)(2,1)}, u32[]{:S(2)}, u32[]{:S(2)}) collective-permute-start(bf16[2064,128]{1,0:T(8,128)(2,1)} %collective-permute-done.10.refs_3_), channel_id=1, source_target_pairs={{0,32},{32,64},{64,96},{96,128},{128,160},{160,192},{192,224},{224... | collective-permute-start | bytes 1585160 | tf_op jit(solution)/shard_map/ppermute | solution.py:373
  103.2 4.6 %collective-permute-start.14 = (bf16[2064,128]{1,0:T(8,128)(2,1)S(1)}, bf16[2064,128]{1,0:T(8,128)(2,1)}, u32[]{:S(2)}, u32[]{:S(2)}) collective-permute-start(bf16[2064,128]{1,0:T(8,128)(2,1)S(1)} %collective-permute-done.12.refs_2_.refs_1_), channel_id=1, source_target_pairs={{0,480},{32,0},{64,32},{96,64},{128,96},{160,128},{192,160},{224,1... | collective-permute-start | bytes 1585160 | tf_op jit(solution)/shard_map/ppermute | solution.py:373
  107.8 1.2 node.10
  109.0 3.2 %collective-permute-start.15 = (bf16[4,112,128]{2,1,0:T(8,128)(2,1)S(1)}, bf16[4,112,128]{2,1,0:T(8,128)(2,1)}, u32[]{:S(2)}, u32[]{:S(2)}) collective-permute-start(bf16[4,112,128]{2,1,0:T(8,128)(2,1)S(1)} %node.10), channel_id=1, source_target_pairs={{0,448},{32,480},{64,0},{96,32},{128,64},{160,96},{192,128},{224,1... | collective-permute-start | bytes 344072 | tf_op jit(solution)/shard_map/ppermute | solution.py:388
  112.2 2.9 %node.9 = bf16[4,208,128]{2,1,0:T(8,128)(2,1)S(1)} custom-call(bf16[4,48,32,128]{3,2,1,0:T(8,128)(2,1)S(1)} %all-to-all-done.1.refs_0_.refs_1_.refs_2_.refs_3_.refs_4_.refs_5_, bf16[4,48,32,128]{3,2,1,0:T(8,128)(2,1)S(1)} %all-to-all-done.1.refs_0_.refs_1_.refs_2_.refs_3_.refs_4_.refs_5_, bf16[2064,128]{1,0:T(8,128)(2,1)S(1)} %collective-permute-done.12.refs_2_.refs_1_, ...), custom_call_target="tpu_custom_call" | custom-call | flops 1024 | bytes 1024 | tf_op jit(solution)/shard_map/node/pallas_call | solution.py:188
  115.1 3.0 %collective-permute-done.15 = bf16[4,112,128]{2,1,0:T(8,128)(2,1)} collective-permute-done((bf16[4,112,128]{2,1,0:T(8,128)(2,1)S(1)}, bf16[4,112,128]{2,1,0:T(8,128)(2,1)}, u32[]{:S(2)}, u32[]{:S(2)}) %collective-permute-start.15) | collective-permute-done | bytes 114720 | tf_op jit(solution)/shard_map/ppermute | solution.py:388
  118.1 3.0 %node.11 = bf16[4,208,128]{2,1,0:T(8,128)(2,1)S(1)} custom-call(bf16[4,48,32,128]{3,2,1,0:T(8,128)(2,1)S(1)} %all-to-all-done.1.refs_0_.refs_1_.refs_2_.refs_3_.refs_4_.refs_5_, bf16[4,48,32,128]{3,2,1,0:T(8,128)(2,1)S(1)} %all-to-all-done.1.refs_0_.refs_1_.refs_2_.refs_3_.refs_4_.refs_5_, bf16[2064,128]{1,0:T(8,128)(2,1)} %collective-permute-done.14.refs_2_, ...), custom_call_target="tpu_custom_call" | custom-call | flops 1024 | bytes 1024 | tf_op jit(solution)/shard_map/node/pallas_call | solution.py:188
  121.1 0.9 pad_maximum_fusion.1
  122.1 10.8 %all_to_all.25.refs_1_ = bf16[4,528,128]{2,1,0:T(8,128)(2,1)S(1)} all-to-all(bf16[4,528,128]{2,1,0:T(8,128)(2,1)S(1)} %pad_maximum_fusion.1), channel_id=1, replica_groups=mesh['z'=16,'x'=4,'y'=4,'core'=2] {'x'}, dimensions={0} | all-to-all | bytes 1081344 | tf_op jit(solution)/shard_map/all_to_all | solution.py:393
  132.9 2.7 %merge.1 = bf16[8,304,128]{2,1,0:T(8,128)(2,1)} custom-call(s32[192]{0:T(256)S(1)} %broadcast_add_fusion.table_ref, bf16[4,1152,128]{2,1,0:T(8,128)(2,1)S(1)} %all-to-all-done.2.refs_0_, bf16[4,528,128]{2,1,0:T(8,128)(2,1)S(1)} %all_to_all.25.refs_1_), custom_call_target="tpu_custom_call" | custom-call | flops 4194304 | bytes 4194304 | tf_op jit(solution)/shard_map/merge/pallas_call | solution.py:251
  135.6 13.5 %all-to-all-start.4 = ((bf16[8,304,128]{2,1,0:T(8,128)(2,1)}), bf16[8,304,128]{2,1,0:T(8,128)(2,1)S(1)}, u32[]{:S(2)}, u32[]{:S(2)}) async-start(bf16[8,304,128]{2,1,0:T(8,128)(2,1)} %merge.1), calls=%async_computation.4 | async-start | bytes 1245184 | tf_op jit(solution)/shard_map/all_to_all | solution.py:395
  149.1 4.9 %suffix.1 = (f32[8,256,128]{2,1,0:T(8,128)S(1)}, f32[8,8,256]{2,1,0:T(8,128)S(1)}) custom-call(s32[8]{0:T(128)S(1)} %copy-done.8, bf16[8,256,128]{2,1,0:T(8,128)(2,1)S(1)} %bitcast.27, bf16[8,256,128]{2,1,0:T(8,128)(2,1)S(1)} %bitcast.30, bf16[8,32,128]{2,1,0:T(8,128)(2,1)S(1)} %bitcast.32, bf16[8,256,128]{2,1,0:T(8,128)(2,1)S(1)} %bitcast.31, ...), custom_call_target="tpu_custom_call" | custom-call | flops 268435456 | bytes 4194304 | tf_op jit(solution)/shard_map/suffix/pallas_call | solution.py:91
  154.1 0.2 reshape.131
  154.3 0.2 reshape.132
  154.5 5.1 %all-to-all-done.4.arrived_ref = bf16[8,304,128]{2,1,0:T(8,128)(2,1)S(1)} async-done(((bf16[8,304,128]{2,1,0:T(8,128)(2,1)}), bf16[8,304,128]{2,1,0:T(8,128)(2,1)S(1)}, u32[]{:S(2)}, u32[]{:S(2)}) %all-to-all-start.4) | async-done | bytes 622624 | tf_op jit(solution)/shard_map/all_to_all | solution.py:395
  159.6 1.6 final.1
  (40 shorter events, 0.3 us)
Async XLA Ops:
  0.0 16.1 %copy-start = (bf16[8,4,64,128]{3,2,1,0:T(8,128)(2,1)S(1)}, bf16[8,4,64,128]{3,2,1,0:T(8,128)(2,1)}, u32[]{:S(2)}) copy-start(bf16[8,4,64,128]{3,2,1,0:T(8,128)(2,1)} %param.10) | copy-start | bytes 1572868
  2.2 20.2 %copy-start.9 = (s32[64,2]{0,1:T(2,128)S(1)}, s32[64,2]{0,1:T(2,128)}, u32[]{:S(2)}) copy-start(s32[64,2]{0,1:T(2,128)} %param.16) | copy-start | bytes 1540
  2.2 23.7 %collective-permute-start = (bf16[2064,128]{1,0:T(8,128)(2,1)S(1)}, bf16[2064,128]{1,0:T(8,128)(2,1)S(1)}, u32[]{:S(2)}, u32[]{:S(2)}) collective-permute-start(bf16[2064,128]{1,0:T(8,128)(2,1)S(1)} %maximum_maximum_fusion.refs_3_), channel_id=1, source_target_pairs={{0,32},{32,64},{64,96},{96,128},{128,160},{160,192},{192,224},{224... | collective-permute-start | bytes 1585160 | tf_op jit(solution)/shard_map/ppermute | solution.py:373
  6.6 21.2 %collective-permute-start.4 = (bf16[2064,128]{1,0:T(8,128)(2,1)S(1)}, bf16[2064,128]{1,0:T(8,128)(2,1)S(1)}, u32[]{:S(2)}, u32[]{:S(2)}) collective-permute-start(bf16[2064,128]{1,0:T(8,128)(2,1)S(1)} %maximum_maximum_fusion.refs_3_), channel_id=1, source_target_pairs={{0,480},{32,0},{64,32},{96,64},{128,96},{160,128},{192,160},{224,1... | collective-permute-start | bytes 1585160 | tf_op jit(solution)/shard_map/ppermute | solution.py:373
  17.0 15.5 %all-to-all-start = ((bf16[8,32,8,128]{3,2,1,0:T(8,128)(2,1)}), bf16[8,32,8,128]{3,2,1,0:T(8,128)(2,1)S(1)}, u32[]{:S(2)}, u32[]{:S(2)}) async-start(bf16[8,32,8,128]{3,2,1,0:T(8,128)(2,1)} %bitcast.20), calls=%async_computation | async-start | bytes 1048576 | tf_op jit(solution)/shard_map/all_to_all | solution.py:345
  25.9 15.5 %collective-permute-start.1 = (bf16[2064,128]{1,0:T(8,128)(2,1)S(1)}, bf16[2064,128]{1,0:T(8,128)(2,1)}, u32[]{:S(2)}, u32[]{:S(2)}) collective-permute-start(bf16[2064,128]{1,0:T(8,128)(2,1)S(1)} %collective-permute-done.refs_5_), channel_id=1, source_target_pairs={{0,32},{32,64},{64,96},{96,128},{128,160},{160,192},{192,224},{224... | collective-permute-start | bytes 1585160 | tf_op jit(solution)/shard_map/ppermute | solution.py:373
  27.8 15.5 %collective-permute-start.5 = (bf16[2064,128]{1,0:T(8,128)(2,1)S(1)}, bf16[2064,128]{1,0:T(8,128)(2,1)}, u32[]{:S(2)}, u32[]{:S(2)}) collective-permute-start(bf16[2064,128]{1,0:T(8,128)(2,1)S(1)} %collective-permute-done.4.refs_4_), channel_id=1, source_target_pairs={{0,480},{32,0},{64,32},{96,64},{128,96},{160,128},{192,160},{224,1... | collective-permute-start | bytes 1585160 | tf_op jit(solution)/shard_map/ppermute | solution.py:373
  34.8 27.9 %all-to-all-start.1 = ((bf16[4,48,32,128]{3,2,1,0:T(8,128)(2,1)}), bf16[4,48,32,128]{3,2,1,0:T(8,128)(2,1)S(1)}, u32[]{:S(2)}, u32[]{:S(2)}) async-start(bf16[4,48,32,128]{3,2,1,0:T(8,128)(2,1)} %bitcast.9), calls=%async_computation.1 | async-start | bytes 3145728 | tf_op jit(solution)/shard_map/all_to_all | solution.py:376
  41.4 14.8 %collective-permute-start.2 = (bf16[2064,128]{1,0:T(8,128)(2,1)}, bf16[2064,128]{1,0:T(8,128)(2,1)}, u32[]{:S(2)}, u32[]{:S(2)}) collective-permute-start(bf16[2064,128]{1,0:T(8,128)(2,1)} %collective-permute-done.1.refs_11_), channel_id=1, source_target_pairs={{0,32},{32,64},{64,96},{96,128},{128,160},{160,192},{192,224},{224... | collective-permute-start | bytes 1585160 | tf_op jit(solution)/shard_map/ppermute | solution.py:373
  43.3 14.8 %collective-permute-start.6 = (bf16[2064,128]{1,0:T(8,128)(2,1)}, bf16[2064,128]{1,0:T(8,128)(2,1)}, u32[]{:S(2)}, u32[]{:S(2)}) collective-permute-start(bf16[2064,128]{1,0:T(8,128)(2,1)} %collective-permute-done.5.refs_6_), channel_id=1, source_target_pairs={{0,480},{32,0},{64,32},{96,64},{128,96},{160,128},{192,160},{224,1... | collective-permute-start | bytes 1585160 | tf_op jit(solution)/shard_map/ppermute | solution.py:373
  56.1 16.3 %collective-permute-start.3 = (bf16[2064,128]{1,0:T(8,128)(2,1)}, bf16[2064,128]{1,0:T(8,128)(2,1)}, u32[]{:S(2)}, u32[]{:S(2)}) collective-permute-start(bf16[2064,128]{1,0:T(8,128)(2,1)} %collective-permute-done.2.refs_10_), channel_id=1, source_target_pairs={{0,32},{32,64},{64,96},{96,128},{128,160},{160,192},{192,224},{224... | collective-permute-start | bytes 1585160 | tf_op jit(solution)/shard_map/ppermute | solution.py:373
  58.1 14.4 %collective-permute-start.7 = (bf16[2064,128]{1,0:T(8,128)(2,1)}, bf16[2064,128]{1,0:T(8,128)(2,1)}, u32[]{:S(2)}, u32[]{:S(2)}) collective-permute-start(bf16[2064,128]{1,0:T(8,128)(2,1)} %collective-permute-done.6.refs_7_), channel_id=1, source_target_pairs={{0,480},{32,0},{64,32},{96,64},{128,96},{160,128},{192,160},{224,1... | collective-permute-start | bytes 1585160 | tf_op jit(solution)/shard_map/ppermute | solution.py:373
  62.7 9.1 %collective-permute-start.8 = (bf16[4,3,32,128]{3,2,1,0:T(8,128)(2,1)S(1)}, bf16[4,3,32,128]{3,2,1,0:T(8,128)(2,1)S(1)}, u32[]{:S(2)}, u32[]{:S(2)}) collective-permute-start(bf16[4,3,32,128]{3,2,1,0:T(8,128)(2,1)S(1)} %slice.8), channel_id=1, source_target_pairs={{0,64},{32,96},{64,128},{96,160},{128,192},{160,224},{192,256},{22... | collective-permute-start | bytes 294920 | tf_op jit(solution)/shard_map/ppermute | solution.py:379
  71.8 0.6 copy-start.4
  72.5 12.4 %collective-permute-start.9 = (bf16[2064,128]{1,0:T(8,128)(2,1)}, bf16[2064,128]{1,0:T(8,128)(2,1)}, u32[]{:S(2)}, u32[]{:S(2)}) collective-permute-start(bf16[2064,128]{1,0:T(8,128)(2,1)} %collective-permute-done.3.refs_9_), channel_id=1, source_target_pairs={{0,32},{32,64},{64,96},{96,128},{128,160},{160,192},{192,224},{224... | collective-permute-start | bytes 1585160 | tf_op jit(solution)/shard_map/ppermute | solution.py:373
  76.5 11.2 %collective-permute-start.11 = (bf16[2064,128]{1,0:T(8,128)(2,1)}, bf16[2064,128]{1,0:T(8,128)(2,1)}, u32[]{:S(2)}, u32[]{:S(2)}) collective-permute-start(bf16[2064,128]{1,0:T(8,128)(2,1)} %collective-permute-done.7.refs_8_), channel_id=1, source_target_pairs={{0,480},{32,0},{64,32},{96,64},{128,96},{160,128},{192,160},{224,1... | collective-permute-start | bytes 1585160 | tf_op jit(solution)/shard_map/ppermute | solution.py:373
  84.9 14.8 %collective-permute-start.10 = (bf16[2064,128]{1,0:T(8,128)(2,1)}, bf16[2064,128]{1,0:T(8,128)(2,1)}, u32[]{:S(2)}, u32[]{:S(2)}) collective-permute-start(bf16[2064,128]{1,0:T(8,128)(2,1)} %collective-permute-done.9.refs_3_), channel_id=1, source_target_pairs={{0,32},{32,64},{64,96},{96,128},{128,160},{160,192},{192,224},{224... | collective-permute-start | bytes 1585160 | tf_op jit(solution)/shard_map/ppermute | solution.py:373
  90.7 10.6 %collective-permute-start.12 = (bf16[2064,128]{1,0:T(8,128)(2,1)}, bf16[2064,128]{1,0:T(8,128)(2,1)S(1)}, u32[]{:S(2)}, u32[]{:S(2)}) collective-permute-start(bf16[2064,128]{1,0:T(8,128)(2,1)} %collective-permute-done.11.refs_2_), channel_id=1, source_target_pairs={{0,480},{32,0},{64,32},{96,64},{128,96},{160,128},{192,160},{224,1... | collective-permute-start | bytes 1585160 | tf_op jit(solution)/shard_map/ppermute | solution.py:373
  95.5 12.3 %copy-start.5 = (bf16[4,3,32,128]{3,2,1,0:T(8,128)(2,1)S(1)}, bf16[4,3,32,128]{3,2,1,0:T(8,128)(2,1)}, u32[]{:S(2)}) copy-start(bf16[4,3,32,128]{3,2,1,0:T(8,128)(2,1)} %copy-done.4) | copy-start | bytes 294916
  95.5 22.6 %all-to-all-start.2 = ((bf16[4,1152,128]{2,1,0:T(8,128)(2,1)}), bf16[4,1152,128]{2,1,0:T(8,128)(2,1)S(1)}, u32[]{:S(2)}, u32[]{:S(2)}) async-start(bf16[4,1152,128]{2,1,0:T(8,128)(2,1)} %pad_maximum_fusion), calls=%async_computation.2 | async-start | bytes 2359296 | tf_op jit(solution)/shard_map/all_to_all | solution.py:362
  101.3 16.8 %collective-permute-start.13 = (bf16[2064,128]{1,0:T(8,128)(2,1)}, bf16[2064,128]{1,0:T(8,128)(2,1)}, u32[]{:S(2)}, u32[]{:S(2)}) collective-permute-start(bf16[2064,128]{1,0:T(8,128)(2,1)} %collective-permute-done.10.refs_3_), channel_id=1, source_target_pairs={{0,32},{32,64},{64,96},{96,128},{128,160},{160,192},{192,224},{224... | collective-permute-start | bytes 1585160 | tf_op jit(solution)/shard_map/ppermute | solution.py:373
  103.2 14.9 %collective-permute-start.14 = (bf16[2064,128]{1,0:T(8,128)(2,1)S(1)}, bf16[2064,128]{1,0:T(8,128)(2,1)}, u32[]{:S(2)}, u32[]{:S(2)}) collective-permute-start(bf16[2064,128]{1,0:T(8,128)(2,1)S(1)} %collective-permute-done.12.refs_2_.refs_1_), channel_id=1, source_target_pairs={{0,480},{32,0},{64,32},{96,64},{128,96},{160,128},{192,160},{224,1... | collective-permute-start | bytes 1585160 | tf_op jit(solution)/shard_map/ppermute | solution.py:373
  109.0 9.1 %collective-permute-start.15 = (bf16[4,112,128]{2,1,0:T(8,128)(2,1)S(1)}, bf16[4,112,128]{2,1,0:T(8,128)(2,1)}, u32[]{:S(2)}, u32[]{:S(2)}) collective-permute-start(bf16[4,112,128]{2,1,0:T(8,128)(2,1)S(1)} %node.10), channel_id=1, source_target_pairs={{0,448},{32,480},{64,0},{96,32},{128,64},{160,96},{192,128},{224,1... | collective-permute-start | bytes 344072 | tf_op jit(solution)/shard_map/ppermute | solution.py:388
  132.9 16.2 %copy-start.3 = (bf16[8,32,8,128]{3,2,1,0:T(8,128)(2,1)S(1)}, bf16[8,32,8,128]{3,2,1,0:T(8,128)(2,1)}, u32[]{:S(2)}) copy-start(bf16[8,32,8,128]{3,2,1,0:T(8,128)(2,1)} %param.14) | copy-start | bytes 1572868
  135.6 13.5 %copy-start.1 = (bf16[8,4,64,128]{3,2,1,0:T(8,128)(2,1)S(1)}, bf16[8,4,64,128]{3,2,1,0:T(8,128)(2,1)}, u32[]{:S(2)}) copy-start(bf16[8,4,64,128]{3,2,1,0:T(8,128)(2,1)} %param.10) | copy-start | bytes 1572868
  135.6 13.5 %copy-start.2 = (bf16[8,32,8,128]{3,2,1,0:T(8,128)(2,1)S(1)}, bf16[8,32,8,128]{3,2,1,0:T(8,128)(2,1)}, u32[]{:S(2)}) copy-start(bf16[8,32,8,128]{3,2,1,0:T(8,128)(2,1)} %param.13) | copy-start | bytes 1572868
  135.6 13.5 %copy-start.6 = (bf16[8,4,8,128]{3,2,1,0:T(8,128)(2,1)S(1)}, bf16[8,4,8,128]{3,2,1,0:T(8,128)(2,1)}, u32[]{:S(2)}) copy-start(bf16[8,4,8,128]{3,2,1,0:T(8,128)(2,1)} %param.11) | copy-start | bytes 196612
  135.6 13.5 %copy-start.7 = (bf16[8,4,8,128]{3,2,1,0:T(8,128)(2,1)S(1)}, bf16[8,4,8,128]{3,2,1,0:T(8,128)(2,1)}, u32[]{:S(2)}) copy-start(bf16[8,4,8,128]{3,2,1,0:T(8,128)(2,1)} %param.12) | copy-start | bytes 196612
  135.6 13.6 %copy-start.8 = (s32[8]{0:T(128)S(1)}, s32[8]{0:T(128)}, u32[]{:S(2)}) copy-start(s32[8]{0:T(128)} %len_ref.1) | copy-start | bytes 100
  135.6 24.0 %all-to-all-start.4 = ((bf16[8,304,128]{2,1,0:T(8,128)(2,1)}), bf16[8,304,128]{2,1,0:T(8,128)(2,1)S(1)}, u32[]{:S(2)}, u32[]{:S(2)}) async-start(bf16[8,304,128]{2,1,0:T(8,128)(2,1)} %merge.1), calls=%async_computation.4 | async-start | bytes 1245184 | tf_op jit(solution)/shard_map/all_to_all | solution.py:395

commit v4 on v3

--- a/solution.py
+++ b/solution.py
@@ -17,7 +17,7 @@
 CUTS = [[0, 1, 2], [3, 4]]
 F32 = jnp.float32
 BF16 = jnp.bfloat16
-VMEM_LIMIT = 20 * 1024 * 1024
+VMEM_LIMIT = 10 * 1024 * 1024
 VM = pl.BlockSpec(memory_space=pltpu.VMEM)
 
 

time: 162 us -> 162 us (level)
  no operation moved by 1% of the time
where the time goes in v4:
time: 162 us; the launch traced here: 161 us
  starting transfers between devices  85.5 us (53%)
  Pallas kernels  29.8 us (18%)
  waiting for transfers between devices  28.1 us (17%)
  blocking collectives  10.8 us (7%)
  other arithmetic  3.8 us (2%)
    ppermute x7, starting transfers between devices, per_device(): lax.ppermute(going_down, 'z', down)  34 us
    ppermute x7, starting transfers between devices, per_device(): lax.ppermute(going_up, 'z', up)  18.8 us
    pallas_call x6, Pallas kernels, node_part(): pl.pallas_call(functools.partial(node_kernel, dim ** (-0.5), count), grid...  18.4 us
    ppermute x7, waiting for transfers between devices, per_device(): lax.ppermute(going_up, 'z', up)  14 us
    all_to_all x1, starting transfers between devices, per_device(): lax.all_to_all(merged, ('y', 'core'), split_axis=0, concat_axis=0, tiled=...  14 us
    all_to_all x1, blocking collectives, per_device(): lax.all_to_all(last, 'x', split_axis=0, concat_axis=0, tiled=True)  10.8 us
    all_to_all x1, starting transfers between devices, per_device(): lax.all_to_all(by_head, ('y', 'core'), split_axis=0, concat_axis=0, tiled...  5.42 us
    all_to_all x1, waiting for transfers between devices, per_device(): lax.all_to_all(merged, ('y', 'core'), split_axis=0, concat_axis=0, tiled=...  5.14 us
  transfers between devices with their start and end apart: 20, of which 7 were waited for; matrix products, arithmetic and copies ran while one was open for 2% of the time, Pallas kernels for 14%

profile of v4, /device:TPU:1, one launch (start us, length us, event | category | flops | bytes accessed | tf_op | source)
XLA Modules:
  0.0 160.6 jit_solution(18089292724443423997)
XLA Ops:
  0.7 0.1 fusion.2
  0.8 1.4 maximum_maximum_fusion.refs_3_
  2.2 4.4 %collective-permute-start = (bf16[2064,128]{1,0:T(8,128)(2,1)S(1)}, bf16[2064,128]{1,0:T(8,128)(2,1)S(1)}, u32[]{:S(2)}, u32[]{:S(2)}) collective-permute-start(bf16[2064,128]{1,0:T(8,128)(2,1)S(1)} %maximum_maximum_fusion.refs_3_), channel_id=1, source_target_pairs={{0,32},{32,64},{64,96},{96,128},{128,160},{160,192},{192,224},{224... | collective-permute-start | bytes 1585160 | tf_op jit(solution)/shard_map/ppermute | solution.py:373
  6.6 9.5 %collective-permute-start.4 = (bf16[2064,128]{1,0:T(8,128)(2,1)S(1)}, bf16[2064,128]{1,0:T(8,128)(2,1)S(1)}, u32[]{:S(2)}, u32[]{:S(2)}) collective-permute-start(bf16[2064,128]{1,0:T(8,128)(2,1)S(1)} %maximum_maximum_fusion.refs_3_), channel_id=1, source_target_pairs={{0,480},{32,0},{64,32},{96,64},{128,96},{160,128},{192,160},{224,1... | collective-permute-start | bytes 1585160 | tf_op jit(solution)/shard_map/ppermute | solution.py:373
  16.1 0.9 copy.17
  17.0 5.4 %all-to-all-start = ((bf16[8,32,8,128]{3,2,1,0:T(8,128)(2,1)}), bf16[8,32,8,128]{3,2,1,0:T(8,128)(2,1)S(1)}, u32[]{:S(2)}, u32[]{:S(2)}) async-start(bf16[8,32,8,128]{3,2,1,0:T(8,128)(2,1)} %bitcast.20), calls=%async_computation | async-start | bytes 1048576 | tf_op jit(solution)/shard_map/all_to_all | solution.py:345
  22.4 0.1 reshape.119
  22.5 0.2 convert_reduce_fusion
  22.7 3.2 %collective-permute-done.refs_5_ = bf16[2064,128]{1,0:T(8,128)(2,1)S(1)} collective-permute-done((bf16[2064,128]{1,0:T(8,128)(2,1)S(1)}, bf16[2064,128]{1,0:T(8,128)(2,1)S(1)}, u32[]{:S(2)}, u32[]{:S(2)}) %collective-permute-start) | collective-permute-done | bytes 528416 | tf_op jit(solution)/shard_map/ppermute | solution.py:373
  25.9 1.9 %collective-permute-start.1 = (bf16[2064,128]{1,0:T(8,128)(2,1)S(1)}, bf16[2064,128]{1,0:T(8,128)(2,1)}, u32[]{:S(2)}, u32[]{:S(2)}) collective-permute-start(bf16[2064,128]{1,0:T(8,128)(2,1)S(1)} %collective-permute-done.refs_5_), channel_id=1, source_target_pairs={{0,32},{32,64},{64,96},{96,128},{128,160},{160,192},{192,224},{224... | collective-permute-start | bytes 1585160 | tf_op jit(solution)/shard_map/ppermute | solution.py:373
  27.8 4.6 %collective-permute-start.5 = (bf16[2064,128]{1,0:T(8,128)(2,1)S(1)}, bf16[2064,128]{1,0:T(8,128)(2,1)}, u32[]{:S(2)}, u32[]{:S(2)}) collective-permute-start(bf16[2064,128]{1,0:T(8,128)(2,1)S(1)} %collective-permute-done.4.refs_4_), channel_id=1, source_target_pairs={{0,480},{32,0},{64,32},{96,64},{128,96},{160,128},{192,160},{224,1... | collective-permute-start | bytes 1585160 | tf_op jit(solution)/shard_map/ppermute | solution.py:373
  32.4 0.1 select_reduce_fusion
  32.5 2.2 %pack.1 = bf16[192,32,128]{2,1,0:T(8,128)(2,1)} custom-call(s32[192]{0:T(256)S(1)} %broadcast_add_fusion.table_ref, bf16[64,32,128]{2,1,0:T(8,128)(2,1)S(1)} %bitcast.28), custom_call_target="tpu_custom_call" | custom-call | flops 1024 | bytes 1024 | tf_op jit(solution)/shard_map/pack/pallas_call | solution.py:135
  34.8 4.0 %all-to-all-start.1 = ((bf16[4,48,32,128]{3,2,1,0:T(8,128)(2,1)}), bf16[4,48,32,128]{3,2,1,0:T(8,128)(2,1)S(1)}, u32[]{:S(2)}, u32[]{:S(2)}) async-start(bf16[4,48,32,128]{3,2,1,0:T(8,128)(2,1)} %bitcast.9), calls=%async_computation.1 | async-start | bytes 3145728 | tf_op jit(solution)/shard_map/all_to_all | solution.py:376
  38.8 2.6 %collective-permute-done.1.refs_11_ = bf16[2064,128]{1,0:T(8,128)(2,1)} collective-permute-done((bf16[2064,128]{1,0:T(8,128)(2,1)S(1)}, bf16[2064,128]{1,0:T(8,128)(2,1)}, u32[]{:S(2)}, u32[]{:S(2)}) %collective-permute-start.1) | collective-permute-done | bytes 528416 | tf_op jit(solution)/shard_map/ppermute | solution.py:373
  41.4 1.9 %collective-permute-start.2 = (bf16[2064,128]{1,0:T(8,128)(2,1)}, bf16[2064,128]{1,0:T(8,128)(2,1)}, u32[]{:S(2)}, u32[]{:S(2)}) collective-permute-start(bf16[2064,128]{1,0:T(8,128)(2,1)} %collective-permute-done.1.refs_11_), channel_id=1, source_target_pairs={{0,32},{32,64},{64,96},{96,128},{128,160},{160,192},{192,224},{224... | collective-permute-start | bytes 1585160 | tf_op jit(solution)/shard_map/ppermute | solution.py:373
  43.3 4.6 %collective-permute-start.6 = (bf16[2064,128]{1,0:T(8,128)(2,1)}, bf16[2064,128]{1,0:T(8,128)(2,1)}, u32[]{:S(2)}, u32[]{:S(2)}) collective-permute-start(bf16[2064,128]{1,0:T(8,128)(2,1)} %collective-permute-done.5.refs_6_), channel_id=1, source_target_pairs={{0,480},{32,0},{64,32},{96,64},{128,96},{160,128},{192,160},{224,1... | collective-permute-start | bytes 1585160 | tf_op jit(solution)/shard_map/ppermute | solution.py:373
  47.9 8.3 %collective-permute-done.2.refs_10_ = bf16[2064,128]{1,0:T(8,128)(2,1)} collective-permute-done((bf16[2064,128]{1,0:T(8,128)(2,1)}, bf16[2064,128]{1,0:T(8,128)(2,1)}, u32[]{:S(2)}, u32[]{:S(2)}) %collective-permute-start.2) | collective-permute-done | bytes 528416 | tf_op jit(solution)/shard_map/ppermute | solution.py:373
  56.1 1.9 %collective-permute-start.3 = (bf16[2064,128]{1,0:T(8,128)(2,1)}, bf16[2064,128]{1,0:T(8,128)(2,1)}, u32[]{:S(2)}, u32[]{:S(2)}) collective-permute-start(bf16[2064,128]{1,0:T(8,128)(2,1)} %collective-permute-done.2.refs_10_), channel_id=1, source_target_pairs={{0,32},{32,64},{64,96},{96,128},{128,160},{160,192},{192,224},{224... | collective-permute-start | bytes 1585160 | tf_op jit(solution)/shard_map/ppermute | solution.py:373
  58.1 4.6 %collective-permute-start.7 = (bf16[2064,128]{1,0:T(8,128)(2,1)}, bf16[2064,128]{1,0:T(8,128)(2,1)}, u32[]{:S(2)}, u32[]{:S(2)}) collective-permute-start(bf16[2064,128]{1,0:T(8,128)(2,1)} %collective-permute-done.6.refs_7_), channel_id=1, source_target_pairs={{0,480},{32,0},{64,32},{96,64},{128,96},{160,128},{192,160},{224,1... | collective-permute-start | bytes 1585160 | tf_op jit(solution)/shard_map/ppermute | solution.py:373
  62.7 1.9 %collective-permute-start.8 = (bf16[4,3,32,128]{3,2,1,0:T(8,128)(2,1)S(1)}, bf16[4,3,32,128]{3,2,1,0:T(8,128)(2,1)S(1)}, u32[]{:S(2)}, u32[]{:S(2)}) collective-permute-start(bf16[4,3,32,128]{3,2,1,0:T(8,128)(2,1)S(1)} %slice.8), channel_id=1, source_target_pairs={{0,64},{32,96},{64,128},{96,160},{128,192},{160,224},{192,256},{22... | collective-permute-start | bytes 294920 | tf_op jit(solution)/shard_map/ppermute | solution.py:379
  64.6 2.4 %node.6 = bf16[4,320,128]{2,1,0:T(8,128)(2,1)S(1)} custom-call(bf16[4,48,32,128]{3,2,1,0:T(8,128)(2,1)S(1)} %all-to-all-done.1.refs_0_.refs_1_.refs_2_.refs_3_.refs_4_.refs_5_, bf16[4,48,32,128]{3,2,1,0:T(8,128)(2,1)S(1)} %all-to-all-done.1.refs_0_.refs_1_.refs_2_.refs_3_.refs_4_.refs_5_, ...), custom_call_target="tpu_custom_call" | custom-call | flops 1024 | bytes 1024 | tf_op jit(solution)/shard_map/node/pallas_call | solution.py:188
  67.0 4.8 %collective-permute-done.8.refs_0_ = bf16[4,3,32,128]{3,2,1,0:T(8,128)(2,1)S(1)} collective-permute-done((bf16[4,3,32,128]{3,2,1,0:T(8,128)(2,1)S(1)}, bf16[4,3,32,128]{3,2,1,0:T(8,128)(2,1)S(1)}, u32[]{:S(2)}, u32[]{:S(2)}) %collective-permute-start.8) | collective-permute-done | bytes 98336 | tf_op jit(solution)/shard_map/ppermute | solution.py:379
  71.8 4.0 %collective-permute-start.9 = (bf16[2064,128]{1,0:T(8,128)(2,1)}, bf16[2064,128]{1,0:T(8,128)(2,1)}, u32[]{:S(2)}, u32[]{:S(2)}) collective-permute-start(bf16[2064,128]{1,0:T(8,128)(2,1)} %collective-permute-done.3.refs_9_), channel_id=1, source_target_pairs={{0,32},{32,64},{64,96},{96,128},{128,160},{160,192},{192,224},{224... | collective-permute-start | bytes 1585160 | tf_op jit(solution)/shard_map/ppermute | solution.py:373
  75.9 2.5 %collective-permute-start.11 = (bf16[2064,128]{1,0:T(8,128)(2,1)}, bf16[2064,128]{1,0:T(8,128)(2,1)}, u32[]{:S(2)}, u32[]{:S(2)}) collective-permute-start(bf16[2064,128]{1,0:T(8,128)(2,1)} %collective-permute-done.7.refs_8_), channel_id=1, source_target_pairs={{0,480},{32,0},{64,32},{96,64},{128,96},{160,128},{192,160},{224,1... | collective-permute-start | bytes 1585160 | tf_op jit(solution)/shard_map/ppermute | solution.py:373
  78.3 5.9 %node.7 = bf16[4,624,128]{2,1,0:T(8,128)(2,1)S(1)} custom-call(bf16[4,48,32,128]{3,2,1,0:T(8,128)(2,1)S(1)} %all-to-all-done.1.refs_0_.refs_1_.refs_2_.refs_3_.refs_4_.refs_5_, bf16[4,48,32,128]{3,2,1,0:T(8,128)(2,1)S(1)} %all-to-all-done.1.refs_0_.refs_1_.refs_2_.refs_3_.refs_4_.refs_5_, ...), custom_call_target="tpu_custom_call" | custom-call | flops 1024 | bytes 1024 | tf_op jit(solution)/shard_map/node/pallas_call | solution.py:188
  84.2 2.8 %collective-permute-start.10 = (bf16[2064,128]{1,0:T(8,128)(2,1)}, bf16[2064,128]{1,0:T(8,128)(2,1)}, u32[]{:S(2)}, u32[]{:S(2)}) collective-permute-start(bf16[2064,128]{1,0:T(8,128)(2,1)} %collective-permute-done.9.refs_3_), channel_id=1, source_target_pairs={{0,32},{32,64},{64,96},{96,128},{128,160},{160,192},{192,224},{224... | collective-permute-start | bytes 1585160 | tf_op jit(solution)/shard_map/ppermute | solution.py:373
  87.1 3.0 %node.8 = bf16[4,208,128]{2,1,0:T(8,128)(2,1)S(1)} custom-call(bf16[4,48,32,128]{3,2,1,0:T(8,128)(2,1)S(1)} %all-to-all-done.1.refs_0_.refs_1_.refs_2_.refs_3_.refs_4_.refs_5_, bf16[4,48,32,128]{3,2,1,0:T(8,128)(2,1)S(1)} %all-to-all-done.1.refs_0_.refs_1_.refs_2_.refs_3_.refs_4_.refs_5_, bf16[2064,128]{1,0:T(8,128)(2,1)} %collective-permute-done.11.refs_2_, ...), custom_call_target="tpu_custom_call" | custom-call | flops 1024 | bytes 1024 | tf_op jit(solution)/shard_map/node/pallas_call | solution.py:188
  90.1 3.7 %collective-permute-start.12 = (bf16[2064,128]{1,0:T(8,128)(2,1)}, bf16[2064,128]{1,0:T(8,128)(2,1)S(1)}, u32[]{:S(2)}, u32[]{:S(2)}) collective-permute-start(bf16[2064,128]{1,0:T(8,128)(2,1)} %collective-permute-done.11.refs_2_), channel_id=1, source_target_pairs={{0,480},{32,0},{64,32},{96,64},{128,96},{160,128},{192,160},{224,1... | collective-permute-start | bytes 1585160 | tf_op jit(solution)/shard_map/ppermute | solution.py:373
  93.8 1.1 pad_maximum_fusion
  94.9 4.1 %all-to-all-start.2 = ((bf16[4,1152,128]{2,1,0:T(8,128)(2,1)}), bf16[4,1152,128]{2,1,0:T(8,128)(2,1)S(1)}, u32[]{:S(2)}, u32[]{:S(2)}) async-start(bf16[4,1152,128]{2,1,0:T(8,128)(2,1)} %pad_maximum_fusion), calls=%async_computation.2 | async-start | bytes 2359296 | tf_op jit(solution)/shard_map/all_to_all | solution.py:362
  99.0 1.6 %collective-permute-done.12.refs_2_.refs_1_ = bf16[2064,128]{1,0:T(8,128)(2,1)S(1)} collective-permute-done((bf16[2064,128]{1,0:T(8,128)(2,1)}, bf16[2064,128]{1,0:T(8,128)(2,1)S(1)}, u32[]{:S(2)}, u32[]{:S(2)}) %collective-permute-start.12) | collective-permute-done | bytes 528416 | tf_op jit(solution)/shard_map/ppermute | solution.py:373
  100.7 1.9 %collective-permute-start.13 = (bf16[2064,128]{1,0:T(8,128)(2,1)}, bf16[2064,128]{1,0:T(8,128)(2,1)}, u32[]{:S(2)}, u32[]{:S(2)}) collective-permute-start(bf16[2064,128]{1,0:T(8,128)(2,1)} %collective-permute-done.10.refs_3_), channel_id=1, source_target_pairs={{0,32},{32,64},{64,96},{96,128},{128,160},{160,192},{192,224},{224... | collective-permute-start | bytes 1585160 | tf_op jit(solution)/shard_map/ppermute | solution.py:373
  102.6 4.6 %collective-permute-start.14 = (bf16[2064,128]{1,0:T(8,128)(2,1)S(1)}, bf16[2064,128]{1,0:T(8,128)(2,1)}, u32[]{:S(2)}, u32[]{:S(2)}) collective-permute-start(bf16[2064,128]{1,0:T(8,128)(2,1)S(1)} %collective-permute-done.12.refs_2_.refs_1_), channel_id=1, source_target_pairs={{0,480},{32,0},{64,32},{96,64},{128,96},{160,128},{192,160},{224,1... | collective-permute-start | bytes 1585160 | tf_op jit(solution)/shard_map/ppermute | solution.py:373
  107.2 1.2 node.10
  108.4 3.2 %collective-permute-start.15 = (bf16[4,112,128]{2,1,0:T(8,128)(2,1)S(1)}, bf16[4,112,128]{2,1,0:T(8,128)(2,1)}, u32[]{:S(2)}, u32[]{:S(2)}) collective-permute-start(bf16[4,112,128]{2,1,0:T(8,128)(2,1)S(1)} %node.10), channel_id=1, source_target_pairs={{0,448},{32,480},{64,0},{96,32},{128,64},{160,96},{192,128},{224,1... | collective-permute-start | bytes 344072 | tf_op jit(solution)/shard_map/ppermute | solution.py:388
  111.6 2.9 %node.9 = bf16[4,208,128]{2,1,0:T(8,128)(2,1)S(1)} custom-call(bf16[4,48,32,128]{3,2,1,0:T(8,128)(2,1)S(1)} %all-to-all-done.1.refs_0_.refs_1_.refs_2_.refs_3_.refs_4_.refs_5_, bf16[4,48,32,128]{3,2,1,0:T(8,128)(2,1)S(1)} %all-to-all-done.1.refs_0_.refs_1_.refs_2_.refs_3_.refs_4_.refs_5_, bf16[2064,128]{1,0:T(8,128)(2,1)S(1)} %collective-permute-done.12.refs_2_.refs_1_, ...), custom_call_target="tpu_custom_call" | custom-call | flops 1024 | bytes 1024 | tf_op jit(solution)/shard_map/node/pallas_call | solution.py:188
  114.5 2.4 %collective-permute-done.15 = bf16[4,112,128]{2,1,0:T(8,128)(2,1)} collective-permute-done((bf16[4,112,128]{2,1,0:T(8,128)(2,1)S(1)}, bf16[4,112,128]{2,1,0:T(8,128)(2,1)}, u32[]{:S(2)}, u32[]{:S(2)}) %collective-permute-start.15) | collective-permute-done | bytes 114720 | tf_op jit(solution)/shard_map/ppermute | solution.py:388
  116.9 3.0 %node.11 = bf16[4,208,128]{2,1,0:T(8,128)(2,1)S(1)} custom-call(bf16[4,48,32,128]{3,2,1,0:T(8,128)(2,1)S(1)} %all-to-all-done.1.refs_0_.refs_1_.refs_2_.refs_3_.refs_4_.refs_5_, bf16[4,48,32,128]{3,2,1,0:T(8,128)(2,1)S(1)} %all-to-all-done.1.refs_0_.refs_1_.refs_2_.refs_3_.refs_4_.refs_5_, bf16[2064,128]{1,0:T(8,128)(2,1)} %collective-permute-done.14.refs_2_, ...), custom_call_target="tpu_custom_call" | custom-call | flops 1024 | bytes 1024 | tf_op jit(solution)/shard_map/node/pallas_call | solution.py:188
  120.0 0.9 pad_maximum_fusion.1
  120.9 10.8 %all_to_all.25.refs_1_ = bf16[4,528,128]{2,1,0:T(8,128)(2,1)S(1)} all-to-all(bf16[4,528,128]{2,1,0:T(8,128)(2,1)S(1)} %pad_maximum_fusion.1), channel_id=1, replica_groups=mesh['z'=16,'x'=4,'y'=4,'core'=2] {'x'}, dimensions={0} | all-to-all | bytes 1081344 | tf_op jit(solution)/shard_map/all_to_all | solution.py:393
  131.8 2.7 %merge.1 = bf16[8,304,128]{2,1,0:T(8,128)(2,1)} custom-call(s32[192]{0:T(256)S(1)} %broadcast_add_fusion.table_ref, bf16[4,1152,128]{2,1,0:T(8,128)(2,1)S(1)} %all-to-all-done.2.refs_0_, bf16[4,528,128]{2,1,0:T(8,128)(2,1)S(1)} %all_to_all.25.refs_1_), custom_call_target="tpu_custom_call" | custom-call | flops 4194304 | bytes 4194304 | tf_op jit(solution)/shard_map/merge/pallas_call | solution.py:251
  134.5 14.0 %all-to-all-start.4 = ((bf16[8,304,128]{2,1,0:T(8,128)(2,1)}), bf16[8,304,128]{2,1,0:T(8,128)(2,1)S(1)}, u32[]{:S(2)}, u32[]{:S(2)}) async-start(bf16[8,304,128]{2,1,0:T(8,128)(2,1)} %merge.1), calls=%async_computation.4 | async-start | bytes 1245184 | tf_op jit(solution)/shard_map/all_to_all | solution.py:395
  148.5 4.9 %suffix.1 = (f32[8,256,128]{2,1,0:T(8,128)S(1)}, f32[8,8,256]{2,1,0:T(8,128)S(1)}) custom-call(s32[8]{0:T(128)S(1)} %copy-done.8, bf16[8,256,128]{2,1,0:T(8,128)(2,1)S(1)} %bitcast.27, bf16[8,256,128]{2,1,0:T(8,128)(2,1)S(1)} %bitcast.30, bf16[8,32,128]{2,1,0:T(8,128)(2,1)S(1)} %bitcast.32, bf16[8,256,128]{2,1,0:T(8,128)(2,1)S(1)} %bitcast.31, ...), custom_call_target="tpu_custom_call" | custom-call | flops 268435456 | bytes 4194304 | tf_op jit(solution)/shard_map/suffix/pallas_call | solution.py:91
  153.4 0.2 reshape.131
  153.7 0.2 reshape.132
  153.9 5.1 %all-to-all-done.4.arrived_ref = bf16[8,304,128]{2,1,0:T(8,128)(2,1)S(1)} async-done(((bf16[8,304,128]{2,1,0:T(8,128)(2,1)}), bf16[8,304,128]{2,1,0:T(8,128)(2,1)S(1)}, u32[]{:S(2)}, u32[]{:S(2)}) %all-to-all-start.4) | async-done | bytes 622624 | tf_op jit(solution)/shard_map/all_to_all | solution.py:395
  159.0 1.6 final.1
  (40 shorter events, 0.2 us)
Async XLA Ops:
  0.0 16.1 %copy-start = (bf16[8,4,64,128]{3,2,1,0:T(8,128)(2,1)S(1)}, bf16[8,4,64,128]{3,2,1,0:T(8,128)(2,1)}, u32[]{:S(2)}) copy-start(bf16[8,4,64,128]{3,2,1,0:T(8,128)(2,1)} %param.10) | copy-start | bytes 1572868
  2.2 20.2 %copy-start.9 = (s32[64,2]{0,1:T(2,128)S(1)}, s32[64,2]{0,1:T(2,128)}, u32[]{:S(2)}) copy-start(s32[64,2]{0,1:T(2,128)} %param.16) | copy-start | bytes 1540
  2.2 23.7 %collective-permute-start = (bf16[2064,128]{1,0:T(8,128)(2,1)S(1)}, bf16[2064,128]{1,0:T(8,128)(2,1)S(1)}, u32[]{:S(2)}, u32[]{:S(2)}) collective-permute-start(bf16[2064,128]{1,0:T(8,128)(2,1)S(1)} %maximum_maximum_fusion.refs_3_), channel_id=1, source_target_pairs={{0,32},{32,64},{64,96},{96,128},{128,160},{160,192},{192,224},{224... | collective-permute-start | bytes 1585160 | tf_op jit(solution)/shard_map/ppermute | solution.py:373
  6.6 21.2 %collective-permute-start.4 = (bf16[2064,128]{1,0:T(8,128)(2,1)S(1)}, bf16[2064,128]{1,0:T(8,128)(2,1)S(1)}, u32[]{:S(2)}, u32[]{:S(2)}) collective-permute-start(bf16[2064,128]{1,0:T(8,128)(2,1)S(1)} %maximum_maximum_fusion.refs_3_), channel_id=1, source_target_pairs={{0,480},{32,0},{64,32},{96,64},{128,96},{160,128},{192,160},{224,1... | collective-permute-start | bytes 1585160 | tf_op jit(solution)/shard_map/ppermute | solution.py:373
  17.0 15.5 %all-to-all-start = ((bf16[8,32,8,128]{3,2,1,0:T(8,128)(2,1)}), bf16[8,32,8,128]{3,2,1,0:T(8,128)(2,1)S(1)}, u32[]{:S(2)}, u32[]{:S(2)}) async-start(bf16[8,32,8,128]{3,2,1,0:T(8,128)(2,1)} %bitcast.20), calls=%async_computation | async-start | bytes 1048576 | tf_op jit(solution)/shard_map/all_to_all | solution.py:345
  25.9 15.5 %collective-permute-start.1 = (bf16[2064,128]{1,0:T(8,128)(2,1)S(1)}, bf16[2064,128]{1,0:T(8,128)(2,1)}, u32[]{:S(2)}, u32[]{:S(2)}) collective-permute-start(bf16[2064,128]{1,0:T(8,128)(2,1)S(1)} %collective-permute-done.refs_5_), channel_id=1, source_target_pairs={{0,32},{32,64},{64,96},{96,128},{128,160},{160,192},{192,224},{224... | collective-permute-start | bytes 1585160 | tf_op jit(solution)/shard_map/ppermute | solution.py:373
  27.8 15.5 %collective-permute-start.5 = (bf16[2064,128]{1,0:T(8,128)(2,1)S(1)}, bf16[2064,128]{1,0:T(8,128)(2,1)}, u32[]{:S(2)}, u32[]{:S(2)}) collective-permute-start(bf16[2064,128]{1,0:T(8,128)(2,1)S(1)} %collective-permute-done.4.refs_4_), channel_id=1, source_target_pairs={{0,480},{32,0},{64,32},{96,64},{128,96},{160,128},{192,160},{224,1... | collective-permute-start | bytes 1585160 | tf_op jit(solution)/shard_map/ppermute | solution.py:373
  34.8 27.9 %all-to-all-start.1 = ((bf16[4,48,32,128]{3,2,1,0:T(8,128)(2,1)}), bf16[4,48,32,128]{3,2,1,0:T(8,128)(2,1)S(1)}, u32[]{:S(2)}, u32[]{:S(2)}) async-start(bf16[4,48,32,128]{3,2,1,0:T(8,128)(2,1)} %bitcast.9), calls=%async_computation.1 | async-start | bytes 3145728 | tf_op jit(solution)/shard_map/all_to_all | solution.py:376
  41.4 14.8 %collective-permute-start.2 = (bf16[2064,128]{1,0:T(8,128)(2,1)}, bf16[2064,128]{1,0:T(8,128)(2,1)}, u32[]{:S(2)}, u32[]{:S(2)}) collective-permute-start(bf16[2064,128]{1,0:T(8,128)(2,1)} %collective-permute-done.1.refs_11_), channel_id=1, source_target_pairs={{0,32},{32,64},{64,96},{96,128},{128,160},{160,192},{192,224},{224... | collective-permute-start | bytes 1585160 | tf_op jit(solution)/shard_map/ppermute | solution.py:373
  43.3 14.8 %collective-permute-start.6 = (bf16[2064,128]{1,0:T(8,128)(2,1)}, bf16[2064,128]{1,0:T(8,128)(2,1)}, u32[]{:S(2)}, u32[]{:S(2)}) collective-permute-start(bf16[2064,128]{1,0:T(8,128)(2,1)} %collective-permute-done.5.refs_6_), channel_id=1, source_target_pairs={{0,480},{32,0},{64,32},{96,64},{128,96},{160,128},{192,160},{224,1... | collective-permute-start | bytes 1585160 | tf_op jit(solution)/shard_map/ppermute | solution.py:373
  56.1 15.7 %collective-permute-start.3 = (bf16[2064,128]{1,0:T(8,128)(2,1)}, bf16[2064,128]{1,0:T(8,128)(2,1)}, u32[]{:S(2)}, u32[]{:S(2)}) collective-permute-start(bf16[2064,128]{1,0:T(8,128)(2,1)} %collective-permute-done.2.refs_10_), channel_id=1, source_target_pairs={{0,32},{32,64},{64,96},{96,128},{128,160},{160,192},{192,224},{224... | collective-permute-start | bytes 1585160 | tf_op jit(solution)/shard_map/ppermute | solution.py:373
  58.1 13.8 %collective-permute-start.7 = (bf16[2064,128]{1,0:T(8,128)(2,1)}, bf16[2064,128]{1,0:T(8,128)(2,1)}, u32[]{:S(2)}, u32[]{:S(2)}) collective-permute-start(bf16[2064,128]{1,0:T(8,128)(2,1)} %collective-permute-done.6.refs_7_), channel_id=1, source_target_pairs={{0,480},{32,0},{64,32},{96,64},{128,96},{160,128},{192,160},{224,1... | collective-permute-start | bytes 1585160 | tf_op jit(solution)/shard_map/ppermute | solution.py:373
  62.7 9.1 %collective-permute-start.8 = (bf16[4,3,32,128]{3,2,1,0:T(8,128)(2,1)S(1)}, bf16[4,3,32,128]{3,2,1,0:T(8,128)(2,1)S(1)}, u32[]{:S(2)}, u32[]{:S(2)}) collective-permute-start(bf16[4,3,32,128]{3,2,1,0:T(8,128)(2,1)S(1)} %slice.8), channel_id=1, source_target_pairs={{0,64},{32,96},{64,128},{96,160},{128,192},{160,224},{192,256},{22... | collective-permute-start | bytes 294920 | tf_op jit(solution)/shard_map/ppermute | solution.py:379
  71.8 12.4 %copy-start.4 = (bf16[4,3,32,128]{3,2,1,0:T(8,128)(2,1)}, bf16[4,3,32,128]{3,2,1,0:T(8,128)(2,1)S(1)}, u32[]{:S(2)}) copy-start(bf16[4,3,32,128]{3,2,1,0:T(8,128)(2,1)S(1)} %collective-permute-done.8.refs_0_) | copy-start | bytes 294916
  71.8 12.4 %collective-permute-start.9 = (bf16[2064,128]{1,0:T(8,128)(2,1)}, bf16[2064,128]{1,0:T(8,128)(2,1)}, u32[]{:S(2)}, u32[]{:S(2)}) collective-permute-start(bf16[2064,128]{1,0:T(8,128)(2,1)} %collective-permute-done.3.refs_9_), channel_id=1, source_target_pairs={{0,32},{32,64},{64,96},{96,128},{128,160},{160,192},{192,224},{224... | collective-permute-start | bytes 1585160 | tf_op jit(solution)/shard_map/ppermute | solution.py:373
  75.9 11.2 %collective-permute-start.11 = (bf16[2064,128]{1,0:T(8,128)(2,1)}, bf16[2064,128]{1,0:T(8,128)(2,1)}, u32[]{:S(2)}, u32[]{:S(2)}) collective-permute-start(bf16[2064,128]{1,0:T(8,128)(2,1)} %collective-permute-done.7.refs_8_), channel_id=1, source_target_pairs={{0,480},{32,0},{64,32},{96,64},{128,96},{160,128},{192,160},{224,1... | collective-permute-start | bytes 1585160 | tf_op jit(solution)/shard_map/ppermute | solution.py:373
  84.2 14.8 %collective-permute-start.10 = (bf16[2064,128]{1,0:T(8,128)(2,1)}, bf16[2064,128]{1,0:T(8,128)(2,1)}, u32[]{:S(2)}, u32[]{:S(2)}) collective-permute-start(bf16[2064,128]{1,0:T(8,128)(2,1)} %collective-permute-done.9.refs_3_), channel_id=1, source_target_pairs={{0,32},{32,64},{64,96},{96,128},{128,160},{160,192},{192,224},{224... | collective-permute-start | bytes 1585160 | tf_op jit(solution)/shard_map/ppermute | solution.py:373
  90.1 10.6 %collective-permute-start.12 = (bf16[2064,128]{1,0:T(8,128)(2,1)}, bf16[2064,128]{1,0:T(8,128)(2,1)S(1)}, u32[]{:S(2)}, u32[]{:S(2)}) collective-permute-start(bf16[2064,128]{1,0:T(8,128)(2,1)} %collective-permute-done.11.refs_2_), channel_id=1, source_target_pairs={{0,480},{32,0},{64,32},{96,64},{128,96},{160,128},{192,160},{224,1... | collective-permute-start | bytes 1585160 | tf_op jit(solution)/shard_map/ppermute | solution.py:373
  94.9 12.3 %copy-start.5 = (bf16[4,3,32,128]{3,2,1,0:T(8,128)(2,1)S(1)}, bf16[4,3,32,128]{3,2,1,0:T(8,128)(2,1)}, u32[]{:S(2)}) copy-start(bf16[4,3,32,128]{3,2,1,0:T(8,128)(2,1)} %copy-done.4) | copy-start | bytes 294916
  94.9 22.0 %all-to-all-start.2 = ((bf16[4,1152,128]{2,1,0:T(8,128)(2,1)}), bf16[4,1152,128]{2,1,0:T(8,128)(2,1)S(1)}, u32[]{:S(2)}, u32[]{:S(2)}) async-start(bf16[4,1152,128]{2,1,0:T(8,128)(2,1)} %pad_maximum_fusion), calls=%async_computation.2 | async-start | bytes 2359296 | tf_op jit(solution)/shard_map/all_to_all | solution.py:362
  100.7 16.3 %collective-permute-start.13 = (bf16[2064,128]{1,0:T(8,128)(2,1)}, bf16[2064,128]{1,0:T(8,128)(2,1)}, u32[]{:S(2)}, u32[]{:S(2)}) collective-permute-start(bf16[2064,128]{1,0:T(8,128)(2,1)} %collective-permute-done.10.refs_3_), channel_id=1, source_target_pairs={{0,32},{32,64},{64,96},{96,128},{128,160},{160,192},{192,224},{224... | collective-permute-start | bytes 1585160 | tf_op jit(solution)/shard_map/ppermute | solution.py:373
  102.6 14.4 %collective-permute-start.14 = (bf16[2064,128]{1,0:T(8,128)(2,1)S(1)}, bf16[2064,128]{1,0:T(8,128)(2,1)}, u32[]{:S(2)}, u32[]{:S(2)}) collective-permute-start(bf16[2064,128]{1,0:T(8,128)(2,1)S(1)} %collective-permute-done.12.refs_2_.refs_1_), channel_id=1, source_target_pairs={{0,480},{32,0},{64,32},{96,64},{128,96},{160,128},{192,160},{224,1... | collective-permute-start | bytes 1585160 | tf_op jit(solution)/shard_map/ppermute | solution.py:373
  108.4 8.5 %collective-permute-start.15 = (bf16[4,112,128]{2,1,0:T(8,128)(2,1)S(1)}, bf16[4,112,128]{2,1,0:T(8,128)(2,1)}, u32[]{:S(2)}, u32[]{:S(2)}) collective-permute-start(bf16[4,112,128]{2,1,0:T(8,128)(2,1)S(1)} %node.10), channel_id=1, source_target_pairs={{0,448},{32,480},{64,0},{96,32},{128,64},{160,96},{192,128},{224,1... | collective-permute-start | bytes 344072 | tf_op jit(solution)/shard_map/ppermute | solution.py:388
  131.8 16.7 %copy-start.3 = (bf16[8,32,8,128]{3,2,1,0:T(8,128)(2,1)S(1)}, bf16[8,32,8,128]{3,2,1,0:T(8,128)(2,1)}, u32[]{:S(2)}) copy-start(bf16[8,32,8,128]{3,2,1,0:T(8,128)(2,1)} %param.14) | copy-start | bytes 1572868
  134.4 14.1 %copy-start.1 = (bf16[8,4,64,128]{3,2,1,0:T(8,128)(2,1)S(1)}, bf16[8,4,64,128]{3,2,1,0:T(8,128)(2,1)}, u32[]{:S(2)}) copy-start(bf16[8,4,64,128]{3,2,1,0:T(8,128)(2,1)} %param.10) | copy-start | bytes 1572868
  134.4 14.1 %copy-start.2 = (bf16[8,32,8,128]{3,2,1,0:T(8,128)(2,1)S(1)}, bf16[8,32,8,128]{3,2,1,0:T(8,128)(2,1)}, u32[]{:S(2)}) copy-start(bf16[8,32,8,128]{3,2,1,0:T(8,128)(2,1)} %param.13) | copy-start | bytes 1572868
  134.4 14.1 %copy-start.6 = (bf16[8,4,8,128]{3,2,1,0:T(8,128)(2,1)S(1)}, bf16[8,4,8,128]{3,2,1,0:T(8,128)(2,1)}, u32[]{:S(2)}) copy-start(bf16[8,4,8,128]{3,2,1,0:T(8,128)(2,1)} %param.11) | copy-start | bytes 196612
  134.4 14.1 %copy-start.7 = (bf16[8,4,8,128]{3,2,1,0:T(8,128)(2,1)S(1)}, bf16[8,4,8,128]{3,2,1,0:T(8,128)(2,1)}, u32[]{:S(2)}) copy-start(bf16[8,4,8,128]{3,2,1,0:T(8,128)(2,1)} %param.12) | copy-start | bytes 196612
  134.4 14.1 %copy-start.8 = (s32[8]{0:T(128)S(1)}, s32[8]{0:T(128)}, u32[]{:S(2)}) copy-start(s32[8]{0:T(128)} %len_ref.1) | copy-start | bytes 100
  134.5 24.6 %all-to-all-start.4 = ((bf16[8,304,128]{2,1,0:T(8,128)(2,1)}), bf16[8,304,128]{2,1,0:T(8,128)(2,1)S(1)}, u32[]{:S(2)}, u32[]{:S(2)}) async-start(bf16[8,304,128]{2,1,0:T(8,128)(2,1)} %merge.1), calls=%async_computation.4 | async-start | bytes 1245184 | tf_op jit(solution)/shard_map/all_to_all | solution.py:395
